TPU v7x, 512 devices: a whole 4x4x16 slice. The times are simulated.
512 devices in a mesh: row: 32 (over z, core), col: 16 (over y, x).
Axes of the slice: x: 4, y: 4, z: 16, core: 2. Of those that a mesh axis runs over, the one named last changes fastest.
Arguments:
- inverse_root: float32 [32, 16, 2, 384, 192], P('row', 'col'), may hold values from -0.0546875 to 0.0546875
- inverse_upper: float32 [32, 16, 2, 192, 192], P('row', 'col'), may hold values from -0.078125 to 0.078125
- inverse_middle: float32 [32, 16, 2, 384, 192], P('row', 'col'), may hold values from -0.078125 to 0.078125
- inverse_lower: float32 [32, 16, 2, 192, 192], P('row', 'col'), may hold values from -0.109375 to 0.109375
- leaf_inverse: float32 [32, 16, 2, 384, 384], P('row', 'col'), may hold values from -0.21875 to 0.21875
- source_root: float32 [32, 1, 192, 128], P('row'), may hold values from -6 to 6
- source_upper: float32 [32, 1, 192, 128], P('row'), may hold values from -6 to 6
- source_middle: float32 [32, 2, 192, 128], P('row'), may hold values from -6 to 6
- source_lower: float32 [32, 2, 192, 128], P('row'), may hold values from -6 to 6
- leaf_source: float32 [32, 16, 384, 128], P('row', 'col'), may hold values from -6 to 6
- update_root: float32 [32, 1, 2, 2, 96, 32], P('row'), may hold values from -0.75 to 0.75
- update_upper: float32 [32, 1, 2, 2, 96, 32], P('row'), may hold values from -0.75 to 0.75
- update_middle: float32 [32, 2, 2, 2, 96, 32], P('row'), may hold values from -0.75 to 0.75
- leaf_update: float32 [32, 16, 2, 96, 32], P('row', 'col'), may hold values from -0.75 to 0.75
- slots_root: int32 [32, 1, 2, 96], P('row'), may hold values from 0 to 192, as said below
- slots_upper: int32 [32, 1, 2, 96], P('row'), may hold values from 0 to 192, as said below
- slots_middle: int32 [32, 2, 2, 96], P('row'), may hold values from 0 to 192, as said below
- leaf_slots: int32 [32, 16, 96], P('row', 'col'), may hold values from 0 to 192, as said below
- basis_upper: float32 [16, 2, 2, 192, 32], P('col'), may hold values from -0.078125 to 0.078125
- basis_middle: float32 [16, 2, 2, 384, 32], P('col'), may hold values from -0.078125 to 0.078125
- basis_lower: float32 [16, 4, 2, 192, 32], P('col'), may hold values from -0.109375 to 0.109375
- leaf_basis: float32 [32, 16, 2, 384, 32], P('row', 'col'), may hold values from -0.21875 to 0.21875
- front_ranks: int32 [14], replicated, may hold values from 8 to 32, as said below
- leaf_ranks: int32 [32, 16], P('row', 'col'), may hold values from 8 to 32, as said below
Outputs:
- solution_root: float32 [32, 16, 12, 128], P('row', 'col')
- solution_upper: float32 [32, 16, 12, 128], P('row', 'col')
- solution_middle: float32 [32, 16, 24, 128], P('row', 'col')
- solution_lower: float32 [32, 16, 24, 128], P('row', 'col')
- leaf_solution: float32 [32, 16, 384, 128], P('row', 'col')
Inputs may be any that keep to these rules, and one draw needn't show every extreme that they name: `slots_root`: within one row of slots the entries below 192 are distinct; 192 marks an unused slot; every row of slots has at least half of its slots used and at least one unused. `slots_upper`: as for slots_root. `slots_middle`: as for slots_root. `leaf_slots`: as for slots_root. `front_ranks`: some front has rank 32. `leaf_ranks`: some subtree has rank 32.
All inputs are finite; a program needn't handle non-finite values.
Results may differ from a plain program's by a relative error of at most 0.00013.
Values sent between devices are 32-bit elements; how exact they have to be, the bound alone decides.
No kernel may reach another device: no remote copies, remote signals or barrier semaphores. Data moves between devices by JAX's collectives and lax.ppermute only.
A program may use at most 64 MiB of HBM per device.

v0:
```python
import jax
import jax.numpy as jnp
from jax import lax
from jax.sharding import PartitionSpec as P

precise = lax.Precision.HIGHEST


def from_partner(array, axis, stride):
    return lax.ppermute(array, axis, [(i, i ^ 1 << stride) for i in range(lax.axis_size(axis))])


def combine(stacked):
    half_width = stacked.shape[-1] // 2
    real_part = stacked[..., 0, :, :]
    imag_part = stacked[..., 1, :, :]
    return jnp.concatenate(
        [
            real_part[..., :half_width] - imag_part[..., half_width:],
            real_part[..., half_width:] + imag_part[..., :half_width],
        ],
        axis=-1,
    )


def product(matrix, vector):
    return combine(jnp.einsum("...zmk,...kc->...zmc", matrix, vector, precision=precise))


def product_back(matrix, vector):
    return combine(jnp.einsum("...zkm,...kc->...zmc", matrix, vector, precision=precise))


def spread(row_index, values, height):
    return (
        jnp.zeros((height, values.shape[-1]), values.dtype).at[row_index].add(values, mode="drop")
    )


def pick_rows(source_block, row_index):
    padded = jnp.concatenate(
        [source_block, jnp.zeros((1, source_block.shape[-1]), source_block.dtype)], axis=0
    )
    return jnp.take(padded, row_index, axis=0)


def masked(values, rank_limit):
    keep_rows = jnp.arange(values.shape[-2])[:, None] < rank_limit
    return jnp.where(keep_rows, values, jnp.zeros_like(values))


def select(array, position):
    return lax.dynamic_index_in_dim(array, position, 0, keepdims=False)


def row_total(values, group_span):
    groups = lax.axis_size("row") // group_span
    group_at = lax.axis_index("row") // group_span
    onehot = (jnp.arange(groups) == group_at).astype(jnp.float32)
    slotted = onehot.reshape((groups,) + (1,) * values.ndim) * values[None]
    summed = lax.psum(slotted, "row")
    return select(summed, group_at)


def column_total(values, group_span):
    groups = lax.axis_size("col") // group_span
    group_at = lax.axis_index("col") // group_span
    onehot = (jnp.arange(groups) == group_at).astype(jnp.float32)
    slotted = onehot.reshape((groups,) + (1,) * values.ndim) * values[None]
    summed = lax.psum(slotted, "col")
    return select(summed, group_at)


def row_partner(values, bit_number):
    return from_partner(values, "row", bit_number)


def column_partner(values, bit_number):
    return from_partner(values, "col", bit_number)


def body(
    inverse_root,
    inverse_upper,
    inverse_middle,
    inverse_lower,
    leaf_inverse,
    source_root,
    source_upper,
    source_middle,
    source_lower,
    leaf_source,
    update_root,
    update_upper,
    update_middle,
    leaf_update,
    slots_root,
    slots_upper,
    slots_middle,
    leaf_slots,
    basis_upper,
    basis_middle,
    basis_lower,
    leaf_basis,
    front_ranks,
    leaf_ranks,
):
    row_count = lax.axis_size("row")
    column_count = lax.axis_size("col")
    row_at = lax.axis_index("row")
    column_at = lax.axis_index("col")
    grid_rows = (row_count, row_count // 2, row_count // 2, row_count // 4)
    grid_cols = (column_count, column_count, column_count // 2, column_count // 2)
    col_groups = (1, 1, 2, 2)
    rank_base = (0, 0, 2, 6)
    front_row = [row_at // grid_rows[height] for height in range(4)]
    front_col = [column_at // grid_cols[height] for height in range(4)]

    def rank_of(height):
        return select(
            front_ranks,
            rank_base[height] + front_row[height] * col_groups[height] + front_col[height],
        )

    inverses = (inverse_root[0, 0], inverse_upper[0, 0], inverse_middle[0, 0], inverse_lower[0, 0])
    sources = (source_root, source_upper, source_middle, source_lower)
    right_sides = [select(sources[height][0], front_col[height]) for height in range(4)]
    updates = [
        select(array[0], front_col[parent])
        for parent, array in enumerate((update_root, update_upper, update_middle))
    ]
    slot_maps = [
        select(array[0], front_col[parent])
        for parent, array in enumerate((slots_root, slots_upper, slots_middle))
    ]
    basis_sets = [None] + [
        select(array[0], front_row[height + 1])
        for height, array in enumerate((basis_upper, basis_middle, basis_lower))
    ]
    separator = right_sides[0].shape[0]
    leaf_forward = product(leaf_inverse[0, 0], leaf_source[0, 0])
    leaf_coeffs = masked(product_back(leaf_basis[0, 0], leaf_forward), leaf_ranks[0, 0])
    leaf_term = spread(leaf_slots[0, 0], product(leaf_update[0, 0], leaf_coeffs), separator)
    pending = column_total(leaf_term, grid_cols[3])
    forwards = [None, None, None, None]
    for height in (3, 2, 1, 0):
        partial_forward = product(inverses[height], right_sides[height] - pending)
        forward = row_total(partial_forward, grid_rows[height])
        forwards[height] = forward
        if height > 0:
            weights_now = masked(
                column_total(product_back(basis_sets[height], forward), grid_cols[height]),
                rank_of(height),
            )
            if height == 2:
                sibling = column_partner(weights_now, grid_cols[2].bit_length() - 1)
                child_slot = front_col[2] % 2
            else:
                sibling = row_partner(weights_now, grid_rows[height].bit_length() - 1)
                child_slot = front_row[height] % 2
            left_term = jnp.where(child_slot == 0, weights_now, sibling)
            right_term = jnp.where(child_slot == 0, sibling, weights_now)
            parent = height - 1
            pending = spread(
                slot_maps[parent][0], product(updates[parent][0], left_term), separator
            ) + spread(slot_maps[parent][1], product(updates[parent][1], right_term), separator)
    solved = column_total(product_back(inverses[0], forwards[0]), grid_cols[0])
    backwards = [solved]
    for height in (1, 2, 3):
        parent = height - 1
        left_rows = pick_rows(solved, slot_maps[parent][0])
        right_rows = pick_rows(solved, slot_maps[parent][1])
        partials = jnp.stack(
            [
                product_back(updates[parent][0], left_rows),
                product_back(updates[parent][1], right_rows),
            ]
        )
        summed = row_total(partials, grid_rows[parent])
        child_slot = front_col[2] % 2 if height == 2 else front_row[height] % 2
        coeffs = masked(select(summed, child_slot), rank_of(height))
        partial_back = product_back(
            inverses[height], forwards[height] - product(basis_sets[height], coeffs)
        )
        solved = column_total(partial_back, grid_cols[height])
        backwards.append(solved)
    leaf_rows = pick_rows(solved, leaf_slots[0, 0])
    leaf_back_coeffs = masked(product_back(leaf_update[0, 0], leaf_rows), leaf_ranks[0, 0])
    leaf_back = leaf_forward - product(leaf_basis[0, 0], leaf_back_coeffs)
    leaf_solution = product_back(leaf_inverse[0, 0], leaf_back)
    results = []
    for height in range(4):
        piece_rows = separator // grid_cols[height]
        place_col = column_at % grid_cols[height]
        results.append(
            lax.dynamic_slice_in_dim(backwards[height], place_col * piece_rows, piece_rows, 0)[
                None, None
            ]
        )
    return (results[0], results[1], results[2], results[3], leaf_solution[None, None])


def solution(mesh):
    return jax.shard_map(
        body,
        mesh=mesh,
        in_specs=(
            P("row", "col", None, None, None),
            P("row", "col", None, None, None),
            P("row", "col", None, None, None),
            P("row", "col", None, None, None),
            P("row", "col", None, None, None),
            P("row", None, None, None),
            P("row", None, None, None),
            P("row", None, None, None),
            P("row", None, None, None),
            P("row", "col", None, None),
            P("row", None, None, None, None, None),
            P("row", None, None, None, None, None),
            P("row", None, None, None, None, None),
            P("row", "col", None, None, None),
            P("row", None, None, None),
            P("row", None, None, None),
            P("row", None, None, None),
            P("row", "col", None),
            P("col", None, None, None, None),
            P("col", None, None, None, None),
            P("col", None, None, None, None),
            P("row", "col", None, None, None),
            P(),
            P("row", "col"),
        ),
        out_specs=(
            P("row", "col", None, None),
            P("row", "col", None, None),
            P("row", "col", None, None),
            P("row", "col", None, None),
            P("row", "col", None, None),
        ),
        check_vma=False,
    )
```

profile of v0, /device:TPU:1, one launch (start us, length us, event | category | flops | bytes accessed | tf_op | source)
XLA Modules:
  0.0 2120.2 jit_solution(15002250182580807432)
XLA Ops:
  7.2 1.2 copy-done
  8.4 2.1 fusion.1
  19.2 113.9 %all-reduce.16.cloned.1.call-done = f32[2,192,128]{2,1,0:T(8,128)} async-done(((f32[2,192,128]{2,1,0:T(8,128)}), f32[2,192,128]{2,1,0:T(8,128)}) %all-reduce.16.cloned.1.call-update) | async-done | bytes 196624 | tf_op jit(solution)/shard_map/psum | solution.py:70
  133.2 1.4 convolution_bitcast_fusion.5
  135.8 201.1 %all-reduce.18.cloned.1.call-done = f32[4,192,128]{2,1,0:T(8,128)} async-done(((f32[4,192,128]{2,1,0:T(8,128)}), f32[4,192,128]{2,1,0:T(8,128)}) %all-reduce.18.cloned.1.call-update) | async-done | bytes 393232 | tf_op jit(solution)/shard_map/psum | solution.py:61
  336.9 1.2 fusion.49
  338.3 60.1 %psum.107 = f32[2,32,128]{2,1,0:T(8,128)S(1)} all-reduce(f32[2,32,128]{2,1,0:T(8,128)S(1)} %broadcast_multiply_fusion.9), channel_id=1, replica_groups=mesh['row'=32,'col'=16] {'col'}, use_global_device_ids=true, to_apply=%region_3.4 | all-reduce | flops 8192 | bytes 65536 | tf_op jit(solution)/shard_map/psum | solution.py:70
  398.4 4.9 collective-permute-start
  404.0 2.8 collective-permute-done
  411.9 209.3 %all-reduce.20.cloned.1.call-done = f32[2,384,128]{1,2,0:T(8,128)} async-done(((f32[2,384,128]{1,2,0:T(8,128)}), f32[2,384,128]{1,2,0:T(8,128)}) %all-reduce.20.cloned.1.call-update) | async-done | bytes 393232 | tf_op jit(solution)/shard_map/psum | solution.py:61
  621.2 1.3 fusion.15
  622.8 60.1 %psum.109 = f32[2,32,128]{2,1,0:T(8,128)S(1)} all-reduce(f32[2,32,128]{2,1,0:T(8,128)S(1)} %broadcast_multiply_fusion.8), channel_id=1, replica_groups=mesh['row'=32,'col'=16] {'col'}, use_global_device_ids=true, to_apply=%region_7.8 | all-reduce | flops 8192 | bytes 65536 | tf_op jit(solution)/shard_map/psum | solution.py:70
  682.9 1.9 collective-permute-start.1
  685.3 3.8 collective-permute-done.1
  694.4 207.3 %all-reduce.22.cloned.1.call-done = f32[2,192,128]{2,1,0:T(8,128)} async-done(((f32[2,192,128]{2,1,0:T(8,128)}), f32[2,192,128]{2,1,0:T(8,128)}) %all-reduce.22.cloned.1.call-update) | async-done | bytes 196624 | tf_op jit(solution)/shard_map/psum | solution.py:61
  903.0 60.1 %psum.111 = f32[32,128]{1,0:T(8,128)S(1)} all-reduce(f32[32,128]{1,0:T(8,128)S(1)} %fusion.155), channel_id=1, replica_groups=mesh['row'=32,'col'=16] {'col'}, use_global_device_ids=true, to_apply=%region_11.12 | all-reduce | flops 4096 | bytes 32768 | tf_op jit(solution)/shard_map/psum | solution.py:70
  963.1 8.4 collective-permute-start.2
  972.4 4.1 collective-permute-done.2
  982.9 207.6 %all-reduce.24.cloned.1.call-done = f32[384,128]{0,1:T(8,128)} async-done(((f32[384,128]{0,1:T(8,128)}), f32[384,128]{0,1:T(8,128)}) %all-reduce.24.cloned.1.call-update) | async-done | bytes 196624 | tf_op jit(solution)/shard_map/psum | solution.py:61
  1190.5 1.6 fusion.247
  1193.1 111.1 %all-reduce.26.cloned.1.call-done = f32[1,192,128]{2,1,0:T(8,128)} async-done(((f32[1,192,128]{2,1,0:T(8,128)}), f32[1,192,128]{2,1,0:T(8,128)}) %all-reduce.26.cloned.1.call-update) | async-done | bytes 98320 | tf_op jit(solution)/shard_map/psum | solution.py:70
  1307.2 90.6 %psum.114 = f32[1,2,32,128]{3,2,1,0:T(8,128)S(1)} all-reduce(f32[1,2,32,128]{3,2,1,0:T(8,128)S(1)} %maximum_multiply_fusion.3), channel_id=1, replica_groups=mesh['row'=32,'col'=16] {'row'}, use_global_device_ids=true, to_apply=%region_16.18 | all-reduce | flops 8192 | bytes 65536 | tf_op jit(solution)/shard_map/psum | solution.py:61
  1400.1 111.4 %all-reduce.28.cloned.1.call-done = f32[1,192,128]{2,1,0:T(8,128)} async-done(((f32[1,192,128]{2,1,0:T(8,128)}), f32[1,192,128]{2,1,0:T(8,128)}) %all-reduce.28.cloned.1.call-update) | async-done | bytes 98320 | tf_op jit(solution)/shard_map/psum | solution.py:70
  1515.7 184.0 %all-reduce.30.cloned.1.call-done = f32[2,2,32,128]{3,2,1,0:T(8,128)} async-done(((f32[2,2,32,128]{3,2,1,0:T(8,128)}), f32[2,2,32,128]{3,2,1,0:T(8,128)}) %all-reduce.30.cloned.1.call-update) | async-done | bytes 65552 | tf_op jit(solution)/shard_map/psum | solution.py:61
  1699.6 1.3 fusion.52
  1704.1 105.6 %all-reduce.32.cloned.1.call-done = f32[2,192,128]{2,1,0:T(8,128)} async-done(((f32[2,192,128]{2,1,0:T(8,128)}), f32[2,192,128]{2,1,0:T(8,128)}) %all-reduce.32.cloned.1.call-update) | async-done | bytes 196624 | tf_op jit(solution)/shard_map/psum | solution.py:70
  1814.3 183.6 %all-reduce.34.cloned.1.call-done = f32[2,2,32,128]{3,2,1,0:T(8,128)} async-done(((f32[2,2,32,128]{3,2,1,0:T(8,128)}), f32[2,2,32,128]{3,2,1,0:T(8,128)}) %all-reduce.34.cloned.1.call-update) | async-done | bytes 65552 | tf_op jit(solution)/shard_map/psum | solution.py:61
  1997.8 1.4 fusion.67
  1999.3 1.4 fusion.39
  2002.5 1.3 dynamic-slice_bitcast_fusion.9
  2003.8 104.2 %all-reduce.36.cloned.1.call-done = f32[2,192,128]{2,1,0:T(8,128)} async-done(((f32[2,192,128]{2,1,0:T(8,128)}), f32[2,192,128]{2,1,0:T(8,128)}) %all-reduce.36.cloned.1.call-update) | async-done | bytes 196624 | tf_op jit(solution)/shard_map/psum | solution.py:70
  2112.4 1.3 dynamic-slice_bitcast_fusion.8
  (317 shorter events, 52.6 us)
Async XLA Ops:
  7.2 126.0 %all-reduce.16.cloned.1.call-start = ((), (), s32[]{:S(2)}) async-start(), calls=%async_computation | async-start | bytes 393216 | tf_op jit(solution)/shard_map/psum | solution.py:70
  12.9 609.8 %copy-start.31 = (f32[2]{0:T(128)}, f32[2]{0:T(128)S(1)}, u32[]{:S(2)}) copy-start(f32[2]{0:T(128)S(1)} %compare_convert_fusion.1) | copy-start | bytes 28
  14.8 322.1 %all-reduce.18.cloned.1.call-start = ((), (), s32[]{:S(2)}) async-start(), calls=%async_computation.1 | async-start | bytes 786432 | tf_op jit(solution)/shard_map/psum | solution.py:61
  14.9 678.0 %copy-start.33 = (f32[2]{0:T(128)}, f32[2]{0:T(128)S(1)}, u32[]{:S(2)}) copy-start(f32[2]{0:T(128)S(1)} %compare_convert_fusion.2) | copy-start | bytes 28
  16.8 381.5 %copy-start.40 = (pred[32]{0:T(512)(128)(4,1)}, pred[32]{0:T(512)(128)(4,1)S(1)}, u32[]{:S(2)}) copy-start(pred[32]{0:T(512)(128)(4,1)S(1)} %iota_compare_fusion.1) | copy-start | bytes 100
  134.6 272.2 %copy-start.19 = (f32[1,2,2,2,96,32]{4,5,3,2,1,0:T(8,128)S(1)}, f32[1,2,2,2,96,32]{4,5,3,2,1,0:T(8,128)}, u32[]{:S(2)}) copy-start(f32[1,2,2,2,96,32]{4,5,3,2,1,0:T(8,128)} %param.38) | copy-start | bytes 294916
  135.7 274.1 %copy-start.2 = (f32[1,1,2,384,192]{3,4,2,1,0:T(8,128)S(1)}, f32[1,1,2,384,192]{3,4,2,1,0:T(8,128)}, u32[]{:S(2)}) copy-start(f32[1,1,2,384,192]{3,4,2,1,0:T(8,128)} %param.28) | copy-start | bytes 1769476
  135.7 274.1 %copy-start.29 = (f32[1,2,192,128]{3,2,1,0:T(8,128)S(1)}, f32[1,2,192,128]{3,2,1,0:T(8,128)}, u32[]{:S(2)}) copy-start(f32[1,2,192,128]{3,2,1,0:T(8,128)} %param.33) | copy-start | bytes 589828
  135.7 485.5 %all-reduce.20.cloned.1.call-start = ((), (), s32[]{:S(2)}) async-start(), calls=%async_computation.2 | async-start | bytes 786432 | tf_op jit(solution)/shard_map/psum | solution.py:61
  398.4 8.4 collective-permute-start
  404.0 278.8 %copy-start.56 = (pred[32]{0:T(512)(128)(4,1)}, pred[32]{0:T(512)(128)(4,1)S(1)}, u32[]{:S(2)}) copy-start(pred[32]{0:T(512)(128)(4,1)S(1)} %iota_compare_fusion.2) | copy-start | bytes 100
  410.4 210.8 %copy-start.15 = (f32[1,2,2,384,32]{3,4,2,1,0:T(8,128)S(1)}, f32[1,2,2,384,32]{3,4,2,1,0:T(8,128)}, u32[]{:S(2)}) copy-start(f32[1,2,2,384,32]{3,4,2,1,0:T(8,128)} %param.45) | copy-start | bytes 589828
  411.3 490.4 %all-reduce.22.cloned.1.call-start = ((), (), s32[]{:S(2)}) async-start(), calls=%async_computation.3 | async-start | bytes 393216 | tf_op jit(solution)/shard_map/psum | solution.py:61
  411.9 280.3 %copy-start.3 = (f32[1,1,2,192,192]{4,3,2,1,0:T(8,128)S(1)}, f32[1,1,2,192,192]{4,3,2,1,0:T(8,128)}, u32[]{:S(2)}) copy-start(f32[1,1,2,192,192]{4,3,2,1,0:T(8,128)} %param.27) | copy-start | bytes 884740
  411.9 280.3 %copy-start.27 = (f32[1,1,192,128]{3,2,1,0:T(8,128)S(1)}, f32[1,1,192,128]{3,2,1,0:T(8,128)}, u32[]{:S(2)}) copy-start(f32[1,1,192,128]{3,2,1,0:T(8,128)} %param.32) | copy-start | bytes 294916
  682.9 6.3 collective-permute-start.1
  692.2 209.5 %copy-start.17 = (f32[1,2,2,192,32]{3,4,2,1,0:T(8,128)S(1)}, f32[1,2,2,192,32]{3,4,2,1,0:T(8,128)}, u32[]{:S(2)}) copy-start(f32[1,2,2,192,32]{3,4,2,1,0:T(8,128)} %param.44) | copy-start | bytes 294916
  693.7 496.8 %all-reduce.24.cloned.1.call-start = ((), (), s32[]{:S(2)}) async-start(), calls=%async_computation.4 | async-start | bytes 393216 | tf_op jit(solution)/shard_map/psum | solution.py:61
  694.4 277.8 %copy-start.42 = (pred[32]{0:T(512)(128)(4,1)}, pred[32]{0:T(512)(128)(4,1)S(1)}, u32[]{:S(2)}) copy-start(pred[32]{0:T(512)(128)(4,1)S(1)} %iota_compare_fusion.3) | copy-start | bytes 100
  963.1 13.3 collective-permute-start.2
  982.6 321.6 %all-reduce.26.cloned.1.call-start = ((), (), s32[]{:S(2)}) async-start(), calls=%async_computation.5 | async-start | bytes 196608 | tf_op jit(solution)/shard_map/psum | solution.py:70
  1192.2 205.6 %copy-start.18 = (f32[1,2,2,192,32]{3,4,2,1,0:T(8,128)S(1)}, f32[1,2,2,192,32]{3,4,2,1,0:T(8,128)}, u32[]{:S(2)}) copy-start(f32[1,2,2,192,32]{3,4,2,1,0:T(8,128)} %param.44) | copy-start | bytes 294916
  1192.2 205.6 %copy-start.43 = (pred[32]{0:T(512)(128)(4,1)S(1)}, pred[32]{0:T(512)(128)(4,1)}, u32[]{:S(2)}) copy-start(pred[32]{0:T(512)(128)(4,1)} %copy-done.42) | copy-start | bytes 100
  1193.0 318.5 %all-reduce.28.cloned.1.call-start = ((), (), s32[]{:S(2)}) async-start(), calls=%async_computation.6 | async-start | bytes 196608 | tf_op jit(solution)/shard_map/psum | solution.py:70
  1400.0 299.6 %all-reduce.30.cloned.1.call-start = ((), (), s32[]{:S(2)}) async-start(), calls=%async_computation.7 | async-start | bytes 131072 | tf_op jit(solution)/shard_map/psum | solution.py:61
  1513.0 186.6 %copy-start.16 = (f32[1,2,2,384,32]{3,4,2,1,0:T(8,128)S(1)}, f32[1,2,2,384,32]{3,4,2,1,0:T(8,128)}, u32[]{:S(2)}) copy-start(f32[1,2,2,384,32]{3,4,2,1,0:T(8,128)} %param.45) | copy-start | bytes 589828
  1513.0 186.6 %copy-start.57 = (pred[32]{0:T(512)(128)(4,1)S(1)}, pred[32]{0:T(512)(128)(4,1)}, u32[]{:S(2)}) copy-start(pred[32]{0:T(512)(128)(4,1)} %copy-done.56) | copy-start | bytes 100
  1515.3 294.4 %all-reduce.32.cloned.1.call-start = ((), (), s32[]{:S(2)}) async-start(), calls=%async_computation.8 | async-start | bytes 393216 | tf_op jit(solution)/shard_map/psum | solution.py:70
  1515.4 185.6 %copy-start.11 = (f32[2,384,128]{1,2,0:T(8,128)S(1)}, f32[2,384,128]{1,2,0:T(8,128)}, u32[]{:S(2)}) copy-start(f32[2,384,128]{1,2,0:T(8,128)} %all-reduce.20.cloned.1.call-done) | copy-start | bytes 1179652
  1702.7 295.1 %copy-start.41 = (pred[32]{0:T(512)(128)(4,1)S(1)}, pred[32]{0:T(512)(128)(4,1)}, u32[]{:S(2)}) copy-start(pred[32]{0:T(512)(128)(4,1)} %copy-done.40) | copy-start | bytes 100
  1702.8 295.0 %all-reduce.34.cloned.1.call-start = ((), (), s32[]{:S(2)}) async-start(), calls=%async_computation.9 | async-start | bytes 131072 | tf_op jit(solution)/shard_map/psum | solution.py:61
  1813.5 294.5 %all-reduce.36.cloned.1.call-start = ((), (), s32[]{:S(2)}) async-start(), calls=%async_computation.10 | async-start | bytes 393216 | tf_op jit(solution)/shard_map/psum | solution.py:70
  (44 other events, 2567.4 us)
Sparse Core Ops, SparseCore 0:
  14.9 118.2 all-reduce.15
  135.8 200.9 all-reduce.17
  411.4 209.7 all-reduce.19
  693.8 207.8 all-reduce.21
  982.7 207.7 all-reduce.23
  1194.1 110.0 all-reduce.25
  1400.2 111.3 all-reduce.27
  1515.4 184.1 all-reduce.29
  1703.7 105.9 all-reduce.31
  1813.6 184.1 all-reduce.33
  2002.0 105.9 all-reduce.35
where the time goes:
time: 2120 us
  waiting for transfers between devices  1750 us (83%)
  blocking collectives  271 us (13%)
  other arithmetic  25 us (1%)
  matrix products  23.6 us (1%)
    psum x6, waiting for transfers between devices, row_total(): summed = lax.psum(slotted, 'row')  1190 us
    psum x5, waiting for transfers between devices, column_total(): summed = lax.psum(slotted, 'col')  546 us
    psum x3, blocking collectives, column_total(): summed = lax.psum(slotted, 'col')  180 us
    psum x1, blocking collectives, row_total(): summed = lax.psum(slotted, 'row')  90.6 us
  transfers between devices with their start and end apart: 14, of which 14 were waited for; matrix products, arithmetic and copies ran while one was open for 1% of the time, Pallas kernels for 0%

commit v1 on v0

v1 whole, which is shorter than its diff:
```python
import jax
import jax.numpy as jnp
from jax import lax
from jax.sharding import Mesh, PartitionSpec as P

precise = lax.Precision.HIGHEST

ROW = ("a", "e", "z", "k")
COL = ("d", "c")
CHIPS = ("a", "e", "z")
PLANE = ("k", "d", "c")


def exchange(pieces, axes):
    return lax.all_to_all(pieces, axes, 0, 0)


def share(values, axes, count):
    return exchange(jnp.broadcast_to(values[None], (count,) + values.shape), axes)


def combine(stacked):
    half = stacked.shape[-1] // 2
    real, imag = stacked[..., 0, :, :], stacked[..., 1, :, :]
    return jnp.concatenate(
        [real[..., :half] - imag[..., half:], real[..., half:] + imag[..., :half]], axis=-1
    )


def product(matrix, vector):
    return combine(jnp.einsum("...zmk,...kc->...zmc", matrix, vector, precision=precise))


def product_back(matrix, vector):
    return combine(jnp.einsum("...zkm,...kc->...zmc", matrix, vector, precision=precise))


def product_pair(matrix, left, right):
    stacked = jnp.einsum(
        "zmk,kc->zmc", matrix, jnp.concatenate([left, right], axis=-1), precision=precise
    )
    width = left.shape[-1]
    return combine(stacked[..., :width]), combine(stacked[..., width:])


def product_back_pair(matrix, left, right):
    stacked = jnp.einsum(
        "zkm,kc->zmc", matrix, jnp.concatenate([left, right], axis=-1), precision=precise
    )
    width = left.shape[-1]
    return combine(stacked[..., :width]), combine(stacked[..., width:])


def as_matrix(values):
    half = values.shape[-1] // 2
    return jnp.stack([values[..., :half], values[..., half:]], axis=-3)


def masked(values, rank_limit):
    keep = jnp.arange(values.shape[-2])[:, None] < jnp.asarray(rank_limit)[..., None, None]
    return jnp.where(keep, values, jnp.zeros_like(values))


def select(array, position):
    return lax.dynamic_index_in_dim(array, position, 0, keepdims=False)


def spread(slots, update, height):
    onehot = (jnp.arange(height)[None, :, None] == slots[:, None, :]).astype(jnp.float32)
    flat = jnp.concatenate([update[:, 0], update[:, 1]], axis=-1)
    return jnp.einsum("nhm,nmr->nhr", onehot, flat, precision=precise)


def body(
    inverse_root,
    inverse_upper,
    inverse_middle,
    inverse_lower,
    leaf_inverse,
    source_root,
    source_upper,
    source_middle,
    source_lower,
    leaf_source,
    update_root,
    update_upper,
    update_middle,
    leaf_update,
    slots_root,
    slots_upper,
    slots_middle,
    leaf_slots,
    basis_upper,
    basis_middle,
    basis_lower,
    leaf_basis,
    front_ranks,
    leaf_ranks,
):
    a, e, k, d = (lax.axis_index(name) for name in ("a", "e", "k", "d"))
    inverses = (inverse_root[0, 0], inverse_upper[0, 0], inverse_middle[0, 0], inverse_lower[0, 0])
    sources = (
        source_root[0, 0],
        source_upper[0, 0],
        select(source_middle[0], d),
        select(source_lower[0], d),
    )
    basis1 = select(basis_upper[0], a)
    basis2 = select(basis_middle[0], a)
    basis3 = select(basis_lower[0], 2 * a + e)
    rank1 = front_ranks[0:2]
    rank2 = front_ranks[2:6].reshape(2, 2)
    rank3 = front_ranks[6:14].reshape(2, 2, 2)
    leaf_rank = leaf_ranks[0, 0]
    separator, width = sources[0].shape
    half = width // 2

    all_slots = jnp.concatenate(
        [slots_root[0, 0], slots_upper[0, 0], select(slots_middle[0], d), leaf_slots[0]], axis=0
    )
    all_updates = jnp.concatenate(
        [update_root[0, 0], update_upper[0, 0], select(update_middle[0], d), leaf_update[0]], axis=0
    )
    spreads = spread(all_slots, all_updates, separator)
    rank = spreads.shape[-1] // 2
    children = [
        jnp.concatenate(
            [
                spreads[2 * h, :, :rank],
                spreads[2 * h + 1, :, :rank],
                spreads[2 * h, :, rank:],
                spreads[2 * h + 1, :, rank:],
            ],
            axis=-1,
        )
        for h in range(3)
    ]

    leaf_forward = product(leaf_inverse[0, 0], leaf_source[0, 0])
    leaf_coeffs = masked(product_back(leaf_basis[0, 0], leaf_forward), leaf_rank)
    own_spread = spreads[6]
    packed = jnp.concatenate([own_spread[: separator // 2], own_spread[separator // 2 :]], axis=-1)
    shared = share(jnp.concatenate([leaf_coeffs, packed], axis=0), ("c",), 8)
    others = shared[:, :rank]
    packs = shared[:, rank:]
    leaf_maps = jnp.concatenate([packs[..., :half], packs[..., half:]], axis=1)
    leaf_maps = jnp.stack([leaf_maps[..., :rank], leaf_maps[..., rank:]], axis=1)
    side_lower = sources[3] - product(leaf_maps, others).sum(axis=0)
    partial3 = product(inverses[3], side_lower)

    applied = [product_pair(inverses[h], sources[h], children[h]) for h in range(3)]
    low3 = product_back(basis3, partial3)
    low2 = product_back_pair(basis2, *applied[2])
    low1 = product_back_pair(basis1, *applied[1])

    rows = jnp.stack([low3, low2[0], low2[1], low1[0], low1[1]], axis=1)
    rows = exchange(rows, PLANE).reshape(2, 2, 8, 5, width).sum(axis=(0, 2))
    rows = jnp.concatenate(
        [rows[:, 0], rows[:, 1], rows[:, 2], (rows[0, 3:] + rows[1, 3:])], axis=0
    )
    got = share(rows, CHIPS, 16).reshape(2, 2, 4, 8, width).sum(axis=2)
    merged = got.sum(axis=1)
    rows = jnp.concatenate(
        [
            got[:, :, 0:2].reshape(8, width),
            merged[:, 2:4].reshape(4, width),
            merged[:, 4:6].reshape(4, width),
            merged[:, 6],
            merged[:, 7],
            jnp.zeros((4, width), jnp.float32),
        ],
        axis=0,
    )
    blocks = jnp.transpose(share(rows, PLANE, 32), (1, 0, 2))
    coeffs3 = masked(blocks[0:8].reshape(2, 2, 2, rank, width), rank3)
    total2 = blocks[8:12].reshape(2, 2, rank, width)
    gain2 = as_matrix(blocks[12:16].reshape(2, 2, rank, width))
    total1 = blocks[16:18]
    gain1 = as_matrix(blocks[18:20])
    pairs3 = jnp.transpose(coeffs3, (0, 2, 1, 3, 4)).reshape(2, 2, 2 * rank, width)
    coeffs2 = masked(total2 - product(gain2, pairs3), rank2)
    pairs2 = coeffs2.reshape(2, 2 * rank, width)
    coeffs1 = masked(total1 - product(gain1, pairs2), rank1)
    below = (coeffs1.reshape(2 * rank, width), select(pairs2, a), select(select(pairs3, a), d))

    maps = [as_matrix(applied[h][1]) for h in range(3)]
    partials = [applied[h][0] - product(maps[h], below[h]) for h in range(3)] + [partial3]
    pad = jnp.zeros((2, separator // 6, width), jnp.float32)
    halves = [p.reshape(2, p.shape[0] // 2, width) for p in partials]
    wide = jnp.concatenate([halves[0], halves[2]], axis=1).reshape(2, 16, 24, width)
    thin = jnp.concatenate([halves[1], pad, halves[3], pad], axis=1).reshape(2, 16, 16, width)
    pieces = jnp.concatenate([wide, thin], axis=2)
    pieces = exchange(pieces, ("k",)).sum(axis=0)
    sums = exchange(pieces, CHIPS).reshape(2, 2, 4, 40, width).sum(axis=2)
    upper_sums = jnp.broadcast_to(sums.sum(axis=1, keepdims=True), sums.shape)
    root_sums = jnp.broadcast_to(sums.sum(axis=(0, 1), keepdims=True), sums.shape)
    first = a == 0
    pieces = jnp.concatenate(
        [
            jnp.where(first, root_sums[:, :, :24], upper_sums[:, :, :24]),
            jnp.where(first, upper_sums[:, :, 24:], sums[:, :, 24:]),
        ],
        axis=2,
    )
    pieces = jnp.broadcast_to(pieces[:, :, None], (2, 2, 4, 40, width)).reshape(16, 40, width)
    pieces = exchange(pieces, CHIPS)
    mine = jnp.concatenate(
        [
            pieces[:8, :24].reshape(separator, width),
            pieces[8:, :24].reshape(separator, width),
            pieces[:8, 24:].reshape(128, width)[: separator // 2],
            pieces[8:, 24:].reshape(128, width)[: separator // 2],
        ],
        axis=0,
    )
    both = share(mine, ("k",), 2)
    half_rows = separator // 2
    forwards = (
        both[:, :separator].reshape(2 * separator, width),
        both[:, 2 * separator : 2 * separator + half_rows].reshape(separator, width),
        both[:, separator : 2 * separator].reshape(2 * separator, width),
        both[:, 2 * separator + half_rows :].reshape(separator, width),
    )

    lows = [product_back(maps[h], forwards[h]).reshape(2, rank, width) for h in range(3)]
    rows = jnp.transpose(jnp.concatenate(lows, axis=0), (1, 0, 2))
    rows = exchange(rows, PLANE).reshape(2, 2, 8, 6, width).sum(axis=(0, 2))
    joined = rows[0, :4] + rows[1, :4]
    pieces = jnp.stack(
        [
            jnp.stack(
                [
                    jnp.concatenate(
                        [
                            joined[to_a : to_a + 1],
                            joined[2:4],
                            rows[:, 4 + to_e],
                            jnp.zeros((3, width), jnp.float32),
                        ],
                        axis=0,
                    )
                    for to_e in range(2)
                ]
            )
            for to_a in range(2)
        ]
    )
    pieces = jnp.broadcast_to(pieces[:, :, None], (2, 2, 4, 8, width)).reshape(16, 8, width)
    got = exchange(pieces, CHIPS).reshape(2, 8, 8, width).sum(axis=1)
    near = select(got, a)
    root_row = got[0, 0:1] + got[1, 0:1]
    pieces = jnp.stack(
        [
            jnp.concatenate(
                [root_row, near[1 + to_d : 2 + to_d], near[3 + to_d : 4 + to_d], root_row], axis=0
            )
            for to_d in range(2)
        ]
    )
    pieces = jnp.broadcast_to(pieces[None, :, None], (2, 2, 8, 4, width)).reshape(32, 4, width)
    blocks = jnp.transpose(exchange(pieces, PLANE), (1, 0, 2))
    back1 = masked(blocks[0], select(rank1, a))
    gain1_own = select(gain1, a).reshape(2, rank, 2, rank)
    gain1_own = lax.dynamic_index_in_dim(gain1_own, d, 2, keepdims=False)
    back2 = masked(
        blocks[1] - product_back(gain1_own, back1), select(select(rank2, a), d)
    )
    gain2_own = select(select(gain2, a), d).reshape(2, rank, 2, rank)
    gain2_own = lax.dynamic_index_in_dim(gain2_own, e, 2, keepdims=False)
    back3 = masked(
        blocks[2] - product_back(gain2_own, back2), select(select(select(rank3, a), e), d)
    )

    residuals = (
        forwards[0],
        forwards[1] - product(basis1, back1),
        forwards[2] - product(basis2, back2),
        forwards[3] - product(basis3, back3),
    )
    solved = [product_back(inverses[h], residuals[h]) for h in range(4)]
    leaf_parts = product_back(leaf_maps, jnp.broadcast_to(solved[3][None], (8,) + solved[3].shape))
    tops = [jnp.transpose(solved[h].reshape(2, 8, 12, width), (1, 0, 2, 3)) for h in range(2)]
    tops = jnp.stack(tops, axis=2).reshape(8, 48, width)
    pieces = jnp.concatenate(
        [tops, solved[2].reshape(8, 24, width), solved[3].reshape(8, 24, width), leaf_parts], axis=1
    )
    total = exchange(pieces, ("c",)).sum(axis=0)
    tops = total[:48].reshape(2, 24, width)
    tops = select(tops, d) + lax.ppermute(select(tops, 1 - d), "d", [(0, 1), (1, 0)])
    leaf_back_coeffs = masked(total[96:], leaf_rank)
    leaf_back = leaf_forward - product(leaf_basis[0, 0], leaf_back_coeffs)
    leaf_solution = product_back(leaf_inverse[0, 0], leaf_back)
    return (
        tops[None, None, :12],
        tops[None, None, 12:],
        total[None, None, 48:72],
        total[None, None, 72:96],
        leaf_solution[None, None],
    )


def solution(mesh):
    fine = Mesh(mesh.devices.reshape(2, 2, 4, 2, 2, 8), ROW + COL)
    tile = (ROW, COL)
    in_specs = (
        [P(*tile, None, None, None)] * 5
        + [P(ROW, None, None, None)] * 4
        + [P(*tile, None, None)]
        + [P(ROW, None, None, None, None, None)] * 3
        + [P(*tile, None, None, None)]
        + [P(ROW, None, None, None)] * 3
        + [P(*tile, None)]
        + [P(COL, None, None, None, None)] * 3
        + [P(*tile, None, None, None), P(), P(*tile)]
    )
    return jax.shard_map(
        body,
        mesh=fine,
        in_specs=tuple(in_specs),
        out_specs=(P(*tile, None, None),) * 5,
        check_vma=False,
    )
```

time: 2120 us -> 249 us (0.12)
  waiting for transfers between devices: 1750 us -> 83 us
  blocking collectives: 271 us -> 15.9 us
  starting transfers between devices: 15.9 us -> 71.9 us
    psum x11 -> x0, waiting for transfers between devices: 1740 us -> none  [the longest x6 1190 us: row_total(): summed = lax.psum(slotted, 'row')]
    psum x4 -> x0, blocking collectives: 271 us -> none  [the longest x3 180 us: column_total(): summed = lax.psum(slotted, 'col')]
    all_to_all x0 -> x10, waiting for transfers between devices: none -> 82.3 us  [exchange(): return lax.all_to_all(pieces, axes, 0, 0)]
    all_to_all x0 -> x10, starting transfers between devices: none -> 69.2 us  [exchange(): return lax.all_to_all(pieces, axes, 0, 0)]
  transfers between devices with their start and end apart: 14 -> 11, of which waited for: 14 -> 10; matrix products, arithmetic and copies ran while one was open for 1% -> 10% of each run, Pallas kernels for 0% -> 0%
where the time goes in v1:
time: 249 us; the launch traced here: 247 us
  waiting for transfers between devices  83 us (33%)
  starting transfers between devices  71.9 us (29%)
  local copies, waits for them, and re-layouts  35.5 us (14%)
  matrix products  20 us (8%)
  other arithmetic  17.3 us (7%)
  blocking collectives  15.9 us (6%)
  between operations  3.66 us (1%)
    all_to_all x10, waiting for transfers between devices, exchange(): return lax.all_to_all(pieces, axes, 0, 0)  82.3 us
    all_to_all x10, starting transfers between devices, exchange(): return lax.all_to_all(pieces, axes, 0, 0)  69.2 us
    all_to_all x2, blocking collectives, exchange(): return lax.all_to_all(pieces, axes, 0, 0)  15.9 us
    dot_general x12, matrix products, product(): jnp.einsum('...zmk,...kc->...zmc', matrix, vector, precision=precise)  9.05 us
    concatenate x12, local copies, waits for them, and re-layouts, combine(): jnp.concatenate([real[..., :half] - imag[..., half:], real[..., half:] +...  7.85 us
    unnamed x177, local copies, waits for them, and re-layouts  6.5 us
    sub x32, other arithmetic, combine(): real[..., :half] - imag[..., half:]  5.91 us
  transfers between devices with their start and end apart: 11, of which 10 were waited for; matrix products, arithmetic and copies ran while one was open for 10% of the time, Pallas kernels for 0%

profile of v1, /device:TPU:1, one launch (start us, length us, event | category | flops | bytes accessed | tf_op | source)
XLA Modules:
  0.0 247.2 jit_solution(4581420699704058673)
XLA Ops:
  0.7 0.9 copy.371
  4.9 1.2 fusion.1
  8.7 6.0 %all-to-all-start = ((f32[8,128,128]{2,1,0:T(8,128)}), f32[8,128,128]{2,1,0:T(8,128)S(1)}, u32[]{:S(2)}, u32[]{:S(2)}) async-start(f32[8,128,128]{2,1,0:T(8,128)} %broadcast_in_dim.149), calls=%async_computation | async-start | bytes 1048576 | tf_op jit(solution)/shard_map/all_to_all | solution.py:15
  27.0 2.7 %fusion.9 = f32[8,2,192,128]{3,2,1,0:T(8,128)S(1)} fusion(f32[8,1,192,32]{2,3,1,0:T(8,128)S(1)} %copy.279, f32[8,1,192,32]{2,3,1,0:T(8,128)S(1)} %copy.278, f32[8,128,128]{2,1,0:T(8,128)S(1)} %all-to-all-done), kind=kOutput, calls=%fused_computation.26 | convolution fusion | flops 151093248 | bytes 2228224 | tf_op jit(solution)/shard_map/...zmk,...kc->...zmc/dot_general | solution.py:31
  32.2 1.1 fusion.51
  34.5 10.3 %all-to-all-start.1 = ((f32[32,5,128]{2,1,0:T(8,128)}), f32[32,5,128]{2,1,0:T(8,128)S(1)}, u32[]{:S(2)}, u32[]{:S(2)}) async-start(f32[32,5,128]{2,1,0:T(8,128)} %copy.290), calls=%async_computation.1 | async-start | bytes 262144 | tf_op jit(solution)/shard_map/all_to_all | solution.py:15
  45.3 7.1 %all-to-all-done.1 = f32[32,5,128]{2,1,0:T(8,128)S(1)} async-done(((f32[32,5,128]{2,1,0:T(8,128)}), f32[32,5,128]{2,1,0:T(8,128)S(1)}, u32[]{:S(2)}, u32[]{:S(2)}) %all-to-all-start.1) | async-done | bytes 81952 | tf_op jit(solution)/shard_map/all_to_all | solution.py:15
  53.1 12.9 %all-to-all-start.2 = ((f32[16,8,128]{2,1,0:T(8,128)}), f32[16,8,128]{2,1,0:T(8,128)S(1)}, u32[]{:S(2)}, u32[]{:S(2)}) async-start(f32[16,8,128]{2,1,0:T(8,128)} %broadcast_in_dim.150), calls=%async_computation.2 | async-start | bytes 131072 | tf_op jit(solution)/shard_map/all_to_all | solution.py:15
  69.4 8.1 %all-to-all-done.2 = f32[16,8,128]{2,1,0:T(8,128)S(1)} async-done(((f32[16,8,128]{2,1,0:T(8,128)}), f32[16,8,128]{2,1,0:T(8,128)S(1)}, u32[]{:S(2)}, u32[]{:S(2)}) %all-to-all-start.2) | async-done | bytes 65568 | tf_op jit(solution)/shard_map/all_to_all | solution.py:15
  78.4 5.8 %all-to-all-start.3 = ((f32[32,24,128]{2,1,0:T(8,128)}), f32[32,24,128]{2,1,0:T(8,128)S(1)}, u32[]{:S(2)}, u32[]{:S(2)}) async-start(f32[32,24,128]{2,1,0:T(8,128)} %broadcast_in_dim.152), calls=%async_computation.3 | async-start | bytes 786432 | tf_op jit(solution)/shard_map/all_to_all | solution.py:15
  85.0 8.9 %all-to-all-done.3 = f32[32,24,128]{2,1,0:T(8,128)S(1)} async-done(((f32[32,24,128]{2,1,0:T(8,128)}), f32[32,24,128]{2,1,0:T(8,128)S(1)}, u32[]{:S(2)}, u32[]{:S(2)}) %all-to-all-start.3) | async-done | bytes 393248 | tf_op jit(solution)/shard_map/all_to_all | solution.py:15
  100.4 1.7 copy.343
  103.1 1.3 maximum_subtract_fusion.1
  104.4 1.1 maximum_subtract_fusion
  105.8 5.1 %all_to_all.60 = f32[2,16,40,128]{3,2,1,0:T(8,128)S(1)} all-to-all(f32[2,16,40,128]{3,2,1,0:T(8,128)S(1)} %pad_maximum_fusion.1), channel_id=1, replica_groups=mesh['a'=2,'e'=2,'z'=4,'k'=2,'d'=2,'c'=8] {'k'}, dimensions={0} | all-to-all | bytes 1310720 | tf_op jit(solution)/shard_map/all_to_all | solution.py:15
  111.7 3.5 %all-to-all-start.5 = ((f32[16,40,128]{2,1,0:T(8,128)}), f32[16,40,128]{2,1,0:T(8,128)S(1)}, u32[]{:S(2)}, u32[]{:S(2)}) async-start(f32[16,40,128]{2,1,0:T(8,128)} %reduce_sum.106), calls=%async_computation.5 | async-start | bytes 655360 | tf_op jit(solution)/shard_map/all_to_all | solution.py:15
  115.3 15.7 %all-to-all-done.5 = f32[16,40,128]{2,1,0:T(8,128)S(1)} async-done(((f32[16,40,128]{2,1,0:T(8,128)}), f32[16,40,128]{2,1,0:T(8,128)S(1)}, u32[]{:S(2)}, u32[]{:S(2)}) %all-to-all-start.5) | async-done | bytes 327712 | tf_op jit(solution)/shard_map/all_to_all | solution.py:15
  131.8 11.5 %all-to-all-start.6 = ((f32[16,40,128]{2,1,0:T(8,128)}), f32[16,40,128]{2,1,0:T(8,128)S(1)}, u32[]{:S(2)}, u32[]{:S(2)}) async-start(f32[16,40,128]{2,1,0:T(8,128)} %bitcast.162), calls=%async_computation.6 | async-start | bytes 655360 | tf_op jit(solution)/shard_map/all_to_all | solution.py:15
  145.1 0.9 copy.317
  150.6 7.8 %all-to-all-done.6 = f32[16,40,128]{2,1,0:T(8,128)S(1)} async-done(((f32[16,40,128]{2,1,0:T(8,128)}), f32[16,40,128]{2,1,0:T(8,128)S(1)}, u32[]{:S(2)}, u32[]{:S(2)}) %all-to-all-start.6) | async-done | bytes 327712 | tf_op jit(solution)/shard_map/all_to_all | solution.py:15
  158.6 10.8 %all_to_all.61 = f32[2,576,128]{2,1,0:T(8,128)S(1)} all-to-all(f32[2,576,128]{2,1,0:T(8,128)S(1)} %broadcast_in_dim.161), channel_id=1, replica_groups=mesh['a'=2,'e'=2,'z'=4,'k'=2,'d'=2,'c'=8] {'k'}, dimensions={0} | all-to-all | bytes 1179648 | tf_op jit(solution)/shard_map/all_to_all | solution.py:15
  172.0 4.0 %all-to-all-start.8 = ((f32[32,6,128]{2,1,0:T(8,128)}), f32[32,6,128]{2,1,0:T(8,128)S(1)}, u32[]{:S(2)}, u32[]{:S(2)}) async-start(f32[32,6,128]{2,1,0:T(8,128)} %maximum_bitcast_fusion.6), calls=%async_computation.8 | async-start | bytes 262144 | tf_op jit(solution)/shard_map/all_to_all | solution.py:15
  176.6 6.9 %all-to-all-done.8 = f32[32,6,128]{2,1,0:T(8,128)S(1)} async-done(((f32[32,6,128]{2,1,0:T(8,128)}), f32[32,6,128]{2,1,0:T(8,128)S(1)}, u32[]{:S(2)}, u32[]{:S(2)}) %all-to-all-start.8) | async-done | bytes 98336 | tf_op jit(solution)/shard_map/all_to_all | solution.py:15
  184.3 5.7 %all-to-all-start.9 = ((f32[16,8,128]{2,1,0:T(8,128)}), f32[16,8,128]{2,1,0:T(8,128)S(1)}, u32[]{:S(2)}, u32[]{:S(2)}) async-start(f32[16,8,128]{2,1,0:T(8,128)} %bitcast.205), calls=%async_computation.9 | async-start | bytes 131072 | tf_op jit(solution)/shard_map/all_to_all | solution.py:15
  190.2 11.4 %all-to-all-done.9 = f32[16,8,128]{2,1,0:T(8,128)S(1)} async-done(((f32[16,8,128]{2,1,0:T(8,128)}), f32[16,8,128]{2,1,0:T(8,128)S(1)}, u32[]{:S(2)}, u32[]{:S(2)}) %all-to-all-start.9) | async-done | bytes 65568 | tf_op jit(solution)/shard_map/all_to_all | solution.py:15
  202.3 5.8 %all-to-all-start.10 = ((f32[32,4,128]{2,1,0:T(4,128)}), f32[32,4,128]{2,1,0:T(4,128)S(1)}, u32[]{:S(2)}, u32[]{:S(2)}) async-start(f32[32,4,128]{2,1,0:T(4,128)} %bitcast.214), calls=%async_computation.10 | async-start | bytes 131072 | tf_op jit(solution)/shard_map/all_to_all | solution.py:15
  208.9 6.3 %all-to-all-done.10 = f32[32,4,128]{2,1,0:T(4,128)S(1)} async-done(((f32[32,4,128]{2,1,0:T(4,128)}), f32[32,4,128]{2,1,0:T(4,128)S(1)}, u32[]{:S(2)}, u32[]{:S(2)}) %all-to-all-start.10) | async-done | bytes 65568 | tf_op jit(solution)/shard_map/all_to_all | solution.py:15
  217.1 1.4 fusion.64
  220.2 0.9 fusion.4
  225.5 3.6 %all-to-all-start.11 = ((f32[8,128,128]{2,1,0:T(8,128)}), f32[8,128,128]{2,1,0:T(8,128)S(1)}, u32[]{:S(2)}, u32[]{:S(2)}) async-start(f32[8,128,128]{2,1,0:T(8,128)} %copy.322), calls=%async_computation.11 | async-start | bytes 1048576 | tf_op jit(solution)/shard_map/all_to_all | solution.py:15
  229.2 10.2 %all-to-all-done.11 = f32[8,128,128]{2,1,0:T(8,128)S(1)} async-done(((f32[8,128,128]{2,1,0:T(8,128)}), f32[8,128,128]{2,1,0:T(8,128)S(1)}, u32[]{:S(2)}, u32[]{:S(2)}) %all-to-all-start.11) | async-done | bytes 524320 | tf_op jit(solution)/shard_map/all_to_all | solution.py:15
  240.0 2.8 %collective-permute-start = (f32[24,128]{1,0:T(8,128)S(1)}, f32[24,128]{1,0:T(8,128)S(1)}, u32[]{:S(2)}, u32[]{:S(2)}) collective-permute-start(f32[24,128]{1,0:T(8,128)S(1)} %dynamic-slice_bitcast_fusion.1), channel_id=1, source_target_pairs={{0,8},{8,0},{1,9},{9,1},{2,10},{10,2},{3,11},{11,3},{4,12},{12,4},... | collective-permute-start | bytes 36872 | tf_op jit(solution)/shard_map/ppermute | solution.py:289
  (442 shorter events, 60.1 us)
Async XLA Ops:
  8.7 17.2 %all-to-all-start = ((f32[8,128,128]{2,1,0:T(8,128)}), f32[8,128,128]{2,1,0:T(8,128)S(1)}, u32[]{:S(2)}, u32[]{:S(2)}) async-start(f32[8,128,128]{2,1,0:T(8,128)} %broadcast_in_dim.149), calls=%async_computation | async-start | bytes 1048576 | tf_op jit(solution)/shard_map/all_to_all | solution.py:15
  31.9 13.0 %copy-start.38 = (f32[384,128]{0,1:T(8,128)S(1)}, f32[384,128]{0,1:T(8,128)}, u32[]{:S(2)}) copy-start(f32[384,128]{0,1:T(8,128)} %get-tuple-element.40) | copy-start | bytes 589828
  31.9 13.0 %copy-start.84 = (s32[14]{0:T(128)S(1)}, s32[14]{0:T(128)}, u32[]{:S(2)}) copy-start(s32[14]{0:T(128)} %param.46) | copy-start | bytes 172
  32.0 34.0 %copy-start.55 = (f32[384,64]{0,1:T(8,128)S(1)}, f32[384,64]{0,1:T(8,128)}, u32[]{:S(2)}) copy-start(f32[384,64]{0,1:T(8,128)} %copy-done.54) | copy-start | bytes 294916
  32.1 34.7 %copy-start.30 = (f32[192,128]{1,0:T(8,128)}, f32[192,128]{1,0:T(8,128)S(1)}, u32[]{:S(2)}) copy-start(f32[192,128]{1,0:T(8,128)S(1)} %pad_maximum_fusion.26) | copy-start | bytes 294916
  32.2 34.7 %copy-start.53 = (f32[384,64]{0,1:T(8,128)S(1)}, f32[384,64]{0,1:T(8,128)}, u32[]{:S(2)}) copy-start(f32[384,64]{0,1:T(8,128)} %copy-done.52) | copy-start | bytes 294916
  34.5 17.8 %all-to-all-start.1 = ((f32[32,5,128]{2,1,0:T(8,128)}), f32[32,5,128]{2,1,0:T(8,128)S(1)}, u32[]{:S(2)}, u32[]{:S(2)}) async-start(f32[32,5,128]{2,1,0:T(8,128)} %copy.290), calls=%async_computation.1 | async-start | bytes 262144 | tf_op jit(solution)/shard_map/all_to_all | solution.py:15
  53.1 24.4 %all-to-all-start.2 = ((f32[16,8,128]{2,1,0:T(8,128)}), f32[16,8,128]{2,1,0:T(8,128)S(1)}, u32[]{:S(2)}, u32[]{:S(2)}) async-start(f32[16,8,128]{2,1,0:T(8,128)} %broadcast_in_dim.150), calls=%async_computation.2 | async-start | bytes 131072 | tf_op jit(solution)/shard_map/all_to_all | solution.py:15
  66.8 17.4 %copy-start.85 = (s32[14]{0:T(128)S(1)}, s32[14]{0:T(128)}, u32[]{:S(2)}) copy-start(s32[14]{0:T(128)} %param.46) | copy-start | bytes 172
  66.8 17.4 %copy-start.36 = (f32[384,128]{0,1:T(8,128)S(1)}, f32[384,128]{0,1:T(8,128)}, u32[]{:S(2)}) copy-start(f32[384,128]{0,1:T(8,128)} %get-tuple-element.38) | copy-start | bytes 589828
  66.8 17.4 %copy-start.37 = (f32[384,128]{0,1:T(8,128)S(1)}, f32[384,128]{0,1:T(8,128)}, u32[]{:S(2)}) copy-start(f32[384,128]{0,1:T(8,128)} %get-tuple-element.39) | copy-start | bytes 589828
  78.4 15.4 %all-to-all-start.3 = ((f32[32,24,128]{2,1,0:T(8,128)}), f32[32,24,128]{2,1,0:T(8,128)S(1)}, u32[]{:S(2)}, u32[]{:S(2)}) async-start(f32[32,24,128]{2,1,0:T(8,128)} %broadcast_in_dim.152), calls=%async_computation.3 | async-start | bytes 786432 | tf_op jit(solution)/shard_map/all_to_all | solution.py:15
  84.9 14.2 %copy-start.20 = (f32[1,384,64]{1,2,0:T(8,128)}, f32[1,384,64]{1,2,0:T(8,128)S(1)}, u32[]{:S(2)}) copy-start(f32[1,384,64]{1,2,0:T(8,128)S(1)} %get-tuple-element.84) | copy-start | bytes 294916
  111.7 19.2 %all-to-all-start.5 = ((f32[16,40,128]{2,1,0:T(8,128)}), f32[16,40,128]{2,1,0:T(8,128)S(1)}, u32[]{:S(2)}, u32[]{:S(2)}) async-start(f32[16,40,128]{2,1,0:T(8,128)} %reduce_sum.106), calls=%async_computation.5 | async-start | bytes 655360 | tf_op jit(solution)/shard_map/all_to_all | solution.py:15
  115.2 28.1 %copy-start.86 = (s32[14]{0:T(128)S(1)}, s32[14]{0:T(128)}, u32[]{:S(2)}) copy-start(s32[14]{0:T(128)} %param.46) | copy-start | bytes 172
  131.0 15.1 %copy-start.7 = (f32[1,1,2,192,192]{4,3,2,1,0:T(8,128)S(1)}, f32[1,1,2,192,192]{4,3,2,1,0:T(8,128)}, u32[]{:S(2)}) copy-start(f32[1,1,2,192,192]{4,3,2,1,0:T(8,128)} %param.25) | copy-start | bytes 884740
  131.8 17.2 %copy-start.46 = (f32[2,2,1,32,64]{4,3,2,1,0:T(8,128)S(1)}, f32[2,2,1,32,64]{4,3,2,1,0:T(8,128)}, u32[]{:S(2)}) copy-start(f32[2,2,1,32,64]{4,3,2,1,0:T(8,128)} %copy-done.45) | copy-start | bytes 98308
  131.8 17.2 %copy-start.48 = (f32[2,2,1,32,64]{4,3,2,1,0:T(8,128)S(1)}, f32[2,2,1,32,64]{4,3,2,1,0:T(8,128)}, u32[]{:S(2)}) copy-start(f32[2,2,1,32,64]{4,3,2,1,0:T(8,128)} %copy-done.47) | copy-start | bytes 98308
  131.8 17.4 %copy-start.58 = (f32[2,1,32,64]{3,2,1,0:T(8,128)S(1)}, f32[2,1,32,64]{3,2,1,0:T(8,128)}, u32[]{:S(2)}) copy-start(f32[2,1,32,64]{3,2,1,0:T(8,128)} %copy-done.57) | copy-start | bytes 49156
  131.8 17.4 %copy-start.60 = (f32[2,1,32,64]{3,2,1,0:T(8,128)S(1)}, f32[2,1,32,64]{3,2,1,0:T(8,128)}, u32[]{:S(2)}) copy-start(f32[2,1,32,64]{3,2,1,0:T(8,128)} %copy-done.59) | copy-start | bytes 49156
  131.8 26.6 %all-to-all-start.6 = ((f32[16,40,128]{2,1,0:T(8,128)}), f32[16,40,128]{2,1,0:T(8,128)S(1)}, u32[]{:S(2)}, u32[]{:S(2)}) async-start(f32[16,40,128]{2,1,0:T(8,128)} %bitcast.162), calls=%async_computation.6 | async-start | bytes 655360 | tf_op jit(solution)/shard_map/all_to_all | solution.py:15
  172.0 11.5 %all-to-all-start.8 = ((f32[32,6,128]{2,1,0:T(8,128)}), f32[32,6,128]{2,1,0:T(8,128)S(1)}, u32[]{:S(2)}, u32[]{:S(2)}) async-start(f32[32,6,128]{2,1,0:T(8,128)} %maximum_bitcast_fusion.6), calls=%async_computation.8 | async-start | bytes 262144 | tf_op jit(solution)/shard_map/all_to_all | solution.py:15
  183.5 31.7 %copy-start.63 = (f32[1,2,2,192,32]{3,4,2,1,0:T(8,128)S(1)}, f32[1,2,2,192,32]{3,4,2,1,0:T(8,128)}, u32[]{:S(2)}) copy-start(f32[1,2,2,192,32]{3,4,2,1,0:T(8,128)} %param.42) | copy-start | bytes 294916
  184.3 17.3 %all-to-all-start.9 = ((f32[16,8,128]{2,1,0:T(8,128)}), f32[16,8,128]{2,1,0:T(8,128)S(1)}, u32[]{:S(2)}, u32[]{:S(2)}) async-start(f32[16,8,128]{2,1,0:T(8,128)} %bitcast.205), calls=%async_computation.9 | async-start | bytes 131072 | tf_op jit(solution)/shard_map/all_to_all | solution.py:15
  190.1 25.7 %copy-start.65 = (f32[2,32,1,32]{3,2,1,0:T(1,128)S(1)}, f32[2,32,1,32]{3,2,1,0:T(1,128)}, u32[]{:S(2)}) copy-start(f32[2,32,1,32]{3,2,1,0:T(1,128)} %constant_dynamic-slice_fusion.1) | copy-start | bytes 24580
  190.1 26.2 %copy-start.76 = (f32[1,2,2,384,32]{3,4,2,1,0:T(8,128)S(1)}, f32[1,2,2,384,32]{3,4,2,1,0:T(8,128)}, u32[]{:S(2)}) copy-start(f32[1,2,2,384,32]{3,4,2,1,0:T(8,128)} %param.43) | copy-start | bytes 589828
  201.7 15.1 %copy-start.64 = (f32[2,32,1,32]{3,2,1,0:T(1,128)S(1)}, f32[2,32,1,32]{3,2,1,0:T(1,128)}, u32[]{:S(2)}) copy-start(f32[2,32,1,32]{3,2,1,0:T(1,128)} %constant_dynamic-slice_fusion) | copy-start | bytes 24580
  202.3 12.9 %all-to-all-start.10 = ((f32[32,4,128]{2,1,0:T(4,128)}), f32[32,4,128]{2,1,0:T(4,128)S(1)}, u32[]{:S(2)}, u32[]{:S(2)}) async-start(f32[32,4,128]{2,1,0:T(4,128)} %bitcast.214), calls=%async_computation.10 | async-start | bytes 131072 | tf_op jit(solution)/shard_map/all_to_all | solution.py:15
  225.5 17.4 %copy-start.51 = (f32[1,1,2,384,32]{3,4,2,1,0:T(8,128)S(1)}, f32[1,1,2,384,32]{3,4,2,1,0:T(8,128)}, u32[]{:S(2)}) copy-start(f32[1,1,2,384,32]{3,4,2,1,0:T(8,128)} %param.45) | copy-start | bytes 294916
  225.5 17.4 %copy-start.80 = (pred[32]{0:T(512)(128)(4,1)S(1)}, pred[32]{0:T(512)(128)(4,1)}, u32[]{:S(2)}) copy-start(pred[32]{0:T(512)(128)(4,1)} %copy-done.79) | copy-start | bytes 100
  225.5 13.8 %all-to-all-start.11 = ((f32[8,128,128]{2,1,0:T(8,128)}), f32[8,128,128]{2,1,0:T(8,128)S(1)}, u32[]{:S(2)}, u32[]{:S(2)}) async-start(f32[8,128,128]{2,1,0:T(8,128)} %copy.322), calls=%async_computation.11 | async-start | bytes 1048576 | tf_op jit(solution)/shard_map/all_to_all | solution.py:15
  240.0 5.9 %collective-permute-start = (f32[24,128]{1,0:T(8,128)S(1)}, f32[24,128]{1,0:T(8,128)S(1)}, u32[]{:S(2)}, u32[]{:S(2)}) collective-permute-start(f32[24,128]{1,0:T(8,128)S(1)} %dynamic-slice_bitcast_fusion.1), channel_id=1, source_target_pairs={{0,8},{8,0},{1,9},{9,1},{2,10},{10,2},{3,11},{11,3},{4,12},{12,4},... | collective-permute-start | bytes 36872 | tf_op jit(solution)/shard_map/ppermute | solution.py:289
  (66 other events, 178.9 us)

commit v2 on v1

--- a/solution.py
+++ b/solution.py
@@ -17,6 +17,14 @@
 
 def share(values, axes, count):
     return exchange(jnp.broadcast_to(values[None], (count,) + values.shape), axes)
+
+
+def partner(values, axis):
+    return lax.ppermute(values, axis, [(0, 1), (1, 0)])
+
+
+def fold(halves, place):
+    return select(halves, place) + partner(select(halves, 1 - place), "k")
 
 
 def combine(stacked):
@@ -136,6 +144,17 @@
         for h in range(3)
     ]
 
+    applied = [product_pair(inverses[h], sources[h], children[h]) for h in range(3)]
+    pad = jnp.zeros((2, separator // 6, width), jnp.float32)
+    parts = []
+    for side in range(2):
+        first_half = [applied[h][side].reshape(2, -1, width) for h in range(3)]
+        wide = jnp.concatenate([first_half[0], first_half[2]], axis=1)
+        thin = jnp.concatenate([first_half[1], pad], axis=1)
+        parts += [wide.reshape(2, 16, 24, width), thin.reshape(2, 16, 8, width)]
+    pieces = jnp.concatenate([parts[0], parts[2], parts[1], parts[3]], axis=2)
+    applied_pieces = fold(pieces, k)
+
     leaf_forward = product(leaf_inverse[0, 0], leaf_source[0, 0])
     leaf_coeffs = masked(product_back(leaf_basis[0, 0], leaf_forward), leaf_rank)
     own_spread = spreads[6]
@@ -148,17 +167,24 @@
     side_lower = sources[3] - product(leaf_maps, others).sum(axis=0)
     partial3 = product(inverses[3], side_lower)
 
-    applied = [product_pair(inverses[h], sources[h], children[h]) for h in range(3)]
     low3 = product_back(basis3, partial3)
     low2 = product_back_pair(basis2, *applied[2])
     low1 = product_back_pair(basis1, *applied[1])
+    thin = jnp.concatenate([partial3.reshape(2, -1, width), pad], axis=1)
+    lower_pieces = fold(thin.reshape(2, 16, 8, width), k)
 
     rows = jnp.stack([low3, low2[0], low2[1], low1[0], low1[1]], axis=1)
     rows = exchange(rows, PLANE).reshape(2, 2, 8, 5, width).sum(axis=(0, 2))
     rows = jnp.concatenate(
         [rows[:, 0], rows[:, 1], rows[:, 2], (rows[0, 3:] + rows[1, 3:])], axis=0
     )
-    got = share(rows, CHIPS, 16).reshape(2, 2, 4, 8, width).sum(axis=2)
+    pieces = jnp.concatenate(
+        [jnp.broadcast_to(rows[None], (16, 8, width)), lower_pieces, applied_pieces], axis=1
+    )
+    slices = exchange(pieces, CHIPS).reshape(2, 2, 4, 80, width).sum(axis=2)
+    sums = slices[:, :, 16:].sum(axis=1)
+    got = slices[:, :, :16]
+    lower_slices = got[:, :, 8:]
     merged = got.sum(axis=1)
     rows = jnp.concatenate(
         [
@@ -181,61 +207,41 @@
     coeffs2 = masked(total2 - product(gain2, pairs3), rank2)
     pairs2 = coeffs2.reshape(2, 2 * rank, width)
     coeffs1 = masked(total1 - product(gain1, pairs2), rank1)
-    below = (coeffs1.reshape(2 * rank, width), select(pairs2, a), select(select(pairs3, a), d))
-
-    maps = [as_matrix(applied[h][1]) for h in range(3)]
-    partials = [applied[h][0] - product(maps[h], below[h]) for h in range(3)] + [partial3]
-    pad = jnp.zeros((2, separator // 6, width), jnp.float32)
-    halves = [p.reshape(2, p.shape[0] // 2, width) for p in partials]
-    wide = jnp.concatenate([halves[0], halves[2]], axis=1).reshape(2, 16, 24, width)
-    thin = jnp.concatenate([halves[1], pad, halves[3], pad], axis=1).reshape(2, 16, 16, width)
-    pieces = jnp.concatenate([wide, thin], axis=2)
-    pieces = exchange(pieces, ("k",)).sum(axis=0)
-    sums = exchange(pieces, CHIPS).reshape(2, 2, 4, 40, width).sum(axis=2)
-    upper_sums = jnp.broadcast_to(sums.sum(axis=1, keepdims=True), sums.shape)
-    root_sums = jnp.broadcast_to(sums.sum(axis=(0, 1), keepdims=True), sums.shape)
+    pair1 = coeffs1.reshape(2 * rank, width)
+
     first = a == 0
-    pieces = jnp.concatenate(
-        [
-            jnp.where(first, root_sums[:, :, :24], upper_sums[:, :, :24]),
-            jnp.where(first, upper_sums[:, :, 24:], sums[:, :, 24:]),
-        ],
-        axis=2,
-    )
-    pieces = jnp.broadcast_to(pieces[:, :, None], (2, 2, 4, 40, width)).reshape(16, 40, width)
-    pieces = exchange(pieces, CHIPS)
-    mine = jnp.concatenate(
-        [
-            pieces[:8, :24].reshape(separator, width),
-            pieces[8:, :24].reshape(separator, width),
-            pieces[:8, 24:].reshape(128, width)[: separator // 2],
-            pieces[8:, 24:].reshape(128, width)[: separator // 2],
-        ],
-        axis=0,
-    )
-    both = share(mine, ("k",), 2)
-    half_rows = separator // 2
-    forwards = (
-        both[:, :separator].reshape(2 * separator, width),
-        both[:, 2 * separator : 2 * separator + half_rows].reshape(separator, width),
-        both[:, separator : 2 * separator].reshape(2 * separator, width),
-        both[:, 2 * separator + half_rows :].reshape(separator, width),
-    )
-
-    lows = [product_back(maps[h], forwards[h]).reshape(2, rank, width) for h in range(3)]
-    rows = jnp.transpose(jnp.concatenate(lows, axis=0), (1, 0, 2))
-    rows = exchange(rows, PLANE).reshape(2, 2, 8, 6, width).sum(axis=(0, 2))
-    joined = rows[0, :4] + rows[1, :4]
+    wide = jnp.where(first, jnp.broadcast_to(sums.sum(axis=0), sums.shape), sums)[:, :48]
+    wide_below = jnp.where(
+        first, pair1[None], lax.dynamic_index_in_dim(pairs3, d, 1, keepdims=False)
+    )
+    wide_map = as_matrix(wide[:, 24:])
+    wide_forward = wide[:, :24] - product(wide_map, wide_below)
+    upper_map = as_matrix(sums[:, 56:])
+    upper_forward = sums[:, 48:56] - product(upper_map, pairs2)
+
+    wide_low = product_back(wide_map, wide_forward).reshape(4, rank, width)
+    upper_low = product_back(upper_map, upper_forward).reshape(4, rank, width)
+    rows = jnp.transpose(jnp.concatenate([wide_low, upper_low], axis=0), (1, 0, 2))
+    rows = exchange(rows, PLANE).reshape(2, 2, 8, 8, width).sum(axis=(0, 2))
+    joined = rows[0] + rows[1]
+    nothing = jnp.zeros((1, width), jnp.float32)
+    tail = jnp.zeros((4, width), jnp.float32)
     pieces = jnp.stack(
         [
             jnp.stack(
                 [
                     jnp.concatenate(
                         [
-                            joined[to_a : to_a + 1],
-                            joined[2:4],
-                            rows[:, 4 + to_e],
-                            jnp.zeros((3, width), jnp.float32),
+                            wide_forward[to_a],
+                            upper_forward[to_a],
+                            lower_slices[to_a, to_e],
+                            jnp.where(
+                                first,
+                                jnp.concatenate([joined[to_a : to_a + 1], nothing], axis=0),
+                                rows[:, 2 * to_a + to_e],
+                            ),
+                            joined[4 + 2 * to_a : 6 + 2 * to_a],
+                            tail,
                         ],
                         axis=0,
                     )
@@ -245,14 +251,33 @@
             for to_a in range(2)
         ]
     )
-    pieces = jnp.broadcast_to(pieces[:, :, None], (2, 2, 4, 8, width)).reshape(16, 8, width)
-    got = exchange(pieces, CHIPS).reshape(2, 8, 8, width).sum(axis=1)
-    near = select(got, a)
-    root_row = got[0, 0:1] + got[1, 0:1]
+    pieces = jnp.broadcast_to(pieces[:, :, None], (2, 2, 4, 48, width)).reshape(16, 48, width)
+    got = exchange(pieces, CHIPS)
+    half_rows = separator // 2
+    mine = jnp.concatenate(
+        [
+            got[:8, :24].reshape(separator, width),
+            got[8:, :24].reshape(separator, width),
+            got[:, 24:32].reshape(128, width)[:half_rows],
+            got[:, 32:40].reshape(128, width)[:half_rows],
+        ],
+        axis=0,
+    )
+    theirs = partner(mine, "k")
+    both = jnp.stack([jnp.where(k == 0, mine, theirs), jnp.where(k == 0, theirs, mine)])
+    forwards = (
+        both[:, :separator].reshape(2 * separator, width),
+        both[:, 2 * separator : 2 * separator + half_rows].reshape(separator, width),
+        both[:, separator : 2 * separator].reshape(2 * separator, width),
+        both[:, 2 * separator + half_rows :].reshape(separator, width),
+    )
+    lows = got[:, 40:44].reshape(2, 8, 4, width).sum(axis=1)
+    upper_rows = lows[0, 2:] + lows[1, 2:]
     pieces = jnp.stack(
         [
             jnp.concatenate(
-                [root_row, near[1 + to_d : 2 + to_d], near[3 + to_d : 4 + to_d], root_row], axis=0
+                [lows[0, :1], upper_rows[to_d : to_d + 1], lows[1, to_d : to_d + 1], nothing],
+                axis=0,
             )
             for to_d in range(2)
         ]
@@ -286,7 +311,7 @@
     )
     total = exchange(pieces, ("c",)).sum(axis=0)
     tops = total[:48].reshape(2, 24, width)
-    tops = select(tops, d) + lax.ppermute(select(tops, 1 - d), "d", [(0, 1), (1, 0)])
+    tops = select(tops, d) + partner(select(tops, 1 - d), "d")
     leaf_back_coeffs = masked(total[96:], leaf_rank)
     leaf_back = leaf_forward - product(leaf_basis[0, 0], leaf_back_coeffs)
     leaf_solution = product_back(leaf_inverse[0, 0], leaf_back)

time: 249 us -> 232 us (0.932)
  blocking collectives: 15.9 us -> 0 us
  waiting for transfers between devices: 83 us -> 78.8 us
  starting transfers between devices: 71.9 us -> 74.4 us
    all_to_all x2 -> x0, blocking collectives: 15.9 us -> none  [exchange(): return lax.all_to_all(pieces, axes, 0, 0)]
    ppermute x1 -> x4, starting transfers between devices: 2.78 us -> 13.9 us  [partner(): return lax.ppermute(values, axis, [(0, 1), (1, 0)])]
    all_to_all x10 -> x8, starting transfers between devices: 69.2 us -> 60.5 us  [exchange(): return lax.all_to_all(pieces, axes, 0, 0)]
    all_to_all x10 -> x8, waiting for transfers between devices: 82.3 us -> 76.5 us  [exchange(): return lax.all_to_all(pieces, axes, 0, 0)]
    concatenate x12 -> x7, local copies, waits for them, and re-layouts: 7.85 us -> 2.19 us  [combine(): jnp.concatenate([real[..., :half] - imag[..., half:], real[..., half:] +...]
    another operation x2, local copies, waits for them, and re-layouts: 0.61 us -> 3.14 us  [body(): jnp.stack([leaf_maps[..., :rank], leaf_maps[..., rank:]], axis=1)]
    unnamed x177 -> x98, local copies, waits for them, and re-layouts: 6.5 us -> 6.03 us
    dot_general x12 -> x11, matrix products: 9.05 us -> 9.22 us  [product(): jnp.einsum('...zmk,...kc->...zmc', matrix, vector, precision=precise)]
  transfers between devices with their start and end apart: 11 -> 12, of which waited for: 10 -> 8; matrix products, arithmetic and copies ran while one was open for 10% -> 20% of each run, Pallas kernels for 0% -> 0%
where the time goes in v2:
time: 232 us; the launch traced here: 231 us
  waiting for transfers between devices  78.8 us (34%)
  starting transfers between devices  74.4 us (32%)
  local copies, waits for them, and re-layouts  34.2 us (15%)
  matrix products  22.4 us (10%)
  other arithmetic  17.7 us (8%)
  between operations  3.21 us (1%)
    all_to_all x8, waiting for transfers between devices, exchange(): return lax.all_to_all(pieces, axes, 0, 0)  76.5 us
    all_to_all x8, starting transfers between devices, exchange(): return lax.all_to_all(pieces, axes, 0, 0)  60.5 us
    ppermute x4, starting transfers between devices, partner(): return lax.ppermute(values, axis, [(0, 1), (1, 0)])  13.9 us
    dot_general x11, matrix products, product(): jnp.einsum('...zmk,...kc->...zmc', matrix, vector, precision=precise)  9.22 us
    unnamed x98, local copies, waits for them, and re-layouts  6.03 us
    sub x31, other arithmetic, combine(): real[..., :half] - imag[..., half:]  5.87 us
  transfers between devices with their start and end apart: 12, of which 8 were waited for; matrix products, arithmetic and copies ran while one was open for 20% of the time, Pallas kernels for 0%

profile of v2, /device:TPU:1, one launch (start us, length us, event | category | flops | bytes accessed | tf_op | source)
XLA Modules:
  0.0 230.8 jit_solution(18148487958901835080)
XLA Ops:
  4.3 1.2 fusion.1
  8.8 6.0 %all-to-all-start = ((f32[8,128,128]{2,1,0:T(8,128)}), f32[8,128,128]{2,1,0:T(8,128)S(1)}, u32[]{:S(2)}, u32[]{:S(2)}) async-start(f32[8,128,128]{2,1,0:T(8,128)} %broadcast_in_dim.135), calls=%async_computation | async-start | bytes 1048576 | tf_op jit(solution)/shard_map/all_to_all | solution.py:15
  19.0 1.5 copy.223
  20.5 1.5 copy.224
  23.5 1.9 concatenate.248
  25.4 1.8 convolution_bitcast_fusion
  33.1 6.6 %collective-permute-start.1 = (f32[16,64,128]{2,1,0:T(8,128)}, f32[16,64,128]{2,1,0:T(8,128)}, u32[]{:S(2)}, u32[]{:S(2)}) collective-permute-start(f32[16,64,128]{2,1,0:T(8,128)} %dynamic-slice_bitcast_fusion), channel_id=1, source_target_pairs={{0,16},{16,0},{1,17},{17,1},{2,18},{18,2},{3,19},{19,3},{4,20},{20... | collective-permute-start | bytes 1572872 | tf_op jit(solution)/shard_map/ppermute | solution.py:23
  39.8 1.2 fusion.25
  41.0 1.4 fusion.10
  45.3 1.1 maximum_bitcast_fusion
  46.5 2.1 copy.209
  49.6 3.7 %fusion.9 = f32[8,2,192,128]{3,2,1,0:T(8,128)S(1)} fusion(f32[8,1,192,32]{2,3,1,0:T(8,128)} %copy.210, f32[8,1,192,32]{2,3,1,0:T(8,128)} %copy.209, f32[8,128,128]{2,1,0:T(8,128)S(1)} %all-to-all-done), kind=kOutput, calls=%fused_computation.36 | convolution fusion | flops 151093248 | bytes 2097152 | tf_op jit(solution)/shard_map/...zmk,...kc->...zmc/dot_general | solution.py:39
  58.0 5.9 %all-to-all-start.1 = ((f32[32,5,128]{2,1,0:T(8,128)}), f32[32,5,128]{2,1,0:T(8,128)S(1)}, u32[]{:S(2)}, u32[]{:S(2)}) async-start(f32[32,5,128]{2,1,0:T(8,128)} %copy.221), calls=%async_computation.1 | async-start | bytes 262144 | tf_op jit(solution)/shard_map/all_to_all | solution.py:15
  64.0 2.1 collective-permute-start
  66.1 1.1 bitcast_add_fusion
  67.3 4.2 %all-to-all-done.1 = f32[32,5,128]{2,1,0:T(8,128)S(1)} async-done(((f32[32,5,128]{2,1,0:T(8,128)}), f32[32,5,128]{2,1,0:T(8,128)S(1)}, u32[]{:S(2)}, u32[]{:S(2)}) %all-to-all-start.1) | async-done | bytes 81952 | tf_op jit(solution)/shard_map/all_to_all | solution.py:15
  72.5 12.9 %all-to-all-start.2 = ((f32[16,80,128]{2,1,0:T(8,128)}), f32[16,80,128]{2,1,0:T(8,128)S(1)}, u32[]{:S(2)}, u32[]{:S(2)}) async-start(f32[16,80,128]{2,1,0:T(8,128)} %pad_maximum_fusion.2), calls=%async_computation.2 | async-start | bytes 1310720 | tf_op jit(solution)/shard_map/all_to_all | solution.py:15
  86.0 28.2 %all-to-all-done.2 = f32[16,80,128]{2,1,0:T(8,128)S(1)} async-done(((f32[16,80,128]{2,1,0:T(8,128)}), f32[16,80,128]{2,1,0:T(8,128)S(1)}, u32[]{:S(2)}, u32[]{:S(2)}) %all-to-all-start.2) | async-done | bytes 655392 | tf_op jit(solution)/shard_map/all_to_all | solution.py:15
  115.1 9.5 %all-to-all-start.3 = ((f32[32,24,128]{2,1,0:T(8,128)}), f32[32,24,128]{2,1,0:T(8,128)S(1)}, u32[]{:S(2)}, u32[]{:S(2)}) async-start(f32[32,24,128]{2,1,0:T(8,128)} %broadcast_in_dim.139), calls=%async_computation.3 | async-start | bytes 786432 | tf_op jit(solution)/shard_map/all_to_all | solution.py:15
  124.8 9.4 %all-to-all-done.3 = f32[32,24,128]{2,1,0:T(8,128)S(1)} async-done(((f32[32,24,128]{2,1,0:T(8,128)}), f32[32,24,128]{2,1,0:T(8,128)S(1)}, u32[]{:S(2)}, u32[]{:S(2)}) %all-to-all-start.3) | async-done | bytes 393248 | tf_op jit(solution)/shard_map/all_to_all | solution.py:15
  138.3 5.0 %all-to-all-start.4 = ((f32[32,8,128]{2,1,0:T(8,128)}), f32[32,8,128]{2,1,0:T(8,128)S(1)}, u32[]{:S(2)}, u32[]{:S(2)}) async-start(f32[32,8,128]{2,1,0:T(8,128)} %maximum_bitcast_fusion.6), calls=%async_computation.4 | async-start | bytes 262144 | tf_op jit(solution)/shard_map/all_to_all | solution.py:15
  143.3 7.5 %all-to-all-done.4 = f32[32,8,128]{2,1,0:T(8,128)S(1)} async-done(((f32[32,8,128]{2,1,0:T(8,128)}), f32[32,8,128]{2,1,0:T(8,128)S(1)}, u32[]{:S(2)}, u32[]{:S(2)}) %all-to-all-start.4) | async-done | bytes 131104 | tf_op jit(solution)/shard_map/all_to_all | solution.py:15
  151.9 7.0 %all-to-all-start.5 = ((f32[16,48,128]{2,1,0:T(8,128)}), f32[16,48,128]{2,1,0:T(8,128)S(1)}, u32[]{:S(2)}, u32[]{:S(2)}) async-start(f32[16,48,128]{2,1,0:T(8,128)} %bitcast.190), calls=%async_computation.5 | async-start | bytes 786432 | tf_op jit(solution)/shard_map/all_to_all | solution.py:15
  163.4 13.1 %all-to-all-done.5 = f32[16,48,128]{2,1,0:T(8,128)S(1)} async-done(((f32[16,48,128]{2,1,0:T(8,128)}), f32[16,48,128]{2,1,0:T(8,128)S(1)}, u32[]{:S(2)}, u32[]{:S(2)}) %all-to-all-start.5) | async-done | bytes 393248 | tf_op jit(solution)/shard_map/all_to_all | solution.py:15
  177.3 10.9 %all-to-all-start.6 = ((f32[32,4,128]{2,1,0:T(4,128)}), f32[32,4,128]{2,1,0:T(4,128)S(1)}, u32[]{:S(2)}, u32[]{:S(2)}) async-start(f32[32,4,128]{2,1,0:T(4,128)} %bitcast.216), calls=%async_computation.6 | async-start | bytes 131072 | tf_op jit(solution)/shard_map/all_to_all | solution.py:15
  188.9 2.4 %collective-permute-start.2 = (f32[576,128]{1,0:T(8,128)}, f32[576,128]{1,0:T(8,128)}, u32[]{:S(2)}, u32[]{:S(2)}) collective-permute-start(f32[576,128]{1,0:T(8,128)} %pad_maximum_fusion.9), channel_id=1, source_target_pairs={{0,16},{16,0},{1,17},{17,1},{2,18},{18,2},{3,19},{19,3},{4,20},{20... | collective-permute-start | bytes 884744 | tf_op jit(solution)/shard_map/ppermute | solution.py:23
  191.3 3.9 %all-to-all-done.6 = f32[32,4,128]{2,1,0:T(4,128)S(1)} async-done(((f32[32,4,128]{2,1,0:T(4,128)}), f32[32,4,128]{2,1,0:T(4,128)S(1)}, u32[]{:S(2)}, u32[]{:S(2)}) %all-to-all-start.6) | async-done | bytes 65568 | tf_op jit(solution)/shard_map/all_to_all | solution.py:15
  197.1 1.4 fusion.62
  207.6 3.5 %all-to-all-start.7 = ((f32[8,128,128]{2,1,0:T(8,128)}), f32[8,128,128]{2,1,0:T(8,128)S(1)}, u32[]{:S(2)}, u32[]{:S(2)}) async-start(f32[8,128,128]{2,1,0:T(8,128)} %copy.265), calls=%async_computation.7 | async-start | bytes 1048576 | tf_op jit(solution)/shard_map/all_to_all | solution.py:15
  211.2 10.2 %all-to-all-done.7 = f32[8,128,128]{2,1,0:T(8,128)S(1)} async-done(((f32[8,128,128]{2,1,0:T(8,128)}), f32[8,128,128]{2,1,0:T(8,128)S(1)}, u32[]{:S(2)}, u32[]{:S(2)}) %all-to-all-start.7) | async-done | bytes 524320 | tf_op jit(solution)/shard_map/all_to_all | solution.py:15
  223.6 2.8 %collective-permute-start.3 = (f32[24,128]{1,0:T(8,128)S(1)}, f32[24,128]{1,0:T(8,128)S(1)}, u32[]{:S(2)}, u32[]{:S(2)}) collective-permute-start(f32[24,128]{1,0:T(8,128)S(1)} %dynamic-slice_bitcast_fusion.3), channel_id=1, source_target_pairs={{0,8},{8,0},{1,9},{9,1},{2,10},{10,2},{3,11},{11,3},{4,12},{12,4},... | collective-permute-start | bytes 36872 | tf_op jit(solution)/shard_map/ppermute | solution.py:23
  227.3 2.3 collective-permute-done.3
  (360 shorter events, 54.4 us)
Async XLA Ops:
  0.6 3.6 %copy-start = (f32[1,1,2,384,384]{4,3,2,1,0:T(8,128)S(1)}, f32[1,1,2,384,384]{4,3,2,1,0:T(8,128)}, u32[]{:S(2)}) copy-start(f32[1,1,2,384,384]{4,3,2,1,0:T(8,128)} %param.28) | copy-start | bytes 3538948
  0.7 2.7 %copy-start.43 = (s32[1,1,2,96]{3,2,1,0:T(2,128)S(1)}, s32[1,1,2,96]{3,2,1,0:T(2,128)}, u32[]{:S(2)}) copy-start(s32[1,1,2,96]{3,2,1,0:T(2,128)} %param.38) | copy-start | bytes 2308
  0.7 2.7 %copy-start.42 = (s32[1,1,2,96]{3,2,1,0:T(2,128)S(1)}, s32[1,1,2,96]{3,2,1,0:T(2,128)}, u32[]{:S(2)}) copy-start(s32[1,1,2,96]{3,2,1,0:T(2,128)} %param.39) | copy-start | bytes 2308
  0.7 2.7 %copy-start.46 = (s32[1,1,96]{2,1,0:T(1,128)S(1)}, s32[1,1,96]{2,1,0:T(1,128)}, u32[]{:S(2)}) copy-start(s32[1,1,96]{2,1,0:T(1,128)} %param.41) | copy-start | bytes 1156
  0.7 3.6 %copy-start.28 = (f32[1,1,384,128]{3,2,1,0:T(8,128)S(1)}, f32[1,1,384,128]{3,2,1,0:T(8,128)}, u32[]{:S(2)}) copy-start(f32[1,1,384,128]{3,2,1,0:T(8,128)} %param.33) | copy-start | bytes 589828
  8.8 7.1 %copy-start.30 = (f32[1,1,192,128]{3,2,1,0:T(8,128)S(1)}, f32[1,1,192,128]{3,2,1,0:T(8,128)}, u32[]{:S(2)}) copy-start(f32[1,1,192,128]{3,2,1,0:T(8,128)} %param.30) | copy-start | bytes 294916
  8.8 36.3 %all-to-all-start = ((f32[8,128,128]{2,1,0:T(8,128)}), f32[8,128,128]{2,1,0:T(8,128)S(1)}, u32[]{:S(2)}, u32[]{:S(2)}) async-start(f32[8,128,128]{2,1,0:T(8,128)} %broadcast_in_dim.135), calls=%async_computation | async-start | bytes 1048576 | tf_op jit(solution)/shard_map/all_to_all | solution.py:15
  18.9 6.5 %copy-start.1 = (f32[1,1,2,384,192]{3,4,2,1,0:T(8,128)S(1)}, f32[1,1,2,384,192]{3,4,2,1,0:T(8,128)}, u32[]{:S(2)}) copy-start(f32[1,1,2,384,192]{3,4,2,1,0:T(8,128)} %param.24) | copy-start | bytes 1769476
  32.3 8.7 %copy-start.21 = (f32[384,64]{0,1:T(8,128)S(1)}, f32[384,64]{0,1:T(8,128)}, u32[]{:S(2)}) copy-start(f32[384,64]{0,1:T(8,128)} %copy-done.20) | copy-start | bytes 294916
  32.3 8.7 %copy-start.23 = (f32[384,64]{0,1:T(8,128)S(1)}, f32[384,64]{0,1:T(8,128)}, u32[]{:S(2)}) copy-start(f32[384,64]{0,1:T(8,128)} %copy-done.22) | copy-start | bytes 294916
  32.3 8.7 %copy-start.25 = (f32[384,64]{0,1:T(8,128)S(1)}, f32[384,64]{0,1:T(8,128)}, u32[]{:S(2)}) copy-start(f32[384,64]{0,1:T(8,128)} %copy-done.24) | copy-start | bytes 294916
  32.3 8.7 %copy-start.27 = (f32[384,64]{0,1:T(8,128)S(1)}, f32[384,64]{0,1:T(8,128)}, u32[]{:S(2)}) copy-start(f32[384,64]{0,1:T(8,128)} %copy-done.26) | copy-start | bytes 294916
  33.1 33.0 %collective-permute-start.1 = (f32[16,64,128]{2,1,0:T(8,128)}, f32[16,64,128]{2,1,0:T(8,128)}, u32[]{:S(2)}, u32[]{:S(2)}) collective-permute-start(f32[16,64,128]{2,1,0:T(8,128)} %dynamic-slice_bitcast_fusion), channel_id=1, source_target_pairs={{0,16},{16,0},{1,17},{17,1},{2,18},{18,2},{3,19},{19,3},{4,20},{20... | collective-permute-start | bytes 1572872 | tf_op jit(solution)/shard_map/ppermute | solution.py:23
  58.0 13.4 %all-to-all-start.1 = ((f32[32,5,128]{2,1,0:T(8,128)}), f32[32,5,128]{2,1,0:T(8,128)S(1)}, u32[]{:S(2)}, u32[]{:S(2)}) async-start(f32[32,5,128]{2,1,0:T(8,128)} %copy.221), calls=%async_computation.1 | async-start | bytes 262144 | tf_op jit(solution)/shard_map/all_to_all | solution.py:15
  64.0 3.3 %collective-permute-start = (f32[16,8,128]{2,1,0:T(8,128)S(1)}, f32[16,8,128]{2,1,0:T(8,128)S(1)}, u32[]{:S(2)}, u32[]{:S(2)}) collective-permute-start(f32[16,8,128]{2,1,0:T(8,128)S(1)} %dynamic-slice_bitcast_fusion.2), channel_id=1, source_target_pairs={{0,16},{16,0},{1,17},{17,1},{2,18},{18,2},{3,19},{19,3},{4,20},{20... | collective-permute-start | bytes 196616 | tf_op jit(solution)/shard_map/ppermute | solution.py:23
  71.6 13.8 %copy-start.47 = (s32[14]{0:T(128)S(1)}, s32[14]{0:T(128)}, u32[]{:S(2)}) copy-start(s32[14]{0:T(128)} %param.46) | copy-start | bytes 172
  72.5 41.8 %all-to-all-start.2 = ((f32[16,80,128]{2,1,0:T(8,128)}), f32[16,80,128]{2,1,0:T(8,128)S(1)}, u32[]{:S(2)}, u32[]{:S(2)}) async-start(f32[16,80,128]{2,1,0:T(8,128)} %pad_maximum_fusion.2), calls=%async_computation.2 | async-start | bytes 1310720 | tf_op jit(solution)/shard_map/all_to_all | solution.py:15
  115.1 19.1 %all-to-all-start.3 = ((f32[32,24,128]{2,1,0:T(8,128)}), f32[32,24,128]{2,1,0:T(8,128)S(1)}, u32[]{:S(2)}, u32[]{:S(2)}) async-start(f32[32,24,128]{2,1,0:T(8,128)} %broadcast_in_dim.139), calls=%async_computation.3 | async-start | bytes 786432 | tf_op jit(solution)/shard_map/all_to_all | solution.py:15
  136.4 14.4 %copy-start.44 = (pred[2]{0:T(512)(128)(4,1)S(1)}, pred[2]{0:T(512)(128)(4,1)}, u32[]{:S(2)}) copy-start(pred[2]{0:T(512)(128)(4,1)} %constant.196.clone.1) | copy-start | bytes 10
  138.3 22.3 %copy-start.8 = (f32[1,1,2,192,192]{4,3,2,1,0:T(8,128)S(1)}, f32[1,1,2,192,192]{4,3,2,1,0:T(8,128)}, u32[]{:S(2)}) copy-start(f32[1,1,2,192,192]{4,3,2,1,0:T(8,128)} %param.25) | copy-start | bytes 884740
  138.3 12.5 %all-to-all-start.4 = ((f32[32,8,128]{2,1,0:T(8,128)}), f32[32,8,128]{2,1,0:T(8,128)S(1)}, u32[]{:S(2)}, u32[]{:S(2)}) async-start(f32[32,8,128]{2,1,0:T(8,128)} %maximum_bitcast_fusion.6), calls=%async_computation.4 | async-start | bytes 262144 | tf_op jit(solution)/shard_map/all_to_all | solution.py:15
  151.9 24.7 %all-to-all-start.5 = ((f32[16,48,128]{2,1,0:T(8,128)}), f32[16,48,128]{2,1,0:T(8,128)S(1)}, u32[]{:S(2)}, u32[]{:S(2)}) async-start(f32[16,48,128]{2,1,0:T(8,128)} %bitcast.190), calls=%async_computation.5 | async-start | bytes 786432 | tf_op jit(solution)/shard_map/all_to_all | solution.py:15
  161.0 34.3 %copy-start.29 = (f32[1,2,2,192,32]{3,4,2,1,0:T(8,128)S(1)}, f32[1,2,2,192,32]{3,4,2,1,0:T(8,128)}, u32[]{:S(2)}) copy-start(f32[1,2,2,192,32]{3,4,2,1,0:T(8,128)} %param.42) | copy-start | bytes 294916
  163.3 32.9 %copy-start.38 = (f32[1,2,2,384,32]{3,4,2,1,0:T(8,128)S(1)}, f32[1,2,2,384,32]{3,4,2,1,0:T(8,128)}, u32[]{:S(2)}) copy-start(f32[1,2,2,384,32]{3,4,2,1,0:T(8,128)} %param.43) | copy-start | bytes 589828
  177.3 17.9 %all-to-all-start.6 = ((f32[32,4,128]{2,1,0:T(4,128)}), f32[32,4,128]{2,1,0:T(4,128)S(1)}, u32[]{:S(2)}, u32[]{:S(2)}) async-start(f32[32,4,128]{2,1,0:T(4,128)} %bitcast.216), calls=%async_computation.6 | async-start | bytes 131072 | tf_op jit(solution)/shard_map/all_to_all | solution.py:15
  188.9 10.8 %collective-permute-start.2 = (f32[576,128]{1,0:T(8,128)}, f32[576,128]{1,0:T(8,128)}, u32[]{:S(2)}, u32[]{:S(2)}) collective-permute-start(f32[576,128]{1,0:T(8,128)} %pad_maximum_fusion.9), channel_id=1, source_target_pairs={{0,16},{16,0},{1,17},{17,1},{2,18},{18,2},{3,19},{19,3},{4,20},{20... | collective-permute-start | bytes 884744 | tf_op jit(solution)/shard_map/ppermute | solution.py:23
  206.7 14.6 %copy-start.19 = (f32[1,1,2,384,32]{3,4,2,1,0:T(8,128)S(1)}, f32[1,1,2,384,32]{3,4,2,1,0:T(8,128)}, u32[]{:S(2)}) copy-start(f32[1,1,2,384,32]{3,4,2,1,0:T(8,128)} %param.45) | copy-start | bytes 294916
  206.7 14.6 %copy-start.41 = (pred[32]{0:T(512)(128)(4,1)S(1)}, pred[32]{0:T(512)(128)(4,1)}, u32[]{:S(2)}) copy-start(pred[32]{0:T(512)(128)(4,1)} %copy-done.40) | copy-start | bytes 100
  207.6 13.7 %all-to-all-start.7 = ((f32[8,128,128]{2,1,0:T(8,128)}), f32[8,128,128]{2,1,0:T(8,128)S(1)}, u32[]{:S(2)}, u32[]{:S(2)}) async-start(f32[8,128,128]{2,1,0:T(8,128)} %copy.265), calls=%async_computation.7 | async-start | bytes 1048576 | tf_op jit(solution)/shard_map/all_to_all | solution.py:15
  211.1 11.5 %copy-start.11 = (f32[384,64]{0,1:T(8,128)S(1)}, f32[384,64]{0,1:T(8,128)}, u32[]{:S(2)}) copy-start(f32[384,64]{0,1:T(8,128)} %copy-done.10) | copy-start | bytes 294916
  211.1 11.5 %copy-start.13 = (f32[384,64]{0,1:T(8,128)S(1)}, f32[384,64]{0,1:T(8,128)}, u32[]{:S(2)}) copy-start(f32[384,64]{0,1:T(8,128)} %copy-done.12) | copy-start | bytes 294916
  223.6 5.9 %collective-permute-start.3 = (f32[24,128]{1,0:T(8,128)S(1)}, f32[24,128]{1,0:T(8,128)S(1)}, u32[]{:S(2)}, u32[]{:S(2)}) collective-permute-start(f32[24,128]{1,0:T(8,128)S(1)} %dynamic-slice_bitcast_fusion.3), channel_id=1, source_target_pairs={{0,8},{8,0},{1,9},{9,1},{2,10},{10,2},{3,11},{11,3},{4,12},{12,4},... | collective-permute-start | bytes 36872 | tf_op jit(solution)/shard_map/ppermute | solution.py:23
  (28 other events, 37.5 us)

commit v3 on v2

v3 whole, which is shorter than its diff:
```python
import jax
import jax.numpy as jnp
from jax import lax
from jax.experimental import pallas as pl
from jax.experimental.pallas import tpu as pltpu
from jax.sharding import Mesh, PartitionSpec as P

precise = lax.Precision.HIGHEST

ROW = ("a", "e", "z", "k")
COL = ("d", "c")
CHIPS = ("a", "e", "z")
PLANE = ("k", "d", "c")


def exchange(pieces, axes):
    return lax.all_to_all(pieces, axes, 0, 0)


def share(values, axes, count):
    return exchange(jnp.broadcast_to(values[None], (count,) + values.shape), axes)


def partner(values, axis):
    return lax.ppermute(values, axis, [(0, 1), (1, 0)])


def combine(stacked):
    half = stacked.shape[-1] // 2
    real, imag = stacked[..., 0, :, :], stacked[..., 1, :, :]
    return jnp.concatenate(
        [real[..., :half] - imag[..., half:], real[..., half:] + imag[..., :half]], axis=-1
    )


def product(matrix, vector):
    return combine(jnp.einsum("...zmk,...kc->...zmc", matrix, vector, precision=precise))


def product_back(matrix, vector):
    return combine(jnp.einsum("...zkm,...kc->...zmc", matrix, vector, precision=precise))


def turned(values):
    groups = []
    for at in range(0, values.shape[-1], 128):
        groups += [-values[:, at + 64 : at + 128], values[:, at : at + 64]]
    return jnp.concatenate(groups, axis=-1)


def dot(left, right, contract=1):
    return lax.dot_general(
        left,
        right,
        (((contract,), (0,)), ((), ())),
        precision=precise,
        preferred_element_type=jnp.float32,
    )


def times(real, imag, vector):
    return dot(real, vector) + dot(imag, turned(vector))


def times_back(real, imag, vector):
    return dot(real, vector, 0) + dot(imag, turned(vector), 0)


def cut(values, limit):
    rows = lax.broadcasted_iota(jnp.int32, values.shape, 0)
    return jnp.where(rows < limit, values, jnp.zeros_like(values))


def leaf_kernel(ranks, inverse, source, basis, update, slots, forward, packs):
    inner = inverse.shape[-1]
    result = times(inverse[0, 0, 0], inverse[0, 0, 1], source[0, 0])
    forward[...] = result
    low = cut(times_back(basis[0, 0, 0], basis[0, 0, 1], result), ranks[0, 0])
    height = inner // 2
    places = lax.broadcasted_iota(jnp.int32, (height, slots.shape[-1]), 0)
    onehot = (places == slots[0]).astype(jnp.float32)
    flat = jnp.concatenate([update[0, 0, 0], update[0, 0, 1]], axis=-1)
    spread_out = lax.dot_general(
        flat,
        onehot,
        (((0,), (1,)), ((), ())),
        precision=precise,
        preferred_element_type=jnp.float32,
    )
    half = low.shape[0]
    pack = jnp.concatenate(
        [
            low,
            spread_out[:, :128],
            jnp.concatenate([spread_out[:half, 128:], spread_out[half:, 128:]], axis=-1),
        ],
        axis=0,
    )
    for place in range(packs.shape[0]):
        packs[place] = pack


def apply_kernel(
    spots,
    inverse0,
    inverse1,
    inverse2,
    source0,
    source1,
    source2,
    update0,
    update1,
    update2,
    slots0,
    slots1,
    slots2,
    basis1,
    basis2,
    keep,
    send,
    lows,
):
    a, k, d = spots[0], spots[2], spots[3]
    results = []
    for inverse, source, update, slots, at in (
        (inverse0, source0, update0, slots0, 0),
        (inverse1, source1, update1, slots1, 0),
        (inverse2, source2, update2, slots2, d),
    ):
        right = source[0, at]
        height = right.shape[0]
        lists = slots[0, at]
        places = lax.broadcasted_iota(jnp.int32, (height, lists.shape[-1]), 0)
        spread_out = []
        for child in range(2):
            onehot = (places == lists[child : child + 1]).astype(jnp.float32)
            flat = jnp.concatenate([update[0, at, child, 0], update[0, at, child, 1]], axis=-1)
            spread_out.append(dot(onehot, flat))
        rank = spread_out[0].shape[-1] // 2
        both = jnp.concatenate(
            [
                right,
                spread_out[0][:, :rank],
                spread_out[1][:, :rank],
                spread_out[0][:, rank:],
                spread_out[1][:, rank:],
            ],
            axis=-1,
        )
        results.append(times(inverse[0, 0, 0], inverse[0, 0, 1], both))
    low2 = times_back(basis2[0, a, 0], basis2[0, a, 1], results[2])
    low1 = times_back(basis1[0, a, 0], basis1[0, a, 1], results[1])
    lows[0] = low2[:, :128]
    lows[1] = low2[:, 128:]
    lows[2] = low1[:, :128]
    lows[3] = low1[:, 128:]

    def put(target, half):
        for side in range(2):
            for level, at in ((0, 0), (2, 8)):
                rows = results[level].shape[0] // 2
                part = results[level][half * rows : (half + 1) * rows, side * 128 : side * 128 + 128]
                target[at : at + 8, 24 * side : 24 * side + 24] = part.reshape(8, 24, 128)
            rows = results[1].shape[0] // 2
            part = results[1][half * rows : (half + 1) * rows, side * 128 : side * 128 + 128]
            row = 48 + 8 * side
            target[0:12, row : row + 8] = part.reshape(12, 8, 128)
            target[12:16, row : row + 8] = jnp.zeros((4, 8, 128), jnp.float32)

    for half in range(2):

        @pl.when(k == half)
        def _(half=half):
            put(keep, half)
            put(send, 1 - half)


def lower_kernel(spots, shared, inverse, source, basis, lows, keep, send, rows):
    a, e, k, d = spots[0], spots[1], spots[2], spots[3]
    low = shared[:, 0:32].reshape(256, 128)
    low_turned = turned(low)
    packs = shared[:, 96:128].reshape(256, 128)
    top = dot(shared[:, 32:64].reshape(256, 128), low, 0) + dot(
        shared[:, 64:96].reshape(256, 128), low_turned, 0
    )
    rest = dot(packs[:, :64], low, 0) + dot(packs[:, 64:], low_turned, 0)
    side = source[0, d] - jnp.concatenate([top, rest], axis=0)
    partial = times(inverse[0, 0, 0], inverse[0, 0, 1], side)
    front = 2 * a + e
    low3 = times_back(basis[0, front, 0], basis[0, front, 1], partial)
    rows[:, 0, :] = low3
    for at in range(4):
        rows[:, at + 1, :] = lows[at]
    for at in range(5, 8):
        rows[:, at, :] = jnp.zeros((32, 128), jnp.float32)
    count = partial.shape[0] // 2

    def put(target, half):
        target[0:12] = partial[half * count : (half + 1) * count].reshape(12, 8, 128)
        target[12:16] = jnp.zeros((4, 8, 128), jnp.float32)

    for half in range(2):

        @pl.when(k == half)
        def _(half=half):
            put(keep, half)
            put(send, 1 - half)


def backward_kernel(
    spots,
    ranks,
    gains,
    lows,
    mine,
    theirs,
    inverse0,
    inverse1,
    inverse2,
    inverse3,
    basis1,
    basis2,
    basis3,
    shared,
    pieces,
):
    a, e, k, d = spots[0], spots[1], spots[2], spots[3]

    def gain_back(gain, low, child):
        both = times_back(gain[:, :64], gain[:, 64:], low)
        return jnp.where(child == 0, both[:32], both[32:])

    gain1 = jnp.where(a == 0, gains[:, 18, :], gains[:, 19, :])
    gain2 = jnp.where(
        a == 0,
        jnp.where(d == 0, gains[:, 12, :], gains[:, 13, :]),
        jnp.where(d == 0, gains[:, 14, :], gains[:, 15, :]),
    )
    back1 = cut(lows[:, 0, :], ranks[a])
    back2 = cut(lows[:, 1, :] - gain_back(gain1, back1, d), ranks[2 + 2 * a + d])
    back3 = cut(lows[:, 2, :] - gain_back(gain2, back2, e), ranks[6 + 4 * a + 2 * e + d])

    def whole(start, stop):
        left, right = mine[start:stop], theirs[start:stop]
        return jnp.concatenate(
            [jnp.where(k == 0, left, right), jnp.where(k == 0, right, left)], axis=0
        )

    front = 2 * a + e
    residuals = (
        whole(0, 192),
        whole(384, 480) - times(basis1[0, a, 0], basis1[0, a, 1], back1),
        whole(192, 384) - times(basis2[0, a, 0], basis2[0, a, 1], back2),
        whole(480, 576) - times(basis3[0, front, 0], basis3[0, front, 1], back3),
    )
    solved = [
        times_back(inverse[0, 0, 0], inverse[0, 0, 1], residuals[level])
        for level, inverse in enumerate((inverse0, inverse1, inverse2, inverse3))
    ]
    for level in range(2):
        for place in range(2):
            for to_c in range(8):
                at = 96 * place + 12 * to_c
                row = 24 * place + 12 * level
                pieces[to_c, row : row + 12] = solved[level][at : at + 12]
    pieces[:, 48:72] = solved[2].reshape(8, 24, 128)
    pieces[:, 72:96] = solved[3].reshape(8, 24, 128)
    lowest = solved[3]
    lowest_turned = turned(lowest)
    packs = shared[:, 96:128].reshape(256, 128)
    parts = (
        dot(shared[:, 32:64].reshape(256, 128), lowest[:128])
        + dot(shared[:, 64:96].reshape(256, 128), lowest_turned[:128])
        + dot(packs[:, :64], lowest[128:])
        + dot(packs[:, 64:], lowest_turned[128:])
    )
    pieces[:, 96:128] = parts.reshape(8, 32, 128)


def last_kernel(ranks, low, forward, inverse, basis, solved):
    back = cut(low[...], ranks[0, 0])
    rest = forward[...] - times(basis[0, 0, 0], basis[0, 0, 1], back)
    solved[0, 0] = times_back(inverse[0, 0, 0], inverse[0, 0, 1], rest)


def call(kernel, shapes, scalars, arrays, flops):
    return pl.pallas_call(
        kernel,
        out_shape=[jax.ShapeDtypeStruct(shape, jnp.float32) for shape in shapes],
        in_specs=[pl.BlockSpec(memory_space=pltpu.SMEM)] * len(scalars)
        + [pl.BlockSpec(memory_space=pltpu.VMEM)] * len(arrays),
        out_specs=[pl.BlockSpec(memory_space=pltpu.VMEM)] * len(shapes),
        compiler_params=pltpu.CompilerParams(vmem_limit_bytes=32 * 2**20),
        cost_estimate=pl.CostEstimate(flops=flops, bytes_accessed=4 * 2**20, transcendentals=0),
    )(*scalars, *arrays)


def as_matrix(values):
    half = values.shape[-1] // 2
    return jnp.stack([values[..., :half], values[..., half:]], axis=-3)


def masked(values, rank_limit):
    keep = jnp.arange(values.shape[-2])[:, None] < jnp.asarray(rank_limit)[..., None, None]
    return jnp.where(keep, values, jnp.zeros_like(values))


def select(array, position):
    return lax.dynamic_index_in_dim(array, position, 0, keepdims=False)


def body(
    inverse_root,
    inverse_upper,
    inverse_middle,
    inverse_lower,
    leaf_inverse,
    source_root,
    source_upper,
    source_middle,
    source_lower,
    leaf_source,
    update_root,
    update_upper,
    update_middle,
    leaf_update,
    slots_root,
    slots_upper,
    slots_middle,
    leaf_slots,
    basis_upper,
    basis_middle,
    basis_lower,
    leaf_basis,
    front_ranks,
    leaf_ranks,
):
    a, e, k, d = (lax.axis_index(name) for name in ("a", "e", "k", "d"))
    rank1 = front_ranks[0:2]
    rank2 = front_ranks[2:6].reshape(2, 2)
    rank3 = front_ranks[6:14].reshape(2, 2, 2)
    separator, width = source_root.shape[2:]
    rank = leaf_basis.shape[-1]
    spots = jnp.stack([a, e, k, d]).astype(jnp.int32)

    leaf_forward, packs = call(
        leaf_kernel,
        [leaf_source.shape[2:], (8, 128, width)],
        [leaf_ranks],
        [leaf_inverse, leaf_source, leaf_basis, leaf_update, leaf_slots],
        10**9,
    )
    shared = exchange(packs, ("c",))

    keep, send, lows = call(
        apply_kernel,
        [(16, 64, width), (16, 64, width), (4, rank, width)],
        [spots],
        [
            inverse_root,
            inverse_upper,
            inverse_middle,
            source_root,
            source_upper,
            source_middle,
            update_root,
            update_upper,
            update_middle,
            slots_root,
            slots_upper,
            slots_middle,
            basis_upper,
            basis_middle,
        ],
        4 * 10**9,
    )
    applied_pieces = keep + partner(send, "k")
    keep, send, rows = call(
        lower_kernel,
        [(16, 8, width), (16, 8, width), (rank, 8, width)],
        [spots],
        [shared, inverse_lower, source_lower, basis_lower, lows],
        10**9,
    )
    lower_pieces = keep + partner(send, "k")

    rows = exchange(rows, PLANE).reshape(2, 2, 8, 8, width).sum(axis=(0, 2))
    rows = jnp.concatenate(
        [rows[:, 0], rows[:, 1], rows[:, 2], (rows[0, 3:5] + rows[1, 3:5])], axis=0
    )
    pieces = jnp.concatenate(
        [jnp.broadcast_to(rows[None], (16, 8, width)), lower_pieces, applied_pieces], axis=1
    )
    slices = exchange(pieces, CHIPS).reshape(2, 2, 4, 80, width).sum(axis=2)
    sums = slices[:, :, 16:].sum(axis=1)
    got = slices[:, :, :16]
    lower_slices = got[:, :, 8:]
    merged = got.sum(axis=1)
    rows = jnp.concatenate(
        [
            got[:, :, 0:2].reshape(8, width),
            merged[:, 2:4].reshape(4, width),
            merged[:, 4:6].reshape(4, width),
            merged[:, 6],
            merged[:, 7],
            jnp.zeros((4, width), jnp.float32),
        ],
        axis=0,
    )
    gains = share(rows, PLANE, 32)
    blocks = jnp.transpose(gains, (1, 0, 2))
    coeffs3 = masked(blocks[0:8].reshape(2, 2, 2, rank, width), rank3)
    total2 = blocks[8:12].reshape(2, 2, rank, width)
    gain2 = as_matrix(blocks[12:16].reshape(2, 2, rank, width))
    total1 = blocks[16:18]
    gain1 = as_matrix(blocks[18:20])
    pairs3 = jnp.transpose(coeffs3, (0, 2, 1, 3, 4)).reshape(2, 2, 2 * rank, width)
    coeffs2 = masked(total2 - product(gain2, pairs3), rank2)
    pairs2 = coeffs2.reshape(2, 2 * rank, width)
    coeffs1 = masked(total1 - product(gain1, pairs2), rank1)
    pair1 = coeffs1.reshape(2 * rank, width)

    first = a == 0
    wide = jnp.where(first, jnp.broadcast_to(sums.sum(axis=0), sums.shape), sums)[:, :48]
    wide_below = jnp.where(
        first, pair1[None], lax.dynamic_index_in_dim(pairs3, d, 1, keepdims=False)
    )
    wide_map = as_matrix(wide[:, 24:])
    wide_forward = wide[:, :24] - product(wide_map, wide_below)
    upper_map = as_matrix(sums[:, 56:])
    upper_forward = sums[:, 48:56] - product(upper_map, pairs2)

    wide_low = product_back(wide_map, wide_forward).reshape(4, rank, width)
    upper_low = product_back(upper_map, upper_forward).reshape(4, rank, width)
    rows = jnp.transpose(jnp.concatenate([wide_low, upper_low], axis=0), (1, 0, 2))
    rows = exchange(rows, PLANE).reshape(2, 2, 8, 8, width).sum(axis=(0, 2))
    joined = rows[0] + rows[1]
    nothing = jnp.zeros((1, width), jnp.float32)
    tail = jnp.zeros((4, width), jnp.float32)
    pieces = jnp.stack(
        [
            jnp.stack(
                [
                    jnp.concatenate(
                        [
                            wide_forward[to_a],
                            upper_forward[to_a],
                            lower_slices[to_a, to_e],
                            jnp.where(
                                first,
                                jnp.concatenate([joined[to_a : to_a + 1], nothing], axis=0),
                                rows[:, 2 * to_a + to_e],
                            ),
                            joined[4 + 2 * to_a : 6 + 2 * to_a],
                            tail,
                        ],
                        axis=0,
                    )
                    for to_e in range(2)
                ]
            )
            for to_a in range(2)
        ]
    )
    pieces = jnp.broadcast_to(pieces[:, :, None], (2, 2, 4, 48, width)).reshape(16, 48, width)
    got = exchange(pieces, CHIPS)
    half_rows = separator // 2
    mine = jnp.concatenate(
        [
            got[:8, :24].reshape(separator, width),
            got[8:, :24].reshape(separator, width),
            got[:, 24:32].reshape(128, width)[:half_rows],
            got[:, 32:40].reshape(128, width)[:half_rows],
        ],
        axis=0,
    )
    theirs = partner(mine, "k")
    lows = got[:, 40:44].reshape(2, 8, 4, width).sum(axis=1)
    upper_rows = lows[0, 2:] + lows[1, 2:]
    pieces = jnp.stack(
        [
            jnp.concatenate(
                [lows[0, :1], upper_rows[to_d : to_d + 1], lows[1, to_d : to_d + 1], nothing],
                axis=0,
            )
            for to_d in range(2)
        ]
    )
    pieces = jnp.broadcast_to(pieces[None, :, None], (2, 2, 8, 4, width)).reshape(32, 4, width)
    low_rows = exchange(pieces, PLANE)

    (pieces,) = call(
        backward_kernel,
        [(8, 128, width)],
        [spots, front_ranks],
        [
            gains,
            low_rows,
            mine,
            theirs,
            inverse_root,
            inverse_upper,
            inverse_middle,
            inverse_lower,
            basis_upper,
            basis_middle,
            basis_lower,
            shared,
        ],
        3 * 10**9,
    )
    total = exchange(pieces, ("c",)).sum(axis=0)
    tops = total[:48].reshape(2, 24, width)
    tops = select(tops, d) + partner(select(tops, 1 - d), "d")
    (leaf_solution,) = call(
        last_kernel,
        [leaf_source.shape],
        [leaf_ranks],
        [total[96:], leaf_forward, leaf_inverse, leaf_basis],
        10**9,
    )
    return (
        tops[None, None, :12],
        tops[None, None, 12:],
        total[None, None, 48:72],
        total[None, None, 72:96],
        leaf_solution,
    )


def solution(mesh):
    fine = Mesh(mesh.devices.reshape(2, 2, 4, 2, 2, 8), ROW + COL)
    tile = (ROW, COL)
    in_specs = (
        [P(*tile, None, None, None)] * 5
        + [P(ROW, None, None, None)] * 4
        + [P(*tile, None, None)]
        + [P(ROW, None, None, None, None, None)] * 3
        + [P(*tile, None, None, None)]
        + [P(ROW, None, None, None)] * 3
        + [P(*tile, None)]
        + [P(COL, None, None, None, None)] * 3
        + [P(*tile, None, None, None), P(), P(*tile)]
    )
    return jax.shard_map(
        body,
        mesh=fine,
        in_specs=tuple(in_specs),
        out_specs=(P(*tile, None, None),) * 5,
        check_vma=False,
    )
```

time: 232 us -> 252 us (1.086)
  Pallas kernels: 0 us -> 21 us
  matrix products: 22.4 us -> 1.6 us
  local copies, waits for them, and re-layouts: 34.2 us -> 51.4 us
  blocking collectives: 0 us -> 10.5 us
  waiting for transfers between devices: 78.8 us -> 71.6 us
  starting transfers between devices: 74.4 us -> 71 us
    pallas_call x0 -> x5, Pallas kernels: none -> 21 us  [call(): pl.pallas_call(kernel, out_shape=[jax.ShapeDtypeStruct(shape, jnp.float32...]
    concatenate x4, local copies, waits for them, and re-layouts: 0.1 us -> 19.1 us  [body(): jnp.concatenate([wide_forward[to_a], upper_forward[to_a], lower_slices[to...]
    unnamed x98 -> x96, local copies, waits for them, and re-layouts: 6.03 us -> 20 us
    all_to_all x8 -> x7, starting transfers between devices: 60.5 us -> 50 us  [exchange(): return lax.all_to_all(pieces, axes, 0, 0)]
    all_to_all x0 -> x1, blocking collectives: none -> 10.5 us  [exchange(): return lax.all_to_all(pieces, axes, 0, 0)]
    dot_general x11 -> x4, matrix products: 9.22 us -> 0.81 us  [product(): jnp.einsum('...zmk,...kc->...zmc', matrix, vector, precision=precise)]
    ppermute x4, starting transfers between devices: 13.9 us -> 21.1 us  [partner(): return lax.ppermute(values, axis, [(0, 1), (1, 0)])]
    dot_general x6 -> x0, matrix products: 6.44 us -> none  [the longest x3 3.09 us: product_pair(): jnp.einsum('zmk,kc->zmc', matrix, jnp.concatenate([left, right], axis=-1)...]
  transfers between devices with their start and end apart: 12 -> 11, of which waited for: 8 -> 7; matrix products, arithmetic and copies ran while one was open for 20% -> 5% of each run, Pallas kernels for 0% -> 5%
where the time goes in v3:
time: 252 us; the launch traced here: 249 us
  waiting for transfers between devices  71.6 us (28%)
  starting transfers between devices  71 us (28%)
  local copies, waits for them, and re-layouts  51.4 us (20%)
  Pallas kernels  21 us (8%)
  other arithmetic  19.6 us (8%)
  blocking collectives  10.5 us (4%)
    all_to_all x7, waiting for transfers between devices, exchange(): return lax.all_to_all(pieces, axes, 0, 0)  71.4 us
    all_to_all x7, starting transfers between devices, exchange(): return lax.all_to_all(pieces, axes, 0, 0)  50 us
    ppermute x4, starting transfers between devices, partner(): return lax.ppermute(values, axis, [(0, 1), (1, 0)])  21.1 us
    pallas_call x5, Pallas kernels, call(): pl.pallas_call(kernel, out_shape=[jax.ShapeDtypeStruct(shape, jnp.float32...  21 us
    unnamed x96, local copies, waits for them, and re-layouts  20 us
    concatenate x4, local copies, waits for them, and re-layouts, body(): jnp.concatenate([wide_forward[to_a], upper_forward[to_a], lower_slices[to...  19.1 us
    all_to_all x1, blocking collectives, exchange(): return lax.all_to_all(pieces, axes, 0, 0)  10.5 us
  transfers between devices with their start and end apart: 11, of which 7 were waited for; matrix products, arithmetic and copies ran while one was open for 5% of the time, Pallas kernels for 5%

profile of v3, /device:TPU:1, one launch (start us, length us, event | category | flops | bytes accessed | tf_op | source)
XLA Modules:
  0.0 248.9 jit_solution(14326906526258140721)
XLA Ops:
  6.1 2.8 %shard_map.263 = (f32[384,128]{1,0:T(8,128)S(1)}, f32[8,128,128]{2,1,0:T(8,128)}) custom-call(s32[1,1]{1,0:T(1,128)S(6)} %copy.210.ranks, f32[1,1,2,384,384]{4,3,2,1,0:T(8,128)S(1)} %copy-done.7, f32[1,1,384,128]{3,2,1,0:T(8,128)S(1)} %copy-done.13, f32[1,1,2,384,32]{4,3,2,1,0:T(8,128)S(1)} %copy.137.basis, f32[1,1,2,96,32]{4,3,2,1,0:T(8,128)S(1)} %copy.138.update, ...), custom_call_target="tpu_custom_call" | custom-call | flops 1000000000 | bytes 4194304 | tf_op jit(solution)/shard_map/pallas_call | solution.py:287
  9.6 6.0 %all-to-all-start = ((f32[8,128,128]{2,1,0:T(8,128)}), f32[8,128,128]{2,1,0:T(8,128)}, u32[]{:S(2)}, u32[]{:S(2)}) async-start(f32[8,128,128]{2,1,0:T(8,128)} %get-tuple-element.13), calls=%async_computation | async-start | bytes 1048576 | tf_op jit(solution)/shard_map/all_to_all | solution.py:17
  22.2 6.3 %shard_map.264 = (f32[16,64,128]{2,1,0:T(8,128)S(1)}, f32[16,64,128]{2,1,0:T(8,128)}, f32[4,32,128]{2,1,0:T(8,128)S(1)}) custom-call(s32[4]{0:T(128)S(1)} %pad_add_fusion.spots, f32[1,1,2,384,192]{4,3,2,1,0:T(8,128)S(1)} %copy.139.inverse0, f32[1,1,2,192,192]{4,3,2,1,0:T(8,128)S(1)} %copy-done.9, f32[1,1,2,384,192]{4,3,2,1,0:T(8,128)S(1)} %copy.140.inverse2, ...), custom_call_target="tpu_custom_call" | custom-call | flops 4000000000 | bytes 4194304 | tf_op jit(solution)/shard_map/pallas_call | solution.py:287
  29.9 7.0 %collective-permute-start.1 = (f32[16,64,128]{2,1,0:T(8,128)}, f32[16,64,128]{2,1,0:T(8,128)}, u32[]{:S(2)}, u32[]{:S(2)}) collective-permute-start(f32[16,64,128]{2,1,0:T(8,128)} %get-tuple-element.19), channel_id=1, source_target_pairs={{0,16},{16,0},{1,17},{17,1},{2,18},{18,2},{3,19},{19,3},{4,20},{20... | collective-permute-start | bytes 1572872 | tf_op jit(solution)/shard_map/ppermute | solution.py:25
  41.0 3.5 %shard_map.265 = (f32[16,8,128]{2,1,0:T(8,128)S(1)}, f32[16,8,128]{2,1,0:T(8,128)S(1)}, f32[32,8,128]{2,1,0:T(8,128)}) custom-call(s32[4]{0:T(128)S(1)} %pad_add_fusion.spots, f32[8,128,128]{2,1,0:T(8,128)} %all-to-all-done.shared, f32[1,1,2,192,192]{4,3,2,1,0:T(8,128)S(1)} %copy-done.11, f32[1,2,192,128]{3,2,1,0:T(8,128)S(1)} %copy-done.15, ...), custom_call_target="tpu_custom_call" | custom-call | flops 1000000000 | bytes 4194304 | tf_op jit(solution)/shard_map/pallas_call | solution.py:287
  44.4 5.9 %all-to-all-start.1 = ((f32[32,8,128]{2,1,0:T(8,128)}), f32[32,8,128]{2,1,0:T(8,128)S(1)}, u32[]{:S(2)}, u32[]{:S(2)}) async-start(f32[32,8,128]{2,1,0:T(8,128)} %get-tuple-element.15), calls=%async_computation.1 | async-start | bytes 262144 | tf_op jit(solution)/shard_map/all_to_all | solution.py:17
  50.3 2.1 collective-permute-start
  52.5 2.1 add.56
  54.6 3.3 %all-to-all-done.1 = f32[32,8,128]{2,1,0:T(8,128)S(1)} async-done(((f32[32,8,128]{2,1,0:T(8,128)}), f32[32,8,128]{2,1,0:T(8,128)S(1)}, u32[]{:S(2)}, u32[]{:S(2)}) %all-to-all-start.1) | async-done | bytes 131104 | tf_op jit(solution)/shard_map/all_to_all | solution.py:17
  57.9 1.9 pad_maximum_fusion
  59.9 12.3 %all-to-all-start.2 = ((f32[16,80,128]{2,1,0:T(8,128)}), f32[16,80,128]{2,1,0:T(8,128)}, u32[]{:S(2)}, u32[]{:S(2)}) async-start(f32[16,80,128]{2,1,0:T(8,128)} %pad_maximum_fusion), calls=%async_computation.2 | async-start | bytes 1310720 | tf_op jit(solution)/shard_map/all_to_all | solution.py:17
  73.9 27.2 %all-to-all-done.2 = f32[16,80,128]{2,1,0:T(8,128)} async-done(((f32[16,80,128]{2,1,0:T(8,128)}), f32[16,80,128]{2,1,0:T(8,128)}, u32[]{:S(2)}, u32[]{:S(2)}) %all-to-all-start.2) | async-done | bytes 655392 | tf_op jit(solution)/shard_map/all_to_all | solution.py:17
  105.7 10.1 %all-to-all-start.3 = ((f32[32,24,128]{2,1,0:T(8,128)}), f32[32,24,128]{2,1,0:T(8,128)S(1)}, u32[]{:S(2)}, u32[]{:S(2)}) async-start(f32[32,24,128]{2,1,0:T(8,128)} %broadcast_in_dim.87), calls=%async_computation.3 | async-start | bytes 786432 | tf_op jit(solution)/shard_map/all_to_all | solution.py:17
  116.6 1.3 slice_bitcast_fusion.26
  118.6 6.7 %all-to-all-done.3.gains = f32[32,24,128]{2,1,0:T(8,128)S(1)} async-done(((f32[32,24,128]{2,1,0:T(8,128)}), f32[32,24,128]{2,1,0:T(8,128)S(1)}, u32[]{:S(2)}, u32[]{:S(2)}) %all-to-all-start.3) | async-done | bytes 393248 | tf_op jit(solution)/shard_map/all_to_all | solution.py:17
  133.3 5.5 %all-to-all-start.4 = ((f32[32,8,128]{2,1,0:T(8,128)}), f32[32,8,128]{2,1,0:T(8,128)}, u32[]{:S(2)}, u32[]{:S(2)}) async-start(f32[32,8,128]{2,1,0:T(8,128)} %maximum_bitcast_fusion), calls=%async_computation.4 | async-start | bytes 262144 | tf_op jit(solution)/shard_map/all_to_all | solution.py:17
  140.0 6.3 %all-to-all-done.4 = f32[32,8,128]{2,1,0:T(8,128)} async-done(((f32[32,8,128]{2,1,0:T(8,128)}), f32[32,8,128]{2,1,0:T(8,128)}, u32[]{:S(2)}, u32[]{:S(2)}) %all-to-all-start.4) | async-done | bytes 131104 | tf_op jit(solution)/shard_map/all_to_all | solution.py:17
  146.3 1.5 reduce_sum.77
  151.3 5.1 %concatenate.80 = f32[48,128]{1,0:T(8,128)} concatenate(f32[24,128]{1,0:T(8,128)} %get-tuple-element.64, f32[8,128]{1,0:T(8,128)} %get-tuple-element.80, f32[8,128]{1,0:T(8,128)} %get-tuple-element.33, f32[2,128]{1,0:T(2,128)} %get-tuple-element.95, f32[2,128]{1,0:T(2,128)} %get-tuple-element.90, f32[4,128]{1,0:T(4,128)S(1)} %broadcast.56), dimensions={0} | concatenate | bytes 49152 | tf_op jit(solution)/shard_map/concatenate | solution.py:444
  156.4 5.1 %concatenate.81 = f32[48,128]{1,0:T(8,128)} concatenate(f32[24,128]{1,0:T(8,128)} %get-tuple-element.64, f32[8,128]{1,0:T(8,128)} %get-tuple-element.80, f32[8,128]{1,0:T(8,128)} %get-tuple-element.32, f32[2,128]{1,0:T(2,128)} %get-tuple-element.96, f32[2,128]{1,0:T(2,128)} %get-tuple-element.90, f32[4,128]{1,0:T(4,128)S(1)} %broadcast.56), dimensions={0} | concatenate | bytes 49152 | tf_op jit(solution)/shard_map/concatenate | solution.py:444
  161.5 1.4 maximum_bitcast_fusion.2
  162.9 4.4 %concatenate.78 = f32[48,128]{1,0:T(8,128)} concatenate(f32[24,128]{1,0:T(8,128)} %get-tuple-element.63, f32[8,128]{1,0:T(8,128)S(1)} %get-tuple-element.79, f32[8,128]{1,0:T(8,128)} %get-tuple-element.34, f32[2,128]{1,0:T(2,128)} %get-tuple-element.97, f32[2,128]{1,0:T(2,128)} %get-tuple-element.89, f32[4,128]{1,0:T(4,128)S(1)} %broadcast.56), dimensions={0} | concatenate | bytes 49152 | tf_op jit(solution)/shard_map/concatenate | solution.py:444
  167.3 4.4 %concatenate.77 = f32[48,128]{1,0:T(8,128)} concatenate(f32[24,128]{1,0:T(8,128)} %get-tuple-element.63, f32[8,128]{1,0:T(8,128)S(1)} %get-tuple-element.79, f32[8,128]{1,0:T(8,128)} %get-tuple-element.31, f32[2,128]{1,0:T(2,128)} %get-tuple-element.98, f32[2,128]{1,0:T(2,128)} %get-tuple-element.89, f32[4,128]{1,0:T(4,128)S(1)} %broadcast.56), dimensions={0} | concatenate | bytes 49152 | tf_op jit(solution)/shard_map/concatenate | solution.py:444
  174.1 6.6 %all-to-all-start.5 = ((f32[16,48,128]{2,1,0:T(8,128)}), f32[16,48,128]{2,1,0:T(8,128)}, u32[]{:S(2)}, u32[]{:S(2)}) async-start(f32[16,48,128]{2,1,0:T(8,128)} %bitcast.204), calls=%async_computation.5 | async-start | bytes 786432 | tf_op jit(solution)/shard_map/all_to_all | solution.py:17
  180.8 17.7 %all-to-all-done.5 = f32[16,48,128]{2,1,0:T(8,128)} async-done(((f32[16,48,128]{2,1,0:T(8,128)}), f32[16,48,128]{2,1,0:T(8,128)}, u32[]{:S(2)}, u32[]{:S(2)}) %all-to-all-start.5) | async-done | bytes 393248 | tf_op jit(solution)/shard_map/all_to_all | solution.py:17
  201.3 9.2 %collective-permute-start.2 = (f32[576,128]{1,0:T(8,128)S(1)}, f32[576,128]{1,0:T(8,128)S(1)}, u32[]{:S(2)}, u32[]{:S(2)}) collective-permute-start(f32[576,128]{1,0:T(8,128)S(1)} %pad_maximum_fusion.1.mine), channel_id=1, source_target_pairs={{0,16},{16,0},{1,17},{17,1},{2,18},{18,2},{3,19},{19,3},{4,20},{20... | collective-permute-start | bytes 884744 | tf_op jit(solution)/shard_map/ppermute | solution.py:25
  210.5 10.5 %all_to_all.40.lows = f32[32,4,128]{2,1,0:T(4,128)S(1)} all-to-all(f32[32,4,128]{2,1,0:T(4,128)S(1)} %bitcast.216), channel_id=1, replica_groups=mesh['a'=2,'e'=2,'z'=4,'k'=2,'d'=2,'c'=8] {'k','d','c'}, dimensions={0} | all-to-all | bytes 131072 | tf_op jit(solution)/shard_map/all_to_all | solution.py:17
  221.1 5.4 %shard_map.266 = f32[8,128,128]{2,1,0:T(8,128)S(1)} custom-call(s32[4]{0:T(128)S(1)} %pad_add_fusion.spots, s32[14]{0:T(128)S(1)} %copy-done.6, f32[32,24,128]{2,1,0:T(8,128)S(1)} %all-to-all-done.3.gains, f32[32,4,128]{2,1,0:T(4,128)S(1)} %all_to_all.40.lows, f32[576,128]{1,0:T(8,128)S(1)} %pad_maximum_fusion.1.mine, ...), custom_call_target="tpu_custom_call" | custom-call | flops 3000000000 | bytes 4194304 | tf_op jit(solution)/shard_map/pallas_call | solution.py:287
  227.3 3.6 %all-to-all-start.7 = ((f32[8,128,128]{2,1,0:T(8,128)}), f32[8,128,128]{2,1,0:T(8,128)S(1)}, u32[]{:S(2)}, u32[]{:S(2)}) async-start(f32[8,128,128]{2,1,0:T(8,128)} %copy-done.1), calls=%async_computation.7 | async-start | bytes 1048576 | tf_op jit(solution)/shard_map/all_to_all | solution.py:17
  230.9 10.2 %all-to-all-done.7 = f32[8,128,128]{2,1,0:T(8,128)S(1)} async-done(((f32[8,128,128]{2,1,0:T(8,128)}), f32[8,128,128]{2,1,0:T(8,128)S(1)}, u32[]{:S(2)}, u32[]{:S(2)}) %all-to-all-start.7) | async-done | bytes 524320 | tf_op jit(solution)/shard_map/all_to_all | solution.py:17
  241.7 2.8 %collective-permute-start.3 = (f32[24,128]{1,0:T(8,128)S(1)}, f32[24,128]{1,0:T(8,128)S(1)}, u32[]{:S(2)}, u32[]{:S(2)}) collective-permute-start(f32[24,128]{1,0:T(8,128)S(1)} %dynamic-slice_bitcast_fusion), channel_id=1, source_target_pairs={{0,8},{8,0},{1,9},{9,1},{2,10},{10,2},{3,11},{11,3},{4,12},{12,4},... | collective-permute-start | bytes 36872 | tf_op jit(solution)/shard_map/ppermute | solution.py:25
  244.6 2.9 %shard_map.267 = f32[1,1,384,128]{3,2,1,0:T(8,128)} custom-call(s32[1,1]{1,0:T(1,128)S(6)} %copy.210.ranks, f32[32,128]{1,0:T(8,128)S(1)} %slice.565.low, f32[384,128]{1,0:T(8,128)S(1)} %copy-done.23, f32[1,1,2,384,384]{4,3,2,1,0:T(8,128)S(1)} %copy-done.8, f32[1,1,2,384,32]{4,3,2,1,0:T(8,128)S(1)} %copy-done.5), custom_call_target="tpu_custom_call" | custom-call | flops 1000000000 | bytes 4194304 | tf_op jit(solution)/shard_map/pallas_call | solution.py:287
  (197 shorter events, 45.6 us)
Async XLA Ops:
  6.0 2.8 %copy-start.4 = (f32[1,1,2,384,32]{4,3,2,1,0:T(8,128)}, f32[1,1,2,384,32]{4,3,2,1,0:T(8,128)S(1)}, u32[]{:S(2)}) copy-start(f32[1,1,2,384,32]{4,3,2,1,0:T(8,128)S(1)} %copy.137.basis) | copy-start | bytes 294916
  6.1 9.5 %copy-start.38 = (f32[1,1,2,2,96,32]{4,5,3,2,1,0:T(8,128)S(1)}, f32[1,1,2,2,96,32]{4,5,3,2,1,0:T(8,128)}, u32[]{:S(2)}) copy-start(f32[1,1,2,2,96,32]{4,5,3,2,1,0:T(8,128)} %param.34) | copy-start | bytes 147460
  9.6 6.1 %copy-start.39 = (f32[1,1,2,2,96,32]{4,5,3,2,1,0:T(8,128)S(1)}, f32[1,1,2,2,96,32]{4,5,3,2,1,0:T(8,128)}, u32[]{:S(2)}) copy-start(f32[1,1,2,2,96,32]{4,5,3,2,1,0:T(8,128)} %param.35) | copy-start | bytes 147460
  9.6 6.3 %copy-start.33 = (f32[1,2,2,192,32]{3,4,2,1,0:T(8,128)S(1)}, f32[1,2,2,192,32]{3,4,2,1,0:T(8,128)}, u32[]{:S(2)}) copy-start(f32[1,2,2,192,32]{3,4,2,1,0:T(8,128)} %param.42) | copy-start | bytes 294916
  9.6 6.5 %copy-start.34 = (f32[1,2,2,2,96,32]{4,5,3,2,1,0:T(8,128)S(1)}, f32[1,2,2,2,96,32]{4,5,3,2,1,0:T(8,128)}, u32[]{:S(2)}) copy-start(f32[1,2,2,2,96,32]{4,5,3,2,1,0:T(8,128)} %param.36) | copy-start | bytes 294916
  9.6 6.7 %copy-start.27 = (f32[1,1,2,384,192]{3,4,2,1,0:T(8,128)S(1)}, f32[1,1,2,384,192]{3,4,2,1,0:T(8,128)}, u32[]{:S(2)}) copy-start(f32[1,1,2,384,192]{3,4,2,1,0:T(8,128)} %param.24) | copy-start | bytes 1769476
  9.6 28.6 %all-to-all-start = ((f32[8,128,128]{2,1,0:T(8,128)}), f32[8,128,128]{2,1,0:T(8,128)}, u32[]{:S(2)}, u32[]{:S(2)}) async-start(f32[8,128,128]{2,1,0:T(8,128)} %get-tuple-element.13), calls=%async_computation | async-start | bytes 1048576 | tf_op jit(solution)/shard_map/all_to_all | solution.py:17
  16.1 2.4 copy-start.2
  16.9 1.6 copy-start.18
  16.9 1.6 copy-start.19
  16.9 1.6 copy-start.20
  29.9 22.5 %collective-permute-start.1 = (f32[16,64,128]{2,1,0:T(8,128)}, f32[16,64,128]{2,1,0:T(8,128)}, u32[]{:S(2)}, u32[]{:S(2)}) collective-permute-start(f32[16,64,128]{2,1,0:T(8,128)} %get-tuple-element.19), channel_id=1, source_target_pairs={{0,16},{16,0},{1,17},{17,1},{2,18},{18,2},{3,19},{19,3},{4,20},{20... | collective-permute-start | bytes 1572872 | tf_op jit(solution)/shard_map/ppermute | solution.py:25
  44.4 13.4 %all-to-all-start.1 = ((f32[32,8,128]{2,1,0:T(8,128)}), f32[32,8,128]{2,1,0:T(8,128)S(1)}, u32[]{:S(2)}, u32[]{:S(2)}) async-start(f32[32,8,128]{2,1,0:T(8,128)} %get-tuple-element.15), calls=%async_computation.1 | async-start | bytes 262144 | tf_op jit(solution)/shard_map/all_to_all | solution.py:17
  50.3 4.2 %collective-permute-start = (f32[16,8,128]{2,1,0:T(8,128)S(1)}, f32[16,8,128]{2,1,0:T(8,128)S(1)}, u32[]{:S(2)}, u32[]{:S(2)}) collective-permute-start(f32[16,8,128]{2,1,0:T(8,128)S(1)} %get-tuple-element.17), channel_id=1, source_target_pairs={{0,16},{16,0},{1,17},{17,1},{2,18},{18,2},{3,19},{19,3},{4,20},{20... | collective-permute-start | bytes 196616 | tf_op jit(solution)/shard_map/ppermute | solution.py:25
  57.9 14.2 %copy-start.6 = (s32[14]{0:T(128)S(1)}, s32[14]{0:T(128)}, u32[]{:S(2)}) copy-start(s32[14]{0:T(128)} %ranks.3) | copy-start | bytes 172
  59.9 41.2 %all-to-all-start.2 = ((f32[16,80,128]{2,1,0:T(8,128)}), f32[16,80,128]{2,1,0:T(8,128)}, u32[]{:S(2)}, u32[]{:S(2)}) async-start(f32[16,80,128]{2,1,0:T(8,128)} %pad_maximum_fusion), calls=%async_computation.2 | async-start | bytes 1310720 | tf_op jit(solution)/shard_map/all_to_all | solution.py:17
  105.7 19.7 %all-to-all-start.3 = ((f32[32,24,128]{2,1,0:T(8,128)}), f32[32,24,128]{2,1,0:T(8,128)S(1)}, u32[]{:S(2)}, u32[]{:S(2)}) async-start(f32[32,24,128]{2,1,0:T(8,128)} %broadcast_in_dim.87), calls=%async_computation.3 | async-start | bytes 786432 | tf_op jit(solution)/shard_map/all_to_all | solution.py:17
  116.6 1.3 copy-start.30
  125.5 1.7 copy-start.40
  127.0 3.0 %copy-start.35 = (f32[2,1,8,64]{3,2,0,1:T(8,128)S(1)}, f32[2,1,8,64]{3,2,0,1:T(8,128)}, u32[]{:S(2)}) copy-start(f32[2,1,8,64]{3,2,0,1:T(8,128)} %get-tuple-element.49) | copy-start | bytes 12292
  127.0 3.0 %copy-start.36 = (f32[2,1,8,64]{3,2,0,1:T(8,128)S(1)}, f32[2,1,8,64]{3,2,0,1:T(8,128)}, u32[]{:S(2)}) copy-start(f32[2,1,8,64]{3,2,0,1:T(8,128)} %get-tuple-element.50) | copy-start | bytes 12292
  133.3 13.1 %all-to-all-start.4 = ((f32[32,8,128]{2,1,0:T(8,128)}), f32[32,8,128]{2,1,0:T(8,128)}, u32[]{:S(2)}, u32[]{:S(2)}) async-start(f32[32,8,128]{2,1,0:T(8,128)} %maximum_bitcast_fusion), calls=%async_computation.4 | async-start | bytes 262144 | tf_op jit(solution)/shard_map/all_to_all | solution.py:17
  174.1 24.3 %all-to-all-start.5 = ((f32[16,48,128]{2,1,0:T(8,128)}), f32[16,48,128]{2,1,0:T(8,128)}, u32[]{:S(2)}, u32[]{:S(2)}) async-start(f32[16,48,128]{2,1,0:T(8,128)} %bitcast.204), calls=%async_computation.5 | async-start | bytes 786432 | tf_op jit(solution)/shard_map/all_to_all | solution.py:17
  198.4 22.6 %copy-start.3 = (f32[1,2,2,192,32]{4,3,2,1,0:T(8,128)S(1)}, f32[1,2,2,192,32]{4,3,2,1,0:T(8,128)}, u32[]{:S(2)}) copy-start(f32[1,2,2,192,32]{4,3,2,1,0:T(8,128)} %copy-done.2) | copy-start | bytes 294916
  198.4 22.6 %copy-start.10 = (f32[1,1,2,192,192]{4,3,2,1,0:T(8,128)S(1)}, f32[1,1,2,192,192]{4,3,2,1,0:T(8,128)}, u32[]{:S(2)}) copy-start(f32[1,1,2,192,192]{4,3,2,1,0:T(8,128)} %inverse1.3) | copy-start | bytes 884740
  198.4 22.6 %copy-start.12 = (f32[1,1,2,192,192]{4,3,2,1,0:T(8,128)S(1)}, f32[1,1,2,192,192]{4,3,2,1,0:T(8,128)}, u32[]{:S(2)}) copy-start(f32[1,1,2,192,192]{4,3,2,1,0:T(8,128)} %inverse3.1) | copy-start | bytes 884740
  201.3 19.8 %collective-permute-start.2 = (f32[576,128]{1,0:T(8,128)S(1)}, f32[576,128]{1,0:T(8,128)S(1)}, u32[]{:S(2)}, u32[]{:S(2)}) collective-permute-start(f32[576,128]{1,0:T(8,128)S(1)} %pad_maximum_fusion.1.mine), channel_id=1, source_target_pairs={{0,16},{16,0},{1,17},{17,1},{2,18},{18,2},{3,19},{19,3},{4,20},{20... | collective-permute-start | bytes 884744 | tf_op jit(solution)/shard_map/ppermute | solution.py:25
  227.3 17.3 %copy-start.5 = (f32[1,1,2,384,32]{4,3,2,1,0:T(8,128)S(1)}, f32[1,1,2,384,32]{4,3,2,1,0:T(8,128)}, u32[]{:S(2)}) copy-start(f32[1,1,2,384,32]{4,3,2,1,0:T(8,128)} %copy-done.4) | copy-start | bytes 294916
  227.3 17.3 %copy-start.8 = (f32[1,1,2,384,384]{4,3,2,1,0:T(8,128)S(1)}, f32[1,1,2,384,384]{4,3,2,1,0:T(8,128)}, u32[]{:S(2)}) copy-start(f32[1,1,2,384,384]{4,3,2,1,0:T(8,128)} %inverse.5) | copy-start | bytes 3538948
  227.3 17.3 %copy-start.23 = (f32[384,128]{1,0:T(8,128)S(1)}, f32[384,128]{1,0:T(8,128)}, u32[]{:S(2)}) copy-start(f32[384,128]{1,0:T(8,128)} %copy-done.22) | copy-start | bytes 589828
  227.3 13.8 %all-to-all-start.7 = ((f32[8,128,128]{2,1,0:T(8,128)}), f32[8,128,128]{2,1,0:T(8,128)S(1)}, u32[]{:S(2)}, u32[]{:S(2)}) async-start(f32[8,128,128]{2,1,0:T(8,128)} %copy-done.1), calls=%async_computation.7 | async-start | bytes 1048576 | tf_op jit(solution)/shard_map/all_to_all | solution.py:17
  241.7 5.9 %collective-permute-start.3 = (f32[24,128]{1,0:T(8,128)S(1)}, f32[24,128]{1,0:T(8,128)S(1)}, u32[]{:S(2)}, u32[]{:S(2)}) collective-permute-start(f32[24,128]{1,0:T(8,128)S(1)} %dynamic-slice_bitcast_fusion), channel_id=1, source_target_pairs={{0,8},{8,0},{1,9},{9,1},{2,10},{10,2},{3,11},{11,3},{4,12},{12,4},... | collective-permute-start | bytes 36872 | tf_op jit(solution)/shard_map/ppermute | solution.py:25
  (20 other events, 17.5 us)

commit v4 on v3

v4 whole, which is shorter than its diff:
```python
import jax
import jax.numpy as jnp
from jax import lax
from jax.experimental import pallas as pl
from jax.experimental.pallas import tpu as pltpu
from jax.sharding import Mesh, PartitionSpec as P

precise = lax.Precision.HIGHEST

ROW = ("a", "e", "z", "k")
COL = ("d", "c")
CHIPS = ("a", "e", "z")
PLANE = ("k", "d", "c")


def exchange(pieces, axes):
    return lax.all_to_all(pieces, axes, 0, 0)


def partner(values, axis):
    return lax.ppermute(values, axis, [(0, 1), (1, 0)])


def turned(values):
    groups = []
    for at in range(0, values.shape[-1], 128):
        groups += [-values[:, at + 64 : at + 128], values[:, at : at + 64]]
    return jnp.concatenate(groups, axis=-1)


def dot(left, right, contract=1):
    return lax.dot_general(
        left,
        right,
        (((contract,), (0,)), ((), ())),
        precision=precise,
        preferred_element_type=jnp.float32,
    )


def times(real, imag, vector):
    return dot(real, vector) + dot(imag, turned(vector))


def times_back(real, imag, vector):
    return dot(real, vector, 0) + dot(imag, turned(vector), 0)


def cut(values, limit):
    rows = lax.broadcasted_iota(jnp.int32, values.shape, 0)
    return jnp.where(rows < limit, values, jnp.zeros_like(values))


def leaf_kernel(ranks, forward, packs, inverse, source, basis, update, slots):
    inner = inverse.shape[-1]
    result = times(inverse[0, 0, 0], inverse[0, 0, 1], source[0, 0])
    forward[...] = result
    low = cut(times(basis[0, 0, 0], basis[0, 0, 1], result), ranks[0, 0])
    height = inner // 2
    places = lax.broadcasted_iota(jnp.int32, (height, slots.shape[-1]), 0)
    onehot = (places == slots[0]).astype(jnp.float32)
    flat = jnp.concatenate([update[0, 0, 0], update[0, 0, 1]], axis=0)
    spread_out = lax.dot_general(
        flat,
        onehot,
        (((1,), (1,)), ((), ())),
        precision=precise,
        preferred_element_type=jnp.float32,
    )
    half = low.shape[0]
    pack = jnp.concatenate(
        [
            low,
            spread_out[:, :128],
            jnp.concatenate([spread_out[:half, 128:], spread_out[half:, 128:]], axis=-1),
        ],
        axis=0,
    )
    for place in range(packs.shape[0]):
        packs[place] = pack


def apply_kernel(
    spots,
    keep,
    send,
    lows,
    inverse0,
    inverse1,
    inverse2,
    source0,
    source1,
    source2,
    update0,
    update1,
    update2,
    slots0,
    slots1,
    slots2,
    basis1,
    basis2,
):
    a, k, d = spots[0], spots[2], spots[3]
    results = []
    for inverse, source, update, slots, at in (
        (inverse0, source0, update0, slots0, 0),
        (inverse1, source1, update1, slots1, 0),
        (inverse2, source2, update2, slots2, d),
    ):
        right = source[0, at]
        height = right.shape[0]
        lists = slots[0, at]
        places = lax.broadcasted_iota(jnp.int32, (height, lists.shape[-1]), 0)
        spread_out = jnp.zeros((height, 128), jnp.float32)
        for child in range(2):
            onehot = (places == lists[child : child + 1]).astype(jnp.float32)
            real, imag = update[0, at, child, 0], update[0, at, child, 1]
            nothing = jnp.zeros_like(real)
            order = [real, nothing, imag, nothing] if child == 0 else [nothing, real, nothing, imag]
            spread_out += lax.dot_general(
                onehot,
                jnp.concatenate(order, axis=0),
                (((1,), (1,)), ((), ())),
                precision=precise,
                preferred_element_type=jnp.float32,
            )
        both = jnp.concatenate([right, spread_out], axis=-1)
        apply = times if inverse is inverse1 else times_back
        results.append(apply(inverse[0, 0, 0], inverse[0, 0, 1], both))
    low2 = times(basis2[0, a, 0], basis2[0, a, 1], results[2])
    low1 = times(basis1[0, a, 0], basis1[0, a, 1], results[1])
    lows[0] = low2[:, :128]
    lows[1] = low2[:, 128:]
    lows[2] = low1[:, :128]
    lows[3] = low1[:, 128:]

    def put(target, half):
        for side in range(2):
            for level, at in ((0, 0), (2, 8)):
                rows = results[level].shape[0] // 2
                part = results[level][half * rows : (half + 1) * rows, side * 128 : side * 128 + 128]
                target[at : at + 8, 24 * side : 24 * side + 24] = part.reshape(8, 24, 128)
            rows = results[1].shape[0] // 2
            part = results[1][half * rows : (half + 1) * rows, side * 128 : side * 128 + 128]
            row = 48 + 8 * side
            target[0:12, row : row + 8] = part.reshape(12, 8, 128)
            target[12:16, row : row + 8] = jnp.zeros((4, 8, 128), jnp.float32)

    for half in range(2):

        @pl.when(k == half)
        def _(half=half):
            put(keep, half)
            put(send, 1 - half)


def lower_kernel(spots, shared, lows, keep, send, rows, inverse, source, basis):
    a, e, k, d = spots[0], spots[1], spots[2], spots[3]
    low = shared[:, 0:32].reshape(256, 128)
    low_turned = turned(low)
    packs = shared[:, 96:128].reshape(256, 128)
    top = dot(shared[:, 32:64].reshape(256, 128), low, 0) + dot(
        shared[:, 64:96].reshape(256, 128), low_turned, 0
    )
    rest = dot(packs[:, :64], low, 0) + dot(packs[:, 64:], low_turned, 0)
    side = source[0, d] - jnp.concatenate([top, rest], axis=0)
    partial = times(inverse[0, 0, 0], inverse[0, 0, 1], side)
    front = 2 * a + e
    low3 = times(basis[0, front, 0], basis[0, front, 1], partial)
    rows[:, 0, :] = low3
    for at in range(4):
        rows[:, at + 1, :] = lows[at]
    for at in range(5, 8):
        rows[:, at, :] = jnp.zeros((32, 128), jnp.float32)
    count = partial.shape[0] // 2

    def put(target, half):
        target[0:12] = partial[half * count : (half + 1) * count].reshape(12, 8, 128)
        target[12:16] = jnp.zeros((4, 8, 128), jnp.float32)

    for half in range(2):

        @pl.when(k == half)
        def _(half=half):
            put(keep, half)
            put(send, 1 - half)


def backward_kernel(
    spots,
    ranks,
    gains,
    lows,
    mine,
    theirs,
    inverse0,
    inverse1,
    inverse2,
    inverse3,
    basis1,
    basis2,
    basis3,
    shared,
    pieces,
):
    a, e, k, d = spots[0], spots[1], spots[2], spots[3]

    def gain_back(gain, low, child):
        both = times_back(gain[:, :64], gain[:, 64:], low)
        return jnp.where(child == 0, both[:32], both[32:])

    gain1 = jnp.where(a == 0, gains[:, 18, :], gains[:, 19, :])
    gain2 = jnp.where(
        a == 0,
        jnp.where(d == 0, gains[:, 12, :], gains[:, 13, :]),
        jnp.where(d == 0, gains[:, 14, :], gains[:, 15, :]),
    )
    back1 = cut(lows[:, 0, :], ranks[a])
    back2 = cut(lows[:, 1, :] - gain_back(gain1, back1, d), ranks[2 + 2 * a + d])
    back3 = cut(lows[:, 2, :] - gain_back(gain2, back2, e), ranks[6 + 4 * a + 2 * e + d])

    def whole(start, stop):
        left, right = mine[start:stop], theirs[start:stop]
        return jnp.concatenate(
            [jnp.where(k == 0, left, right), jnp.where(k == 0, right, left)], axis=0
        )

    front = 2 * a + e
    residuals = (
        whole(0, 192),
        whole(384, 480) - times_back(basis1[0, a, 0], basis1[0, a, 1], back1),
        whole(192, 384) - times_back(basis2[0, a, 0], basis2[0, a, 1], back2),
        whole(480, 576) - times_back(basis3[0, front, 0], basis3[0, front, 1], back3),
    )
    solved = [
        times(inverse0[0, 0, 0], inverse0[0, 0, 1], residuals[0]),
        times_back(inverse1[0, 0, 0], inverse1[0, 0, 1], residuals[1]),
        times(inverse2[0, 0, 0], inverse2[0, 0, 1], residuals[2]),
        times_back(inverse3[0, 0, 0], inverse3[0, 0, 1], residuals[3]),
    ]
    for level in range(2):
        for place in range(2):
            for to_c in range(8):
                at = 96 * place + 12 * to_c
                row = 24 * place + 12 * level
                pieces[to_c, row : row + 12] = solved[level][at : at + 12]
    pieces[:, 48:72] = solved[2].reshape(8, 24, 128)
    pieces[:, 72:96] = solved[3].reshape(8, 24, 128)
    lowest = solved[3]
    lowest_turned = turned(lowest)
    packs = shared[:, 96:128].reshape(256, 128)
    parts = (
        dot(shared[:, 32:64].reshape(256, 128), lowest[:128])
        + dot(shared[:, 64:96].reshape(256, 128), lowest_turned[:128])
        + dot(packs[:, :64], lowest[128:])
        + dot(packs[:, 64:], lowest_turned[128:])
    )
    pieces[:, 96:128] = parts.reshape(8, 32, 128)


def last_kernel(ranks, low, forward, inverse, basis, solved):
    back = cut(low[...], ranks[0, 0])
    rest = forward[...] - times_back(basis[0, 0, 0], basis[0, 0, 1], back)
    solved[0, 0] = times_back(inverse[0, 0, 0], inverse[0, 0, 1], rest)


def gather_kernel(parts, applied_keep, applied_got, lower_keep, lower_got, pieces):
    sums = []
    for place in range(2):
        total = jnp.zeros((8, 128), jnp.float32)
        for core in range(2):
            for at in range(8):
                total += parts[16 * core + 8 * place + at]
        sums.append(total)
    rows = [sums[place][row : row + 1] for row in range(3) for place in range(2)]
    rows += [sums[0][3:5] + sums[1][3:5]]
    tile = jnp.concatenate(rows, axis=0)
    for chip in range(16):
        pieces[chip, 0:8] = tile
        pieces[chip, 8:16] = lower_keep[chip] + lower_got[chip]
        pieces[chip, 16:80] = applied_keep[chip] + applied_got[chip]


def total_kernel(parts, pieces, sums, lower):
    tiles = []
    for at in range(4):
        total = parts[4 * at]
        for chip in range(1, 4):
            total += parts[4 * at + chip]
        tiles.append(total)
        lower[at] = total[8:16]
    upper = []
    for place in range(2):
        total = tiles[2 * place] + tiles[2 * place + 1]
        sums[place] = total[16:80]
        upper.append(total)
    rows = [tile[0:2] for tile in tiles]
    for start, stop in ((2, 4), (4, 6), (6, 7), (7, 8)):
        rows += [total[start:stop] for total in upper]
    rows += [jnp.zeros((4, 128), jnp.float32)]
    tile = jnp.concatenate(rows, axis=0)
    for place in range(32):
        pieces[place] = tile


def forward_kernel(spots, ranks, gains, sums, wide_out, upper_out, rows):
    a, d = spots[0], spots[3]
    coeffs3 = [cut(gains[:, at, :], ranks[6 + at]) for at in range(8)]
    pairs3 = [
        [jnp.concatenate([coeffs3[4 * x + y], coeffs3[4 * x + 2 + y]], axis=0) for y in range(2)]
        for x in range(2)
    ]

    def chain(total, gain, pair, limit):
        return cut(total - times(gain[:, :64], gain[:, 64:], pair), limit)

    pairs2 = []
    for x in range(2):
        both = [
            chain(
                gains[:, 8 + 2 * x + y, :],
                gains[:, 12 + 2 * x + y, :],
                pairs3[x][y],
                ranks[2 + 2 * x + y],
            )
            for y in range(2)
        ]
        pairs2.append(jnp.concatenate(both, axis=0))
    pair1 = jnp.concatenate(
        [chain(gains[:, 16 + x, :], gains[:, 18 + x, :], pairs2[x], ranks[x]) for x in range(2)],
        axis=0,
    )
    everything = sums[0, 0:48] + sums[1, 0:48]
    for x in range(2):
        below = jnp.where(a == 0, pair1, jnp.where(d == 0, pairs3[x][0], pairs3[x][1]))
        slices = jnp.where(a == 0, everything, sums[x, 0:48])
        gain = slices[24:48]
        result = slices[0:24] - times(gain[:, :64], gain[:, 64:], below)
        wide_out[x] = result
        low = times_back(gain[:, :64], gain[:, 64:], result)
        rows[:, 2 * x, :] = low[:32]
        rows[:, 2 * x + 1, :] = low[32:]
        gain = sums[x, 56:64]
        result = sums[x, 48:56] - times(gain[:, :64], gain[:, 64:], pairs2[x])
        upper_out[x] = result
        low = times_back(gain[:, :64], gain[:, 64:], result)
        rows[:, 4 + 2 * x, :] = low[:32]
        rows[:, 5 + 2 * x, :] = low[32:]


def slices_kernel(spots, parts, wide, upper, lower, pieces):
    a = spots[0]
    sums = []
    for place in range(2):
        total = jnp.zeros((8, 128), jnp.float32)
        for core in range(2):
            for at in range(8):
                total += parts[16 * core + 8 * place + at]
        sums.append(total)
    joined = sums[0] + sums[1]
    nothing = jnp.zeros((1, 128), jnp.float32)
    for to_a in range(2):
        for to_e in range(2):
            row = 2 * to_a + to_e
            tile = jnp.concatenate(
                [
                    jnp.where(a == 0, joined[to_a : to_a + 1], sums[0][row : row + 1]),
                    jnp.where(a == 0, nothing, sums[1][row : row + 1]),
                    joined[4 + 2 * to_a : 6 + 2 * to_a],
                    jnp.zeros((4, 128), jnp.float32),
                ],
                axis=0,
            )
            for chip in range(4):
                place = 8 * to_a + 4 * to_e + chip
                pieces[place, 0:24] = wide[to_a]
                pieces[place, 24:32] = upper[to_a]
                pieces[place, 32:40] = lower[row]
                pieces[place, 40:48] = tile


def arrange_kernel(parts, mine, pieces):
    for chip in range(8):
        mine[24 * chip : 24 * chip + 24] = parts[chip, 0:24]
        mine[192 + 24 * chip : 216 + 24 * chip] = parts[8 + chip, 0:24]
    for chip in range(12):
        mine[384 + 8 * chip : 392 + 8 * chip] = parts[chip, 24:32]
        mine[480 + 8 * chip : 488 + 8 * chip] = parts[chip, 32:40]
    sums = []
    for place in range(2):
        total = parts[8 * place, 40:48]
        for chip in range(1, 8):
            total += parts[8 * place + chip, 40:48]
        sums.append(total)
    upper = sums[0] + sums[1]
    tail = jnp.zeros((5, 128), jnp.float32)
    for to_d in range(2):
        tile = jnp.concatenate(
            [sums[0][0:1], upper[2 + to_d : 3 + to_d], sums[1][to_d : to_d + 1], tail], axis=0
        )
        for core in range(2):
            for to_c in range(8):
                pieces[16 * core + 8 * to_d + to_c] = tile


def flipped(values):
    return jnp.swapaxes(values, -1, -2)


def call(kernel, shapes, scalars, arrays, flops, fetched=()):
    count = len(fetched)
    before = len(scalars) + len(arrays)

    def outer(*refs):
        inputs, sources = refs[:before], refs[before : before + count]
        outputs = refs[before + count : before + count + len(shapes)]
        buffers = refs[before + count + len(shapes) :]
        if count:
            sems = buffers[-1]
            copies = [
                pltpu.make_async_copy(source, buffer, sems.at[at])
                for at, (source, buffer) in enumerate(zip(sources, buffers[:-1]))
            ]
            for copy in copies:
                copy.start()
            for copy in copies:
                copy.wait()
        kernel(*inputs, *outputs, *buffers[:count])

    scratch = [pltpu.VMEM(array.shape, array.dtype) for array in fetched]
    if count:
        scratch.append(pltpu.SemaphoreType.DMA((count,)))
    return pl.pallas_call(
        outer,
        out_shape=[jax.ShapeDtypeStruct(shape, jnp.float32) for shape in shapes],
        in_specs=[pl.BlockSpec(memory_space=pltpu.SMEM)] * len(scalars)
        + [pl.BlockSpec(memory_space=pltpu.VMEM)] * len(arrays)
        + [pl.BlockSpec(memory_space=pltpu.HBM)] * count,
        out_specs=[pl.BlockSpec(memory_space=pltpu.VMEM)] * len(shapes),
        scratch_shapes=scratch,
        compiler_params=pltpu.CompilerParams(vmem_limit_bytes=24 * 2**20),
        cost_estimate=pl.CostEstimate(flops=flops, bytes_accessed=4 * 2**20, transcendentals=0),
    )(*scalars, *arrays, *fetched)


def select(array, position):
    return lax.dynamic_index_in_dim(array, position, 0, keepdims=False)


def body(
    inverse_root,
    inverse_upper,
    inverse_middle,
    inverse_lower,
    leaf_inverse,
    source_root,
    source_upper,
    source_middle,
    source_lower,
    leaf_source,
    update_root,
    update_upper,
    update_middle,
    leaf_update,
    slots_root,
    slots_upper,
    slots_middle,
    leaf_slots,
    basis_upper,
    basis_middle,
    basis_lower,
    leaf_basis,
    front_ranks,
    leaf_ranks,
):
    a, e, k, d = (lax.axis_index(name) for name in ("a", "e", "k", "d"))
    separator, width = source_root.shape[2:]
    rank = leaf_basis.shape[-1]
    spots = jnp.stack([a, e, k, d]).astype(jnp.int32)

    leaf_forward, packs = call(
        leaf_kernel,
        [leaf_source.shape[2:], (8, 128, width)],
        [leaf_ranks],
        [],
        10**9,
        [leaf_inverse, leaf_source, flipped(leaf_basis), flipped(leaf_update), leaf_slots],
    )
    shared = exchange(packs, ("c",))

    keep, send, lows = call(
        apply_kernel,
        [(16, 64, width), (16, 64, width), (4, rank, width)],
        [spots],
        [],
        4 * 10**9,
        [
            flipped(inverse_root),
            inverse_upper,
            flipped(inverse_middle),
            source_root,
            source_upper,
            source_middle,
            flipped(update_root),
            flipped(update_upper),
            flipped(update_middle),
            slots_root,
            slots_upper,
            slots_middle,
            flipped(basis_upper),
            flipped(basis_middle),
        ],
    )
    applied = (keep, partner(send, "k"))
    keep, send, rows = call(
        lower_kernel,
        [(16, 8, width), (16, 8, width), (rank, 8, width)],
        [spots],
        [shared, lows],
        10**9,
        [inverse_lower, source_lower, flipped(basis_lower)],
    )
    lower = (keep, partner(send, "k"))

    parts = exchange(rows, PLANE)
    (pieces,) = call(gather_kernel, [(16, 80, width)], [], [parts, *applied, *lower], 10**7)
    parts = exchange(pieces, CHIPS)
    pieces, sums, lower_slices = call(
        total_kernel, [(32, 24, width), (2, 64, width), (4, 8, width)], [], [parts], 10**7
    )
    gains = exchange(pieces, PLANE)

    wide, upper, rows = call(
        forward_kernel,
        [(2, 24, width), (2, 8, width), (rank, 8, width)],
        [spots, front_ranks],
        [gains, sums],
        10**8,
    )
    parts = exchange(rows, PLANE)
    (pieces,) = call(
        slices_kernel, [(16, 48, width)], [spots], [parts, wide, upper, lower_slices], 10**7
    )
    parts = exchange(pieces, CHIPS)
    mine, pieces = call(
        arrange_kernel, [(3 * separator, width), (32, 8, width)], [], [parts], 10**7
    )
    theirs = partner(mine, "k")
    low_rows = exchange(pieces, PLANE)

    (pieces,) = call(
        backward_kernel,
        [(8, 128, width)],
        [spots, front_ranks],
        [
            gains,
            low_rows,
            mine,
            theirs,
            flipped(inverse_root),
            inverse_upper,
            flipped(inverse_middle),
            inverse_lower,
            flipped(basis_upper),
            flipped(basis_middle),
            flipped(basis_lower),
            shared,
        ],
        3 * 10**9,
    )
    total = exchange(pieces, ("c",)).sum(axis=0)
    tops = total[:48].reshape(2, 24, width)
    tops = select(tops, d) + partner(select(tops, 1 - d), "d")
    (leaf_solution,) = call(
        last_kernel,
        [leaf_source.shape],
        [leaf_ranks],
        [total[96:], leaf_forward, leaf_inverse, flipped(leaf_basis)],
        10**9,
    )
    return (
        tops[None, None, :12],
        tops[None, None, 12:],
        total[None, None, 48:72],
        total[None, None, 72:96],
        leaf_solution,
    )


def solution(mesh):
    fine = Mesh(mesh.devices.reshape(2, 2, 4, 2, 2, 8), ROW + COL)
    tile = (ROW, COL)
    in_specs = (
        [P(*tile, None, None, None)] * 5
        + [P(ROW, None, None, None)] * 4
        + [P(*tile, None, None)]
        + [P(ROW, None, None, None, None, None)] * 3
        + [P(*tile, None, None, None)]
        + [P(ROW, None, None, None)] * 3
        + [P(*tile, None)]
        + [P(COL, None, None, None, None)] * 3
        + [P(*tile, None, None, None), P(), P(*tile)]
    )
    return jax.shard_map(
        body,
        mesh=fine,
        in_specs=tuple(in_specs),
        out_specs=(P(*tile, None, None),) * 5,
        check_vma=False,
    )
```

time: 252 us -> 206 us (0.82)
  blocking collectives: 10.5 us -> 107 us
  waiting for transfers between devices: 71.6 us -> 15.7 us
  starting transfers between devices: 71 us -> 35.8 us
  local copies, waits for them, and re-layouts: 51.4 us -> 17.3 us
  other arithmetic: 19.6 us -> 0.11 us
  Pallas kernels: 21 us -> 26.4 us
    all_to_all x1 -> x5, blocking collectives: 10.5 us -> 107 us  [exchange(): return lax.all_to_all(pieces, axes, 0, 0)]
    all_to_all x7 -> x3, waiting for transfers between devices: 71.4 us -> 14.4 us  [exchange(): return lax.all_to_all(pieces, axes, 0, 0)]
    all_to_all x7 -> x3, starting transfers between devices: 50 us -> 15.4 us  [exchange(): return lax.all_to_all(pieces, axes, 0, 0)]
    concatenate x6 -> x0, local copies, waits for them, and re-layouts: 19.2 us -> none  [the longest x4 19.1 us: body(): jnp.concatenate([wide_forward[to_a], upper_forward[to_a], lower_slices[to...]
    pallas_call x5 -> x10, Pallas kernels: 21 us -> 26.4 us  [call(): pl.pallas_call(outer, out_shape=[jax.ShapeDtypeStruct(shape, jnp.float32)...]
    unnamed x96 -> x70, local copies, waits for them, and re-layouts: 20 us -> 15.5 us
    reduce_sum x6 -> x0, other arithmetic: 4.25 us -> none  [the longest x2 1.54 us: body(): rows = exchange(rows, PLANE).reshape(2, 2, 8, 8, width).sum(axis=(0, 2))]
    slice x17 -> x0, local copies, waits for them, and re-layouts: 3.57 us -> none  [the longest x1 0.96 us: body(): got[:8, :24].reshape(separator, width)]
  transfers between devices with their start and end apart: 11 -> 7, of which waited for: 7 -> 4; matrix products, arithmetic and copies ran while one was open for 5% -> 0% of each run, Pallas kernels for 5% -> 7%
where the time goes in v4:
time: 206 us; the launch traced here: 204 us
  blocking collectives  107 us (52%)
  starting transfers between devices  35.8 us (17%)
  Pallas kernels  26.4 us (13%)
  local copies, waits for them, and re-layouts  17.3 us (8%)
  waiting for transfers between devices  15.7 us (8%)
    all_to_all x5, blocking collectives, exchange(): return lax.all_to_all(pieces, axes, 0, 0)  107 us
    pallas_call x10, Pallas kernels, call(): pl.pallas_call(outer, out_shape=[jax.ShapeDtypeStruct(shape, jnp.float32)...  26.4 us
    ppermute x4, starting transfers between devices, partner(): return lax.ppermute(values, axis, [(0, 1), (1, 0)])  20.4 us
    unnamed x70, local copies, waits for them, and re-layouts  15.5 us
    all_to_all x3, starting transfers between devices, exchange(): return lax.all_to_all(pieces, axes, 0, 0)  15.4 us
    all_to_all x3, waiting for transfers between devices, exchange(): return lax.all_to_all(pieces, axes, 0, 0)  14.4 us
  transfers between devices with their start and end apart: 7, of which 4 were waited for; matrix products, arithmetic and copies ran while one was open for 0% of the time, Pallas kernels for 7%

profile of v4, /device:TPU:1, one launch (start us, length us, event | category | flops | bytes accessed | tf_op | source)
XLA Modules:
  0.0 204.4 jit_solution(16840485873548698100)
XLA Ops:
  1.3 1.3 copy-done.1
  2.6 0.9 copy-done.11
  3.5 0.9 copy-done.21
  5.8 3.5 %shard_map.263 = (f32[384,128]{1,0:T(8,128)S(1)}, f32[8,128,128]{2,1,0:T(8,128)}) custom-call(s32[1,1]{1,0:T(1,128)S(6)} %copy.29.refs_0_, f32[1,1,2,384,384]{4,3,2,1,0:T(8,128)S(1)} %copy-done.1, f32[1,1,384,128]{3,2,1,0:T(8,128)S(1)} %copy-done.11, f32[1,1,2,32,384]{4,3,2,1,0:T(8,128)S(1)} %bitcast.34, f32[1,1,2,32,96]{4,3,2,1,0:T(8,128)S(1)} %bitcast.38, ...), custom_call_target="tpu_custom_call" | custom-call | flops 1000000000 | bytes 4194304 | tf_op jit(solution)/shard_map/pallas_call | solution.py:433
  10.1 5.9 %all-to-all-start = ((f32[8,128,128]{2,1,0:T(8,128)}), f32[8,128,128]{2,1,0:T(8,128)S(1)}, u32[]{:S(2)}, u32[]{:S(2)}) async-start(f32[8,128,128]{2,1,0:T(8,128)} %get-tuple-element.21), calls=%async_computation | async-start | bytes 1048576 | tf_op jit(solution)/shard_map/all_to_all | solution.py:17
  16.1 0.9 copy-done.16
  17.0 0.9 copy-done.17
  17.9 0.9 copy-done.19
  18.8 0.9 copy-done.20
  19.7 0.8 copy-done.23
  21.4 7.3 %shard_map.264 = (f32[16,64,128]{2,1,0:T(8,128)S(1)}, f32[16,64,128]{2,1,0:T(8,128)S(1)}, f32[4,32,128]{2,1,0:T(8,128)S(1)}) custom-call(s32[4]{0:T(128)S(1)} %pad_add_fusion.refs_0_, f32[1,1,2,192,384]{4,3,2,1,0:T(8,128)S(1)} %bitcast.23, f32[1,1,2,192,192]{4,3,2,1,0:T(8,128)S(1)} %copy-done.5, f32[1,1,2,192,384]{4,3,2,1,0:T(8,128)S(1)} %bitcast.25, ...), custom_call_target="tpu_custom_call" | custom-call | flops 4000000000 | bytes 4194304 | tf_op jit(solution)/shard_map/pallas_call | solution.py:433
  29.3 6.3 %collective-permute-start = (f32[16,64,128]{2,1,0:T(8,128)S(1)}, f32[16,64,128]{2,1,0:T(8,128)S(1)}, u32[]{:S(2)}, u32[]{:S(2)}) collective-permute-start(f32[16,64,128]{2,1,0:T(8,128)S(1)} %get-tuple-element.25), channel_id=1, source_target_pairs={{0,16},{16,0},{1,17},{17,1},{2,18},{18,2},{3,19},{19,3},{4,20},{20... | collective-permute-start | bytes 1572872 | tf_op jit(solution)/shard_map/ppermute | solution.py:21
  35.7 1.0 copy-done.7
  36.7 0.9 copy-done.9
  37.6 0.9 copy-done.13
  39.4 3.4 %shard_map.265 = (f32[16,8,128]{2,1,0:T(8,128)S(1)}, f32[16,8,128]{2,1,0:T(8,128)S(1)}, f32[32,8,128]{2,1,0:T(8,128)}) custom-call(s32[4]{0:T(128)S(1)} %pad_add_fusion.refs_0_, f32[8,128,128]{2,1,0:T(8,128)S(1)} %all-to-all-done.refs_1_.refs_13_, f32[4,32,128]{2,1,0:T(8,128)S(1)} %copy-done.34, f32[1,1,2,192,192]{4,3,2,1,0:T(8,128)S(1)} %copy-done.7, ...), custom_call_target="tpu_custom_call" | custom-call | flops 1000000000 | bytes 4194304 | tf_op jit(solution)/shard_map/pallas_call | solution.py:433
  43.5 5.9 %all-to-all-start.1 = ((f32[32,8,128]{2,1,0:T(8,128)}), f32[32,8,128]{2,1,0:T(8,128)S(1)}, u32[]{:S(2)}, u32[]{:S(2)}) async-start(f32[32,8,128]{2,1,0:T(8,128)} %get-tuple-element.23), calls=%async_computation.1 | async-start | bytes 262144 | tf_op jit(solution)/shard_map/all_to_all | solution.py:17
  49.4 2.1 %collective-permute-start.1 = (f32[16,8,128]{2,1,0:T(8,128)}, f32[16,8,128]{2,1,0:T(8,128)S(1)}, u32[]{:S(2)}, u32[]{:S(2)}) collective-permute-start(f32[16,8,128]{2,1,0:T(8,128)} %copy-done.25), channel_id=1, source_target_pairs={{0,16},{16,0},{1,17},{17,1},{2,18},{18,2},{3,19},{19,3},{4,20},{20... | collective-permute-start | bytes 196616 | tf_op jit(solution)/shard_map/ppermute | solution.py:21
  51.5 1.2 collective-permute-done.1.refs_4_
  52.7 4.2 %all-to-all-done.1.refs_0_ = f32[32,8,128]{2,1,0:T(8,128)S(1)} async-done(((f32[32,8,128]{2,1,0:T(8,128)}), f32[32,8,128]{2,1,0:T(8,128)S(1)}, u32[]{:S(2)}, u32[]{:S(2)}) %all-to-all-start.1) | async-done | bytes 131104 | tf_op jit(solution)/shard_map/all_to_all | solution.py:17
  57.0 46.6 %all_to_all.40.refs_0_ = f32[16,80,128]{2,1,0:T(8,128)S(1)} all-to-all(f32[16,80,128]{2,1,0:T(8,128)S(1)} %shard_map.266), channel_id=1, replica_groups=mesh['a'=2,'e'=2,'z'=4,'k'=2,'d'=2,'c'=8] {'a','e','z'}, dimensions={0} | all-to-all | bytes 1310720 | tf_op jit(solution)/shard_map/all_to_all | solution.py:17
  103.6 16.5 %all_to_all.41.refs_2_ = f32[32,24,128]{2,1,0:T(8,128)S(1)} all-to-all(f32[32,24,128]{2,1,0:T(8,128)S(1)} %get-tuple-element.28), channel_id=1, replica_groups=mesh['a'=2,'e'=2,'z'=4,'k'=2,'d'=2,'c'=8] {'k','d','c'}, dimensions={0} | all-to-all | bytes 786432 | tf_op jit(solution)/shard_map/all_to_all | solution.py:17
  120.1 2.7 %shard_map.268 = (f32[2,24,128]{2,1,0:T(8,128)S(1)}, f32[2,8,128]{2,1,0:T(8,128)S(1)}, f32[32,8,128]{2,1,0:T(8,128)S(1)}) custom-call(s32[4]{0:T(128)S(1)} %pad_add_fusion.refs_0_, s32[14]{0:T(128)S(1)} %copy-done, f32[32,24,128]{2,1,0:T(8,128)S(1)} %all_to_all.41.refs_2_, f32[2,64,128]{2,1,0:T(8,128)S(1)} %get-tuple-element.29.refs_3_), custom_call_target="tpu_custom_call" | custom-call | flops 100000000 | bytes 4194304 | tf_op jit(solution)/shard_map/pallas_call | solution.py:433
  122.9 11.8 %all_to_all.42.refs_1_ = f32[32,8,128]{2,1,0:T(8,128)S(1)} all-to-all(f32[32,8,128]{2,1,0:T(8,128)S(1)} %get-tuple-element.30), channel_id=1, replica_groups=mesh['a'=2,'e'=2,'z'=4,'k'=2,'d'=2,'c'=8] {'k','d','c'}, dimensions={0} | all-to-all | bytes 262144 | tf_op jit(solution)/shard_map/all_to_all | solution.py:17
  135.3 21.6 %all_to_all.43.refs_0_ = f32[16,48,128]{2,1,0:T(8,128)S(1)} all-to-all(f32[16,48,128]{2,1,0:T(8,128)S(1)} %shard_map.269), channel_id=1, replica_groups=mesh['a'=2,'e'=2,'z'=4,'k'=2,'d'=2,'c'=8] {'a','e','z'}, dimensions={0} | all-to-all | bytes 786432 | tf_op jit(solution)/shard_map/all_to_all | solution.py:17
  156.9 9.1 %collective-permute-start.2 = (f32[576,128]{1,0:T(8,128)S(1)}, f32[576,128]{1,0:T(8,128)S(1)}, u32[]{:S(2)}, u32[]{:S(2)}) collective-permute-start(f32[576,128]{1,0:T(8,128)S(1)} %get-tuple-element.35.refs_4_), channel_id=1, source_target_pairs={{0,16},{16,0},{1,17},{17,1},{2,18},{18,2},{3,19},{19,3},{4,20},{20... | collective-permute-start | bytes 884744 | tf_op jit(solution)/shard_map/ppermute | solution.py:21
  166.1 11.0 %all_to_all.44.refs_3_ = f32[32,8,128]{2,1,0:T(8,128)S(1)} all-to-all(f32[32,8,128]{2,1,0:T(8,128)S(1)} %get-tuple-element.34), channel_id=1, replica_groups=mesh['a'=2,'e'=2,'z'=4,'k'=2,'d'=2,'c'=8] {'k','d','c'}, dimensions={0} | all-to-all | bytes 262144 | tf_op jit(solution)/shard_map/all_to_all | solution.py:17
  177.1 5.7 %shard_map.271 = f32[8,128,128]{2,1,0:T(8,128)} custom-call(s32[4]{0:T(128)S(1)} %pad_add_fusion.refs_0_, s32[14]{0:T(128)S(1)} %copy-done, f32[32,24,128]{2,1,0:T(8,128)S(1)} %all_to_all.41.refs_2_, f32[32,8,128]{2,1,0:T(8,128)S(1)} %all_to_all.44.refs_3_, f32[576,128]{1,0:T(8,128)S(1)} %get-tuple-element.35.refs_4_, ...), custom_call_target="tpu_custom_call" | custom-call | flops 3000000000 | bytes 4194304 | tf_op jit(solution)/shard_map/pallas_call | solution.py:433
  182.8 3.6 %all-to-all-start.7 = ((f32[8,128,128]{2,1,0:T(8,128)}), f32[8,128,128]{2,1,0:T(8,128)S(1)}, u32[]{:S(2)}, u32[]{:S(2)}) async-start(f32[8,128,128]{2,1,0:T(8,128)} %shard_map.271), calls=%async_computation.7 | async-start | bytes 1048576 | tf_op jit(solution)/shard_map/all_to_all | solution.py:17
  186.4 10.2 %all-to-all-done.7 = f32[8,128,128]{2,1,0:T(8,128)S(1)} async-done(((f32[8,128,128]{2,1,0:T(8,128)}), f32[8,128,128]{2,1,0:T(8,128)S(1)}, u32[]{:S(2)}, u32[]{:S(2)}) %all-to-all-start.7) | async-done | bytes 524320 | tf_op jit(solution)/shard_map/all_to_all | solution.py:17
  197.3 2.8 %collective-permute-start.3 = (f32[24,128]{1,0:T(8,128)S(1)}, f32[24,128]{1,0:T(8,128)S(1)}, u32[]{:S(2)}, u32[]{:S(2)}) collective-permute-start(f32[24,128]{1,0:T(8,128)S(1)} %dynamic-slice_bitcast_fusion), channel_id=1, source_target_pairs={{0,8},{8,0},{1,9},{9,1},{2,10},{10,2},{3,11},{11,3},{4,12},{12,4},... | collective-permute-start | bytes 36872 | tf_op jit(solution)/shard_map/ppermute | solution.py:21
  200.1 3.0 %shard_map.272 = f32[1,1,384,128]{3,2,1,0:T(8,128)} custom-call(s32[1,1]{1,0:T(1,128)S(6)} %copy.29.refs_0_, f32[32,128]{1,0:T(8,128)S(1)} %slice.29.refs_1_, f32[384,128]{1,0:T(8,128)S(1)} %copy-done.32, f32[1,1,2,384,384]{4,3,2,1,0:T(8,128)S(1)} %copy-done.2, f32[1,1,2,32,384]{4,3,2,1,0:T(8,128)S(1)} %bitcast.35), custom_call_target="tpu_custom_call" | custom-call | flops 1000000000 | bytes 4194304 | tf_op jit(solution)/shard_map/pallas_call | solution.py:433
  (77 shorter events, 8.0 us)
Async XLA Ops:
  1.3 1.3 copy-start.1
  2.6 0.9 copy-start.11
  3.5 0.9 copy-start.21
  5.8 10.2 %copy-start.3 = (f32[1,1,2,384,192]{3,4,2,1,0:T(8,128)S(1)}, f32[1,1,2,384,192]{3,4,2,1,0:T(8,128)}, u32[]{:S(2)}) copy-start(f32[1,1,2,384,192]{3,4,2,1,0:T(8,128)} %param.24) | copy-start | bytes 1769476
  5.8 10.2 %copy-start.4 = (f32[1,1,2,384,192]{3,4,2,1,0:T(8,128)S(1)}, f32[1,1,2,384,192]{3,4,2,1,0:T(8,128)}, u32[]{:S(2)}) copy-start(f32[1,1,2,384,192]{3,4,2,1,0:T(8,128)} %param.26) | copy-start | bytes 1769476
  5.8 10.2 %copy-start.5 = (f32[1,1,2,192,192]{4,3,2,1,0:T(8,128)S(1)}, f32[1,1,2,192,192]{4,3,2,1,0:T(8,128)}, u32[]{:S(2)}) copy-start(f32[1,1,2,192,192]{4,3,2,1,0:T(8,128)} %refs_7_.1) | copy-start | bytes 884740
  5.8 10.2 %copy-start.12 = (f32[1,2,192,128]{3,2,1,0:T(8,128)S(1)}, f32[1,2,192,128]{3,2,1,0:T(8,128)}, u32[]{:S(2)}) copy-start(f32[1,2,192,128]{3,2,1,0:T(8,128)} %refs_6_.1) | copy-start | bytes 589828
  5.8 10.2 %copy-start.14 = (f32[1,2,2,384,32]{3,4,2,1,0:T(8,128)S(1)}, f32[1,2,2,384,32]{3,4,2,1,0:T(8,128)}, u32[]{:S(2)}) copy-start(f32[1,2,2,384,32]{3,4,2,1,0:T(8,128)} %param.43) | copy-start | bytes 589828
  5.8 10.2 %copy-start.27 = (s32[1,2,2,96]{3,2,1,0:T(2,128)S(1)}, s32[1,2,2,96]{3,2,1,0:T(2,128)}, u32[]{:S(2)}) copy-start(s32[1,2,2,96]{3,2,1,0:T(2,128)} %refs_12_.1) | copy-start | bytes 4612
  5.8 10.2 %copy-start.28 = (s32[1,1,2,96]{3,2,1,0:T(2,128)S(1)}, s32[1,1,2,96]{3,2,1,0:T(2,128)}, u32[]{:S(2)}) copy-start(s32[1,1,2,96]{3,2,1,0:T(2,128)} %refs_10_.1) | copy-start | bytes 2308
  5.8 10.2 %copy-start.29 = (s32[1,1,2,96]{3,2,1,0:T(2,128)S(1)}, s32[1,1,2,96]{3,2,1,0:T(2,128)}, u32[]{:S(2)}) copy-start(s32[1,1,2,96]{3,2,1,0:T(2,128)} %refs_11_.1) | copy-start | bytes 2308
  10.1 25.6 %all-to-all-start = ((f32[8,128,128]{2,1,0:T(8,128)}), f32[8,128,128]{2,1,0:T(8,128)S(1)}, u32[]{:S(2)}, u32[]{:S(2)}) async-start(f32[8,128,128]{2,1,0:T(8,128)} %get-tuple-element.21), calls=%async_computation | async-start | bytes 1048576 | tf_op jit(solution)/shard_map/all_to_all | solution.py:17
  16.1 0.9 copy-start.16
  17.0 0.9 copy-start.17
  29.3 23.4 %collective-permute-start = (f32[16,64,128]{2,1,0:T(8,128)S(1)}, f32[16,64,128]{2,1,0:T(8,128)S(1)}, u32[]{:S(2)}, u32[]{:S(2)}) collective-permute-start(f32[16,64,128]{2,1,0:T(8,128)S(1)} %get-tuple-element.25), channel_id=1, source_target_pairs={{0,16},{16,0},{1,17},{17,1},{2,18},{18,2},{3,19},{19,3},{4,20},{20... | collective-permute-start | bytes 1572872 | tf_op jit(solution)/shard_map/ppermute | solution.py:21
  35.7 1.0 copy-start.7
  36.7 0.9 copy-start.9
  37.6 0.9 copy-start.13
  43.5 13.4 %all-to-all-start.1 = ((f32[32,8,128]{2,1,0:T(8,128)}), f32[32,8,128]{2,1,0:T(8,128)S(1)}, u32[]{:S(2)}, u32[]{:S(2)}) async-start(f32[32,8,128]{2,1,0:T(8,128)} %get-tuple-element.23), calls=%async_computation.1 | async-start | bytes 262144 | tf_op jit(solution)/shard_map/all_to_all | solution.py:17
  49.4 3.4 %collective-permute-start.1 = (f32[16,8,128]{2,1,0:T(8,128)}, f32[16,8,128]{2,1,0:T(8,128)S(1)}, u32[]{:S(2)}, u32[]{:S(2)}) collective-permute-start(f32[16,8,128]{2,1,0:T(8,128)} %copy-done.25), channel_id=1, source_target_pairs={{0,16},{16,0},{1,17},{17,1},{2,18},{18,2},{3,19},{19,3},{4,20},{20... | collective-permute-start | bytes 196616 | tf_op jit(solution)/shard_map/ppermute | solution.py:21
  57.0 63.1 %copy-start = (s32[14]{0:T(128)S(1)}, s32[14]{0:T(128)}, u32[]{:S(2)}) copy-start(s32[14]{0:T(128)} %refs_1_.5) | copy-start | bytes 172
  122.8 54.2 %copy-start.6 = (f32[1,1,2,192,192]{4,3,2,1,0:T(8,128)S(1)}, f32[1,1,2,192,192]{4,3,2,1,0:T(8,128)}, u32[]{:S(2)}) copy-start(f32[1,1,2,192,192]{4,3,2,1,0:T(8,128)} %refs_7_.1) | copy-start | bytes 884740
  122.8 54.2 %copy-start.8 = (f32[1,1,2,192,192]{4,3,2,1,0:T(8,128)S(1)}, f32[1,1,2,192,192]{4,3,2,1,0:T(8,128)}, u32[]{:S(2)}) copy-start(f32[1,1,2,192,192]{4,3,2,1,0:T(8,128)} %refs_9_.1) | copy-start | bytes 884740
  122.9 54.2 %copy-start.10 = (f32[1,4,2,192,32]{3,4,2,1,0:T(8,128)S(1)}, f32[1,4,2,192,32]{3,4,2,1,0:T(8,128)}, u32[]{:S(2)}) copy-start(f32[1,4,2,192,32]{3,4,2,1,0:T(8,128)} %param.44) | copy-start | bytes 589828
  122.9 54.2 %copy-start.15 = (f32[1,2,2,384,32]{3,4,2,1,0:T(8,128)S(1)}, f32[1,2,2,384,32]{3,4,2,1,0:T(8,128)}, u32[]{:S(2)}) copy-start(f32[1,2,2,384,32]{3,4,2,1,0:T(8,128)} %param.43) | copy-start | bytes 589828
  122.9 54.2 %copy-start.18 = (f32[1,2,2,192,32]{3,4,2,1,0:T(8,128)S(1)}, f32[1,2,2,192,32]{3,4,2,1,0:T(8,128)}, u32[]{:S(2)}) copy-start(f32[1,2,2,192,32]{3,4,2,1,0:T(8,128)} %param.42) | copy-start | bytes 294916
  156.9 20.1 %collective-permute-start.2 = (f32[576,128]{1,0:T(8,128)S(1)}, f32[576,128]{1,0:T(8,128)S(1)}, u32[]{:S(2)}, u32[]{:S(2)}) collective-permute-start(f32[576,128]{1,0:T(8,128)S(1)} %get-tuple-element.35.refs_4_), channel_id=1, source_target_pairs={{0,16},{16,0},{1,17},{17,1},{2,18},{18,2},{3,19},{19,3},{4,20},{20... | collective-permute-start | bytes 884744 | tf_op jit(solution)/shard_map/ppermute | solution.py:21
  182.8 17.3 %copy-start.2 = (f32[1,1,2,384,384]{4,3,2,1,0:T(8,128)S(1)}, f32[1,1,2,384,384]{4,3,2,1,0:T(8,128)}, u32[]{:S(2)}) copy-start(f32[1,1,2,384,384]{4,3,2,1,0:T(8,128)} %refs_3_.3) | copy-start | bytes 3538948
  182.8 17.3 %copy-start.22 = (f32[1,1,2,384,32]{3,4,2,1,0:T(8,128)S(1)}, f32[1,1,2,384,32]{3,4,2,1,0:T(8,128)}, u32[]{:S(2)}) copy-start(f32[1,1,2,384,32]{3,4,2,1,0:T(8,128)} %param.45) | copy-start | bytes 294916
  182.8 17.3 %copy-start.32 = (f32[384,128]{1,0:T(8,128)S(1)}, f32[384,128]{1,0:T(8,128)}, u32[]{:S(2)}) copy-start(f32[384,128]{1,0:T(8,128)} %copy-done.31) | copy-start | bytes 589828
  182.8 13.8 %all-to-all-start.7 = ((f32[8,128,128]{2,1,0:T(8,128)}), f32[8,128,128]{2,1,0:T(8,128)S(1)}, u32[]{:S(2)}, u32[]{:S(2)}) async-start(f32[8,128,128]{2,1,0:T(8,128)} %shard_map.271), calls=%async_computation.7 | async-start | bytes 1048576 | tf_op jit(solution)/shard_map/all_to_all | solution.py:17
  197.3 5.9 %collective-permute-start.3 = (f32[24,128]{1,0:T(8,128)S(1)}, f32[24,128]{1,0:T(8,128)S(1)}, u32[]{:S(2)}, u32[]{:S(2)}) collective-permute-start(f32[24,128]{1,0:T(8,128)S(1)} %dynamic-slice_bitcast_fusion), channel_id=1, source_target_pairs={{0,8},{8,0},{1,9},{9,1},{2,10},{10,2},{3,11},{11,3},{4,12},{12,4},... | collective-permute-start | bytes 36872 | tf_op jit(solution)/shard_map/ppermute | solution.py:21
  (10 other events, 7.7 us)

commit v5 on v4

--- a/solution.py
+++ b/solution.py
@@ -28,14 +28,21 @@
     return jnp.concatenate(groups, axis=-1)
 
 
+def halves(values):
+    high = values.astype(jnp.bfloat16)
+    return high, (values - high.astype(jnp.float32)).astype(jnp.bfloat16)
+
+
 def dot(left, right, contract=1):
-    return lax.dot_general(
-        left,
-        right,
-        (((contract,), (0,)), ((), ())),
-        precision=precise,
-        preferred_element_type=jnp.float32,
-    )
+    left_high, left_low = halves(left)
+    right_high, right_low = halves(right)
+
+    def one(x, y):
+        return lax.dot_general(
+            x, y, (((contract,), (0,)), ((), ())), preferred_element_type=jnp.float32
+        )
+
+    return one(left_high, right_high) + (one(left_high, right_low) + one(left_low, right_high))
 
 
 def times(real, imag, vector):
@@ -438,7 +445,7 @@
         + [pl.BlockSpec(memory_space=pltpu.HBM)] * count,
         out_specs=[pl.BlockSpec(memory_space=pltpu.VMEM)] * len(shapes),
         scratch_shapes=scratch,
-        compiler_params=pltpu.CompilerParams(vmem_limit_bytes=24 * 2**20),
+        compiler_params=pltpu.CompilerParams(vmem_limit_bytes=(60 if count else 24) * 2**20),
         cost_estimate=pl.CostEstimate(flops=flops, bytes_accessed=4 * 2**20, transcendentals=0),
     )(*scalars, *arrays, *fetched)
 

time: 206 us -> 190 us (0.922)
  local copies, waits for them, and re-layouts: 17.3 us -> 3.53 us
  Pallas kernels: 26.4 us -> 22.8 us
    unnamed x70 -> x32, local copies, waits for them, and re-layouts: 15.5 us -> 1.71 us
    pallas_call x10, Pallas kernels: 26.4 us -> 22.8 us  [call(): pl.pallas_call(outer, out_shape=[jax.ShapeDtypeStruct(shape, jnp.float32)...]
where the time goes in v5:
time: 190 us; the launch traced here: 189 us
  blocking collectives  108 us (57%)
  starting transfers between devices  35.8 us (19%)
  Pallas kernels  22.8 us (12%)
  waiting for transfers between devices  16.8 us (9%)
  local copies, waits for them, and re-layouts  3.53 us (2%)
    all_to_all x5, blocking collectives, exchange(): return lax.all_to_all(pieces, axes, 0, 0)  108 us
    pallas_call x10, Pallas kernels, call(): pl.pallas_call(outer, out_shape=[jax.ShapeDtypeStruct(shape, jnp.float32)...  22.8 us
    ppermute x4, starting transfers between devices, partner(): return lax.ppermute(values, axis, [(0, 1), (1, 0)])  20.4 us
    all_to_all x3, starting transfers between devices, exchange(): return lax.all_to_all(pieces, axes, 0, 0)  15.4 us
    all_to_all x3, waiting for transfers between devices, exchange(): return lax.all_to_all(pieces, axes, 0, 0)  14.4 us
  transfers between devices with their start and end apart: 7, of which 4 were waited for; matrix products, arithmetic and copies ran while one was open for 0% of the time, Pallas kernels for 7%

profile of v5, /device:TPU:1, one launch (start us, length us, event | category | flops | bytes accessed | tf_op | source)
XLA Modules:
  0.0 188.8 jit_solution(327607330028728167)
XLA Ops:
  1.3 3.5 %shard_map.263 = (f32[384,128]{1,0:T(8,128)}, f32[8,128,128]{2,1,0:T(8,128)}) custom-call(s32[1,1]{1,0:T(1,128)S(6)} %copy.29.refs_0_, f32[1,1,2,384,384]{4,3,2,1,0:T(8,128)} %refs_3_.3, f32[1,1,384,128]{3,2,1,0:T(8,128)} %refs_2_.2, f32[1,1,2,32,384]{4,3,2,1,0:T(8,128)} %bitcast.33, f32[1,1,2,32,96]{4,3,2,1,0:T(8,128)} %bitcast.40, s32[1,1,96]{2,1,0:T(1,128)} %refs_5_.2), custom_call_target="tpu_custom_call" | custom-call | flops 1000000000 | bytes 4194304 | tf_op jit(solution)/shard_map/pallas_call | solution.py:440
  4.8 5.9 %all-to-all-start = ((f32[8,128,128]{2,1,0:T(8,128)}), f32[8,128,128]{2,1,0:T(8,128)S(1)}, u32[]{:S(2)}, u32[]{:S(2)}) async-start(f32[8,128,128]{2,1,0:T(8,128)} %get-tuple-element.21), calls=%async_computation | async-start | bytes 1048576 | tf_op jit(solution)/shard_map/all_to_all | solution.py:17
  10.7 0.7 pad_add_fusion.refs_0_
  11.3 6.3 %shard_map.264 = (f32[16,64,128]{2,1,0:T(8,128)}, f32[16,64,128]{2,1,0:T(8,128)}, f32[4,32,128]{2,1,0:T(8,128)}) custom-call(s32[4]{0:T(128)} %pad_add_fusion.refs_0_, f32[1,1,2,192,384]{4,3,2,1,0:T(8,128)} %bitcast.23, f32[1,1,2,192,192]{4,3,2,1,0:T(8,128)} %refs_7_.1, f32[1,1,2,192,384]{4,3,2,1,0:T(8,128)} %bitcast.25, f32[1,1,192,128]{3,2,1,0:T(8,128)} %refs_4_.2, ...), custom_call_target="tpu_custom_call" | custom-call | flops 4000000000 | bytes 4194304 | tf_op jit(solution)/shard_map/pallas_call | solution.py:440
  17.6 6.4 %collective-permute-start = (f32[16,64,128]{2,1,0:T(8,128)}, f32[16,64,128]{2,1,0:T(8,128)S(1)}, u32[]{:S(2)}, u32[]{:S(2)}) collective-permute-start(f32[16,64,128]{2,1,0:T(8,128)} %get-tuple-element.25), channel_id=1, source_target_pairs={{0,16},{16,0},{1,17},{17,1},{2,18},{18,2},{3,19},{19,3},{4,20},{20... | collective-permute-start | bytes 1572872 | tf_op jit(solution)/shard_map/ppermute | solution.py:21
  24.0 0.8 copy-done
  24.8 4.1 %shard_map.265 = (f32[16,8,128]{2,1,0:T(8,128)}, f32[16,8,128]{2,1,0:T(8,128)}, f32[32,8,128]{2,1,0:T(8,128)}) custom-call(s32[4]{0:T(128)} %pad_add_fusion.refs_0_, f32[8,128,128]{2,1,0:T(8,128)} %copy-done, f32[4,32,128]{2,1,0:T(8,128)} %get-tuple-element.22.refs_2_, f32[1,1,2,192,192]{4,3,2,1,0:T(8,128)} %refs_9_.1, f32[1,2,192,128]{3,2,1,0:T(8,128)} %refs_4_.3, ...), custom_call_target="tpu_custom_call" | custom-call | flops 1000000000 | bytes 4194304 | tf_op jit(solution)/shard_map/pallas_call | solution.py:440
  29.0 5.9 %all-to-all-start.1 = ((f32[32,8,128]{2,1,0:T(8,128)}), f32[32,8,128]{2,1,0:T(8,128)S(1)}, u32[]{:S(2)}, u32[]{:S(2)}) async-start(f32[32,8,128]{2,1,0:T(8,128)} %get-tuple-element.23), calls=%async_computation.1 | async-start | bytes 262144 | tf_op jit(solution)/shard_map/all_to_all | solution.py:17
  34.9 2.1 %collective-permute-start.1 = (f32[16,8,128]{2,1,0:T(8,128)}, f32[16,8,128]{2,1,0:T(8,128)S(1)}, u32[]{:S(2)}, u32[]{:S(2)}) collective-permute-start(f32[16,8,128]{2,1,0:T(8,128)} %get-tuple-element.27), channel_id=1, source_target_pairs={{0,16},{16,0},{1,17},{17,1},{2,18},{18,2},{3,19},{19,3},{4,20},{20... | collective-permute-start | bytes 196616 | tf_op jit(solution)/shard_map/ppermute | solution.py:21
  37.0 1.2 collective-permute-done.1.refs_4_
  38.3 4.2 %all-to-all-done.1.refs_0_ = f32[32,8,128]{2,1,0:T(8,128)S(1)} async-done(((f32[32,8,128]{2,1,0:T(8,128)}), f32[32,8,128]{2,1,0:T(8,128)S(1)}, u32[]{:S(2)}, u32[]{:S(2)}) %all-to-all-start.1) | async-done | bytes 131104 | tf_op jit(solution)/shard_map/all_to_all | solution.py:17
  42.4 0.8 copy-done.3
  43.3 0.1 shard_map.266
  43.3 0.0 copy-start.5
  43.4 46.6 %all_to_all.40.refs_0_ = f32[16,80,128]{2,1,0:T(8,128)S(1)} all-to-all(f32[16,80,128]{2,1,0:T(8,128)S(1)} %shard_map.266), channel_id=1, replica_groups=mesh['a'=2,'e'=2,'z'=4,'k'=2,'d'=2,'c'=8] {'a','e','z'}, dimensions={0} | all-to-all | bytes 1310720 | tf_op jit(solution)/shard_map/all_to_all | solution.py:17
  89.9 0.1 shard_map.267
  90.0 16.6 %all_to_all.41.refs_2_ = f32[32,24,128]{2,1,0:T(8,128)S(1)} all-to-all(f32[32,24,128]{2,1,0:T(8,128)S(1)} %get-tuple-element.28), channel_id=1, replica_groups=mesh['a'=2,'e'=2,'z'=4,'k'=2,'d'=2,'c'=8] {'k','d','c'}, dimensions={0} | all-to-all | bytes 786432 | tf_op jit(solution)/shard_map/all_to_all | solution.py:17
  106.6 2.5 %shard_map.268 = (f32[2,24,128]{2,1,0:T(8,128)S(1)}, f32[2,8,128]{2,1,0:T(8,128)S(1)}, f32[32,8,128]{2,1,0:T(8,128)S(1)}) custom-call(s32[4]{0:T(128)S(1)} %copy-done.4, s32[14]{0:T(128)S(1)} %copy-done.5, f32[32,24,128]{2,1,0:T(8,128)S(1)} %all_to_all.41.refs_2_, f32[2,64,128]{2,1,0:T(8,128)S(1)} %get-tuple-element.29.refs_3_), custom_call_target="tpu_custom_call" | custom-call | flops 100000000 | bytes 4194304 | tf_op jit(solution)/shard_map/pallas_call | solution.py:440
  109.2 11.8 %all_to_all.42.refs_1_ = f32[32,8,128]{2,1,0:T(8,128)S(1)} all-to-all(f32[32,8,128]{2,1,0:T(8,128)S(1)} %get-tuple-element.30), channel_id=1, replica_groups=mesh['a'=2,'e'=2,'z'=4,'k'=2,'d'=2,'c'=8] {'k','d','c'}, dimensions={0} | all-to-all | bytes 262144 | tf_op jit(solution)/shard_map/all_to_all | solution.py:17
  121.0 0.6 shard_map.269
  121.6 21.6 %all_to_all.43.refs_0_ = f32[16,48,128]{2,1,0:T(8,128)S(1)} all-to-all(f32[16,48,128]{2,1,0:T(8,128)S(1)} %shard_map.269), channel_id=1, replica_groups=mesh['a'=2,'e'=2,'z'=4,'k'=2,'d'=2,'c'=8] {'a','e','z'}, dimensions={0} | all-to-all | bytes 786432 | tf_op jit(solution)/shard_map/all_to_all | solution.py:17
  143.3 9.1 %collective-permute-start.2 = (f32[576,128]{1,0:T(8,128)S(1)}, f32[576,128]{1,0:T(8,128)S(1)}, u32[]{:S(2)}, u32[]{:S(2)}) collective-permute-start(f32[576,128]{1,0:T(8,128)S(1)} %get-tuple-element.35.refs_4_), channel_id=1, source_target_pairs={{0,16},{16,0},{1,17},{17,1},{2,18},{18,2},{3,19},{19,3},{4,20},{20... | collective-permute-start | bytes 884744 | tf_op jit(solution)/shard_map/ppermute | solution.py:21
  152.4 11.0 %all_to_all.44.refs_3_ = f32[32,8,128]{2,1,0:T(8,128)S(1)} all-to-all(f32[32,8,128]{2,1,0:T(8,128)S(1)} %get-tuple-element.34), channel_id=1, replica_groups=mesh['a'=2,'e'=2,'z'=4,'k'=2,'d'=2,'c'=8] {'k','d','c'}, dimensions={0} | all-to-all | bytes 262144 | tf_op jit(solution)/shard_map/all_to_all | solution.py:17
  163.4 3.7 %shard_map.271 = f32[8,128,128]{2,1,0:T(8,128)} custom-call(s32[4]{0:T(128)S(1)} %copy-done.4, s32[14]{0:T(128)S(1)} %copy-done.5, f32[32,24,128]{2,1,0:T(8,128)S(1)} %all_to_all.41.refs_2_, f32[32,8,128]{2,1,0:T(8,128)S(1)} %all_to_all.44.refs_3_, f32[576,128]{1,0:T(8,128)S(1)} %get-tuple-element.35.refs_4_, f32[576,128]{1,0:T(8,128)S(1)} %collective-permute-done.2.refs_5_, ...), custom_call_target="tpu_custom_call" | custom-call | flops 3000000000 | bytes 4194304 | tf_op jit(solution)/shard_map/pallas_call | solution.py:440
  167.1 3.6 %all-to-all-start.7 = ((f32[8,128,128]{2,1,0:T(8,128)}), f32[8,128,128]{2,1,0:T(8,128)S(1)}, u32[]{:S(2)}, u32[]{:S(2)}) async-start(f32[8,128,128]{2,1,0:T(8,128)} %shard_map.271), calls=%async_computation.7 | async-start | bytes 1048576 | tf_op jit(solution)/shard_map/all_to_all | solution.py:17
  170.8 10.2 %all-to-all-done.7 = f32[8,128,128]{2,1,0:T(8,128)S(1)} async-done(((f32[8,128,128]{2,1,0:T(8,128)}), f32[8,128,128]{2,1,0:T(8,128)S(1)}, u32[]{:S(2)}, u32[]{:S(2)}) %all-to-all-start.7) | async-done | bytes 524320 | tf_op jit(solution)/shard_map/all_to_all | solution.py:17
  181.0 0.6 slice_bitcast_fusion
  181.6 2.8 %collective-permute-start.3 = (f32[24,128]{1,0:T(8,128)S(1)}, f32[24,128]{1,0:T(8,128)S(1)}, u32[]{:S(2)}, u32[]{:S(2)}) collective-permute-start(f32[24,128]{1,0:T(8,128)S(1)} %dynamic-slice_bitcast_fusion), channel_id=1, source_target_pairs={{0,8},{8,0},{1,9},{9,1},{2,10},{10,2},{3,11},{11,3},{4,12},{12,4},... | collective-permute-start | bytes 36872 | tf_op jit(solution)/shard_map/ppermute | solution.py:21
  184.4 1.9 %shard_map.272 = f32[1,1,384,128]{3,2,1,0:T(8,128)} custom-call(s32[1,1]{1,0:T(1,128)S(6)} %copy.29.refs_0_, f32[32,128]{1,0:T(8,128)S(1)} %slice.29.refs_1_, f32[384,128]{1,0:T(8,128)S(1)} %copy-done.15, f32[1,1,2,384,384]{4,3,2,1,0:T(8,128)S(1)} %copy-done.6, f32[1,1,2,32,384]{4,3,2,1,0:T(8,128)S(1)} %bitcast.34), custom_call_target="tpu_custom_call" | custom-call | flops 1000000000 | bytes 4194304 | tf_op jit(solution)/shard_map/pallas_call | solution.py:440
  186.3 1.2 collective-permute-done.3
  187.6 0.6 broadcast_in_dim.12
  188.2 0.6 broadcast_in_dim.13
  (39 shorter events, 0.2 us)
Async XLA Ops:
  4.8 19.2 %all-to-all-start = ((f32[8,128,128]{2,1,0:T(8,128)}), f32[8,128,128]{2,1,0:T(8,128)S(1)}, u32[]{:S(2)}, u32[]{:S(2)}) async-start(f32[8,128,128]{2,1,0:T(8,128)} %get-tuple-element.21), calls=%async_computation | async-start | bytes 1048576 | tf_op jit(solution)/shard_map/all_to_all | solution.py:17
  17.6 20.6 %collective-permute-start = (f32[16,64,128]{2,1,0:T(8,128)}, f32[16,64,128]{2,1,0:T(8,128)S(1)}, u32[]{:S(2)}, u32[]{:S(2)}) collective-permute-start(f32[16,64,128]{2,1,0:T(8,128)} %get-tuple-element.25), channel_id=1, source_target_pairs={{0,16},{16,0},{1,17},{17,1},{2,18},{18,2},{3,19},{19,3},{4,20},{20... | collective-permute-start | bytes 1572872 | tf_op jit(solution)/shard_map/ppermute | solution.py:21
  24.0 0.8 copy-start
  24.8 17.6 %copy-start.2 = (f32[16,64,128]{2,1,0:T(8,128)S(1)}, f32[16,64,128]{2,1,0:T(8,128)}, u32[]{:S(2)}) copy-start(f32[16,64,128]{2,1,0:T(8,128)} %get-tuple-element.24.refs_1_) | copy-start | bytes 1572868
  29.0 13.4 %all-to-all-start.1 = ((f32[32,8,128]{2,1,0:T(8,128)}), f32[32,8,128]{2,1,0:T(8,128)S(1)}, u32[]{:S(2)}, u32[]{:S(2)}) async-start(f32[32,8,128]{2,1,0:T(8,128)} %get-tuple-element.23), calls=%async_computation.1 | async-start | bytes 262144 | tf_op jit(solution)/shard_map/all_to_all | solution.py:17
  34.9 3.4 %collective-permute-start.1 = (f32[16,8,128]{2,1,0:T(8,128)}, f32[16,8,128]{2,1,0:T(8,128)S(1)}, u32[]{:S(2)}, u32[]{:S(2)}) collective-permute-start(f32[16,8,128]{2,1,0:T(8,128)} %get-tuple-element.27), channel_id=1, source_target_pairs={{0,16},{16,0},{1,17},{17,1},{2,18},{18,2},{3,19},{19,3},{4,20},{20... | collective-permute-start | bytes 196616 | tf_op jit(solution)/shard_map/ppermute | solution.py:21
  42.4 0.8 copy-start.3
  43.3 63.3 %copy-start.4 = (s32[4]{0:T(128)S(1)}, s32[4]{0:T(128)}, u32[]{:S(2)}) copy-start(s32[4]{0:T(128)} %pad_add_fusion.refs_0_) | copy-start | bytes 52
  43.3 63.3 %copy-start.5 = (s32[14]{0:T(128)S(1)}, s32[14]{0:T(128)}, u32[]{:S(2)}) copy-start(s32[14]{0:T(128)} %refs_1_.5) | copy-start | bytes 172
  90.0 73.4 %copy-start.11 = (f32[1,4,2,192,32]{3,4,2,1,0:T(8,128)S(1)}, f32[1,4,2,192,32]{3,4,2,1,0:T(8,128)}, u32[]{:S(2)}) copy-start(f32[1,4,2,192,32]{3,4,2,1,0:T(8,128)} %param.44) | copy-start | bytes 589828
  90.0 73.4 %copy-start.13 = (f32[1,2,2,192,32]{3,4,2,1,0:T(8,128)S(1)}, f32[1,2,2,192,32]{3,4,2,1,0:T(8,128)}, u32[]{:S(2)}) copy-start(f32[1,2,2,192,32]{3,4,2,1,0:T(8,128)} %param.42) | copy-start | bytes 294916
  106.6 56.8 %copy-start.10 = (f32[1,1,2,192,192]{4,3,2,1,0:T(8,128)S(1)}, f32[1,1,2,192,192]{4,3,2,1,0:T(8,128)}, u32[]{:S(2)}) copy-start(f32[1,1,2,192,192]{4,3,2,1,0:T(8,128)} %refs_9_.1) | copy-start | bytes 884740
  106.6 56.8 %copy-start.12 = (f32[1,2,2,384,32]{3,4,2,1,0:T(8,128)S(1)}, f32[1,2,2,384,32]{3,4,2,1,0:T(8,128)}, u32[]{:S(2)}) copy-start(f32[1,2,2,384,32]{3,4,2,1,0:T(8,128)} %param.43) | copy-start | bytes 589828
  109.2 54.2 %copy-start.1 = (f32[8,128,128]{2,1,0:T(8,128)S(1)}, f32[8,128,128]{2,1,0:T(8,128)}, u32[]{:S(2)}) copy-start(f32[8,128,128]{2,1,0:T(8,128)} %copy-done) | copy-start | bytes 1572868
  109.2 54.2 %copy-start.7 = (f32[1,1,2,384,192]{3,4,2,1,0:T(8,128)S(1)}, f32[1,1,2,384,192]{3,4,2,1,0:T(8,128)}, u32[]{:S(2)}) copy-start(f32[1,1,2,384,192]{3,4,2,1,0:T(8,128)} %param.24) | copy-start | bytes 1769476
  109.2 54.2 %copy-start.8 = (f32[1,1,2,384,192]{3,4,2,1,0:T(8,128)S(1)}, f32[1,1,2,384,192]{3,4,2,1,0:T(8,128)}, u32[]{:S(2)}) copy-start(f32[1,1,2,384,192]{3,4,2,1,0:T(8,128)} %param.26) | copy-start | bytes 1769476
  109.2 54.2 %copy-start.9 = (f32[1,1,2,192,192]{4,3,2,1,0:T(8,128)S(1)}, f32[1,1,2,192,192]{4,3,2,1,0:T(8,128)}, u32[]{:S(2)}) copy-start(f32[1,1,2,192,192]{4,3,2,1,0:T(8,128)} %refs_7_.1) | copy-start | bytes 884740
  143.3 20.1 %collective-permute-start.2 = (f32[576,128]{1,0:T(8,128)S(1)}, f32[576,128]{1,0:T(8,128)S(1)}, u32[]{:S(2)}, u32[]{:S(2)}) collective-permute-start(f32[576,128]{1,0:T(8,128)S(1)} %get-tuple-element.35.refs_4_), channel_id=1, source_target_pairs={{0,16},{16,0},{1,17},{17,1},{2,18},{18,2},{3,19},{19,3},{4,20},{20... | collective-permute-start | bytes 884744 | tf_op jit(solution)/shard_map/ppermute | solution.py:21
  167.1 17.3 %copy-start.6 = (f32[1,1,2,384,384]{4,3,2,1,0:T(8,128)S(1)}, f32[1,1,2,384,384]{4,3,2,1,0:T(8,128)}, u32[]{:S(2)}) copy-start(f32[1,1,2,384,384]{4,3,2,1,0:T(8,128)} %refs_3_.3) | copy-start | bytes 3538948
  167.1 17.3 %copy-start.14 = (f32[1,1,2,384,32]{3,4,2,1,0:T(8,128)S(1)}, f32[1,1,2,384,32]{3,4,2,1,0:T(8,128)}, u32[]{:S(2)}) copy-start(f32[1,1,2,384,32]{3,4,2,1,0:T(8,128)} %param.45) | copy-start | bytes 294916
  167.1 17.3 %copy-start.15 = (f32[384,128]{1,0:T(8,128)S(1)}, f32[384,128]{1,0:T(8,128)}, u32[]{:S(2)}) copy-start(f32[384,128]{1,0:T(8,128)} %get-tuple-element.36.refs_2_) | copy-start | bytes 589828
  167.1 13.8 %all-to-all-start.7 = ((f32[8,128,128]{2,1,0:T(8,128)}), f32[8,128,128]{2,1,0:T(8,128)S(1)}, u32[]{:S(2)}, u32[]{:S(2)}) async-start(f32[8,128,128]{2,1,0:T(8,128)} %shard_map.271), calls=%async_computation.7 | async-start | bytes 1048576 | tf_op jit(solution)/shard_map/all_to_all | solution.py:17
  181.6 5.9 %collective-permute-start.3 = (f32[24,128]{1,0:T(8,128)S(1)}, f32[24,128]{1,0:T(8,128)S(1)}, u32[]{:S(2)}, u32[]{:S(2)}) collective-permute-start(f32[24,128]{1,0:T(8,128)S(1)} %dynamic-slice_bitcast_fusion), channel_id=1, source_target_pairs={{0,8},{8,0},{1,9},{9,1},{2,10},{10,2},{3,11},{11,3},{4,12},{12,4},... | collective-permute-start | bytes 36872 | tf_op jit(solution)/shard_map/ppermute | solution.py:21

commit v6 on v5

--- a/solution.py
+++ b/solution.py
@@ -56,6 +56,13 @@
 def cut(values, limit):
     rows = lax.broadcasted_iota(jnp.int32, values.shape, 0)
     return jnp.where(rows < limit, values, jnp.zeros_like(values))
+
+
+def put_thin(target, row, part):
+    nothing = jnp.zeros((2, 128), jnp.float32)
+    for chip in range(16):
+        slot = jnp.concatenate([part[6 * chip : 6 * chip + 6], nothing], axis=0)
+        target[chip, row : row + 8] = slot
 
 
 def leaf_kernel(ranks, forward, packs, inverse, source, basis, update, slots):
@@ -150,8 +157,7 @@
             rows = results[1].shape[0] // 2
             part = results[1][half * rows : (half + 1) * rows, side * 128 : side * 128 + 128]
             row = 48 + 8 * side
-            target[0:12, row : row + 8] = part.reshape(12, 8, 128)
-            target[12:16, row : row + 8] = jnp.zeros((4, 8, 128), jnp.float32)
+            put_thin(target, row, part)
 
     for half in range(2):
 
@@ -161,7 +167,7 @@
             put(send, 1 - half)
 
 
-def lower_kernel(spots, shared, lows, keep, send, rows, inverse, source, basis):
+def lower_kernel(spots, keep, send, rows, shared, lows, inverse, source, basis):
     a, e, k, d = spots[0], spots[1], spots[2], spots[3]
     low = shared[:, 0:32].reshape(256, 128)
     low_turned = turned(low)
@@ -182,8 +188,7 @@
     count = partial.shape[0] // 2
 
     def put(target, half):
-        target[0:12] = partial[half * count : (half + 1) * count].reshape(12, 8, 128)
-        target[12:16] = jnp.zeros((4, 8, 128), jnp.float32)
+        put_thin(target, 0, partial[half * count : (half + 1) * count])
 
     for half in range(2):
 
@@ -374,31 +379,29 @@
                     jnp.where(a == 0, joined[to_a : to_a + 1], sums[0][row : row + 1]),
                     jnp.where(a == 0, nothing, sums[1][row : row + 1]),
                     joined[4 + 2 * to_a : 6 + 2 * to_a],
-                    jnp.zeros((4, 128), jnp.float32),
                 ],
                 axis=0,
             )
+            tile = jnp.concatenate([upper[to_a][0:6], lower[row][0:6], tile], axis=0)
             for chip in range(4):
                 place = 8 * to_a + 4 * to_e + chip
                 pieces[place, 0:24] = wide[to_a]
-                pieces[place, 24:32] = upper[to_a]
-                pieces[place, 32:40] = lower[row]
-                pieces[place, 40:48] = tile
+                pieces[place, 24:40] = tile
 
 
 def arrange_kernel(parts, mine, pieces):
     for chip in range(8):
         mine[24 * chip : 24 * chip + 24] = parts[chip, 0:24]
         mine[192 + 24 * chip : 216 + 24 * chip] = parts[8 + chip, 0:24]
-    for chip in range(12):
-        mine[384 + 8 * chip : 392 + 8 * chip] = parts[chip, 24:32]
-        mine[480 + 8 * chip : 488 + 8 * chip] = parts[chip, 32:40]
+    tails = [parts[chip, 24:40] for chip in range(16)]
+    mine[384:480] = jnp.concatenate([tail[0:6] for tail in tails], axis=0)
+    mine[480:576] = jnp.concatenate([tail[6:12] for tail in tails], axis=0)
     sums = []
     for place in range(2):
-        total = parts[8 * place, 40:48]
+        total = tails[8 * place]
         for chip in range(1, 8):
-            total += parts[8 * place + chip, 40:48]
-        sums.append(total)
+            total += tails[8 * place + chip]
+        sums.append(total[12:16])
     upper = sums[0] + sums[1]
     tail = jnp.zeros((5, 128), jnp.float32)
     for to_d in range(2):
@@ -416,9 +419,13 @@
 
 def call(kernel, shapes, scalars, arrays, flops, fetched=()):
     count = len(fetched)
+    places = len(scalars[0]) if isinstance(scalars[0:1] and scalars[0], tuple) else 0
     before = len(scalars) + len(arrays)
+    scalars = [*scalars[0], *scalars[1:]] if places else scalars
 
     def outer(*refs):
+        if places:
+            refs = (tuple(ref[0] for ref in refs[:places]),) + refs[places:]
         inputs, sources = refs[:before], refs[before : before + count]
         outputs = refs[before + count : before + count + len(shapes)]
         buffers = refs[before + count + len(shapes) :]
@@ -483,7 +490,7 @@
     a, e, k, d = (lax.axis_index(name) for name in ("a", "e", "k", "d"))
     separator, width = source_root.shape[2:]
     rank = leaf_basis.shape[-1]
-    spots = jnp.stack([a, e, k, d]).astype(jnp.int32)
+    spots = tuple(axis.astype(jnp.int32).reshape(1) for axis in (a, e, k, d))
 
     leaf_forward, packs = call(
         leaf_kernel,
@@ -523,9 +530,9 @@
         lower_kernel,
         [(16, 8, width), (16, 8, width), (rank, 8, width)],
         [spots],
-        [shared, lows],
+        [],
         10**9,
-        [inverse_lower, source_lower, flipped(basis_lower)],
+        [shared, lows, inverse_lower, source_lower, flipped(basis_lower)],
     )
     lower = (keep, partner(send, "k"))
 
@@ -546,7 +553,7 @@
     )
     parts = exchange(rows, PLANE)
     (pieces,) = call(
-        slices_kernel, [(16, 48, width)], [spots], [parts, wide, upper, lower_slices], 10**7
+        slices_kernel, [(16, 40, width)], [spots], [parts, wide, upper, lower_slices], 10**7
     )
     parts = exchange(pieces, CHIPS)
     mine, pieces = call(

time: 190 us -> 184 us (0.968)
  blocking collectives: 108 us -> 105 us
  Pallas kernels: 22.8 us -> 20.7 us
    all_to_all x5, blocking collectives: 108 us -> 105 us  [exchange(): return lax.all_to_all(pieces, axes, 0, 0)]
    pallas_call x10, Pallas kernels: 22.8 us -> 20.7 us  [call(): pl.pallas_call(outer, out_shape=[jax.ShapeDtypeStruct(shape, jnp.float32)...]
  transfers between devices with their start and end apart: 7 -> 7, of which waited for: 4 -> 4; matrix products, arithmetic and copies ran while one was open for 0% -> 0% of each run, Pallas kernels for 7% -> 6%
where the time goes in v6:
time: 184 us; the launch traced here: 183 us
  blocking collectives  105 us (57%)
  starting transfers between devices  35.4 us (19%)
  Pallas kernels  20.7 us (11%)
  waiting for transfers between devices  16.8 us (9%)
  local copies, waits for them, and re-layouts  3.54 us (2%)
    all_to_all x5, blocking collectives, exchange(): return lax.all_to_all(pieces, axes, 0, 0)  105 us
    pallas_call x10, Pallas kernels, call(): pl.pallas_call(outer, out_shape=[jax.ShapeDtypeStruct(shape, jnp.float32)...  20.7 us
    ppermute x4, starting transfers between devices, partner(): return lax.ppermute(values, axis, [(0, 1), (1, 0)])  20 us
    all_to_all x3, starting transfers between devices, exchange(): return lax.all_to_all(pieces, axes, 0, 0)  15.4 us
    all_to_all x3, waiting for transfers between devices, exchange(): return lax.all_to_all(pieces, axes, 0, 0)  14.4 us
  transfers between devices with their start and end apart: 7, of which 4 were waited for; matrix products, arithmetic and copies ran while one was open for 0% of the time, Pallas kernels for 6%

profile of v6, /device:TPU:1, one launch (start us, length us, event | category | flops | bytes accessed | tf_op | source)
XLA Modules:
  0.0 182.9 jit_solution(6654360519967943741)
XLA Ops:
  1.3 3.5 %shard_map.263 = (f32[384,128]{1,0:T(8,128)}, f32[8,128,128]{2,1,0:T(8,128)}) custom-call(s32[1,1]{1,0:T(1,128)S(6)} %copy.29.refs_0_, f32[1,1,2,384,384]{4,3,2,1,0:T(8,128)} %refs_3_.1, f32[1,1,384,128]{3,2,1,0:T(8,128)} %refs_2_.1, f32[1,1,2,32,384]{4,3,2,1,0:T(8,128)} %bitcast.33, f32[1,1,2,32,96]{4,3,2,1,0:T(8,128)} %bitcast.40, s32[1,1,96]{2,1,0:T(1,128)} %refs_5_.2), custom_call_target="tpu_custom_call" | custom-call | flops 1000000000 | bytes 4194304 | tf_op jit(solution)/shard_map/pallas_call | solution.py:447
  4.8 5.9 %all-to-all-start = ((f32[8,128,128]{2,1,0:T(8,128)}), f32[8,128,128]{2,1,0:T(8,128)S(1)}, u32[]{:S(2)}, u32[]{:S(2)}) async-start(f32[8,128,128]{2,1,0:T(8,128)} %get-tuple-element.21), calls=%async_computation | async-start | bytes 1048576 | tf_op jit(solution)/shard_map/all_to_all | solution.py:17
  10.7 5.6 %shard_map.264 = (f32[16,64,128]{2,1,0:T(8,128)}, f32[16,64,128]{2,1,0:T(8,128)}, f32[4,32,128]{2,1,0:T(8,128)}) custom-call(s32[1]{0:T(128)} %bitcast.refs_0_, s32[1]{0:T(128)} %bitcast.1.refs_1_, s32[1]{0:T(128)} %bitcast.2.refs_2_, s32[1]{0:T(128)} %bitcast.3.refs_3_, f32[1,1,2,192,384]{4,3,2,1,0:T(8,128)} %bitcast.23, f32[1,1,2,192,192]{4,3,2,1,0:T(8,128)} %refs_10_.1, ...), custom_call_target="tpu_custom_call" | custom-call | flops 4000000000 | bytes 4194304 | tf_op jit(solution)/shard_map/pallas_call | solution.py:447
  16.3 6.4 %collective-permute-start = (f32[16,64,128]{2,1,0:T(8,128)}, f32[16,64,128]{2,1,0:T(8,128)S(1)}, u32[]{:S(2)}, u32[]{:S(2)}) collective-permute-start(f32[16,64,128]{2,1,0:T(8,128)} %get-tuple-element.25), channel_id=1, source_target_pairs={{0,16},{16,0},{1,17},{17,1},{2,18},{18,2},{3,19},{19,3},{4,20},{20... | collective-permute-start | bytes 1572872 | tf_op jit(solution)/shard_map/ppermute | solution.py:21
  22.7 0.8 copy-done
  23.5 3.2 %shard_map.265 = (f32[16,8,128]{2,1,0:T(8,128)}, f32[16,8,128]{2,1,0:T(8,128)}, f32[32,8,128]{2,1,0:T(8,128)}) custom-call(s32[1]{0:T(128)} %bitcast.refs_0_, s32[1]{0:T(128)} %bitcast.1.refs_1_, s32[1]{0:T(128)} %bitcast.2.refs_2_, s32[1]{0:T(128)} %bitcast.3.refs_3_, f32[8,128,128]{2,1,0:T(8,128)} %copy-done, f32[4,32,128]{2,1,0:T(8,128)} %get-tuple-element.22.refs_5_, ...), custom_call_target="tpu_custom_call" | custom-call | flops 1000000000 | bytes 4194304 | tf_op jit(solution)/shard_map/pallas_call | solution.py:447
  26.8 5.9 %all-to-all-start.1 = ((f32[32,8,128]{2,1,0:T(8,128)}), f32[32,8,128]{2,1,0:T(8,128)S(1)}, u32[]{:S(2)}, u32[]{:S(2)}) async-start(f32[32,8,128]{2,1,0:T(8,128)} %get-tuple-element.23), calls=%async_computation.1 | async-start | bytes 262144 | tf_op jit(solution)/shard_map/all_to_all | solution.py:17
  32.7 2.1 %collective-permute-start.1 = (f32[16,8,128]{2,1,0:T(8,128)}, f32[16,8,128]{2,1,0:T(8,128)S(1)}, u32[]{:S(2)}, u32[]{:S(2)}) collective-permute-start(f32[16,8,128]{2,1,0:T(8,128)} %get-tuple-element.27), channel_id=1, source_target_pairs={{0,16},{16,0},{1,17},{17,1},{2,18},{18,2},{3,19},{19,3},{4,20},{20... | collective-permute-start | bytes 196616 | tf_op jit(solution)/shard_map/ppermute | solution.py:21
  34.8 1.2 collective-permute-done.1.refs_4_
  36.0 4.2 %all-to-all-done.1.refs_0_ = f32[32,8,128]{2,1,0:T(8,128)S(1)} async-done(((f32[32,8,128]{2,1,0:T(8,128)}), f32[32,8,128]{2,1,0:T(8,128)S(1)}, u32[]{:S(2)}, u32[]{:S(2)}) %all-to-all-start.1) | async-done | bytes 131104 | tf_op jit(solution)/shard_map/all_to_all | solution.py:17
  40.2 0.8 copy-done.3
  41.1 0.1 shard_map.266
  41.1 46.6 %all_to_all.40.refs_0_ = f32[16,80,128]{2,1,0:T(8,128)S(1)} all-to-all(f32[16,80,128]{2,1,0:T(8,128)S(1)} %shard_map.266), channel_id=1, replica_groups=mesh['a'=2,'e'=2,'z'=4,'k'=2,'d'=2,'c'=8] {'a','e','z'}, dimensions={0} | all-to-all | bytes 1310720 | tf_op jit(solution)/shard_map/all_to_all | solution.py:17
  87.7 0.1 shard_map.267
  87.8 0.0 copy-start.12
  87.8 16.6 %all_to_all.41.refs_5_ = f32[32,24,128]{2,1,0:T(8,128)S(1)} all-to-all(f32[32,24,128]{2,1,0:T(8,128)S(1)} %get-tuple-element.28), channel_id=1, replica_groups=mesh['a'=2,'e'=2,'z'=4,'k'=2,'d'=2,'c'=8] {'k','d','c'}, dimensions={0} | all-to-all | bytes 786432 | tf_op jit(solution)/shard_map/all_to_all | solution.py:17
  104.4 0.0 copy-start.7
  104.4 0.0 copy-start.8
  104.4 2.5 %shard_map.268 = (f32[2,24,128]{2,1,0:T(8,128)S(1)}, f32[2,8,128]{2,1,0:T(8,128)S(1)}, f32[32,8,128]{2,1,0:T(8,128)S(1)}) custom-call(s32[1]{0:T(128)} %bitcast.refs_0_, s32[1]{0:T(128)} %bitcast.1.refs_1_, s32[1]{0:T(128)} %bitcast.2.refs_2_, s32[1]{0:T(128)} %bitcast.3.refs_3_, s32[14]{0:T(128)S(1)} %copy-done.4, f32[32,24,128]{2,1,0:T(8,128)S(1)} %all_to_all.41.refs_5_, ...), custom_call_target="tpu_custom_call" | custom-call | flops 100000000 | bytes 4194304 | tf_op jit(solution)/shard_map/pallas_call | solution.py:447
  107.0 11.7 %all_to_all.42.refs_4_ = f32[32,8,128]{2,1,0:T(8,128)S(1)} all-to-all(f32[32,8,128]{2,1,0:T(8,128)S(1)} %get-tuple-element.30), channel_id=1, replica_groups=mesh['a'=2,'e'=2,'z'=4,'k'=2,'d'=2,'c'=8] {'k','d','c'}, dimensions={0} | all-to-all | bytes 262144 | tf_op jit(solution)/shard_map/all_to_all | solution.py:17
  118.7 19.1 %all_to_all.43.refs_0_ = f32[16,40,128]{2,1,0:T(8,128)S(1)} all-to-all(f32[16,40,128]{2,1,0:T(8,128)S(1)} %shard_map.269), channel_id=1, replica_groups=mesh['a'=2,'e'=2,'z'=4,'k'=2,'d'=2,'c'=8] {'a','e','z'}, dimensions={0} | all-to-all | bytes 655360 | tf_op jit(solution)/shard_map/all_to_all | solution.py:17
  137.8 8.7 %collective-permute-start.2 = (f32[576,128]{1,0:T(8,128)S(1)}, f32[576,128]{1,0:T(8,128)S(1)}, u32[]{:S(2)}, u32[]{:S(2)}) collective-permute-start(f32[576,128]{1,0:T(8,128)S(1)} %get-tuple-element.35.refs_7_), channel_id=1, source_target_pairs={{0,16},{16,0},{1,17},{17,1},{2,18},{18,2},{3,19},{19,3},{4,20},{20... | collective-permute-start | bytes 884744 | tf_op jit(solution)/shard_map/ppermute | solution.py:21
  146.5 11.0 %all_to_all.44.refs_6_ = f32[32,8,128]{2,1,0:T(8,128)S(1)} all-to-all(f32[32,8,128]{2,1,0:T(8,128)S(1)} %get-tuple-element.34), channel_id=1, replica_groups=mesh['a'=2,'e'=2,'z'=4,'k'=2,'d'=2,'c'=8] {'k','d','c'}, dimensions={0} | all-to-all | bytes 262144 | tf_op jit(solution)/shard_map/all_to_all | solution.py:17
  157.6 3.7 %shard_map.271 = f32[8,128,128]{2,1,0:T(8,128)} custom-call(s32[1]{0:T(128)} %bitcast.refs_0_, s32[1]{0:T(128)} %bitcast.1.refs_1_, s32[1]{0:T(128)} %bitcast.2.refs_2_, s32[1]{0:T(128)} %bitcast.3.refs_3_, s32[14]{0:T(128)S(1)} %copy-done.4, f32[32,24,128]{2,1,0:T(8,128)S(1)} %all_to_all.41.refs_5_, f32[32,8,128]{2,1,0:T(8,128)S(1)} %all_to_all.44.refs_6_, ...), custom_call_target="tpu_custom_call" | custom-call | flops 3000000000 | bytes 4194304 | tf_op jit(solution)/shard_map/pallas_call | solution.py:447
  161.3 3.6 %all-to-all-start.7 = ((f32[8,128,128]{2,1,0:T(8,128)}), f32[8,128,128]{2,1,0:T(8,128)S(1)}, u32[]{:S(2)}, u32[]{:S(2)}) async-start(f32[8,128,128]{2,1,0:T(8,128)} %shard_map.271), calls=%async_computation.7 | async-start | bytes 1048576 | tf_op jit(solution)/shard_map/all_to_all | solution.py:17
  164.9 10.2 %all-to-all-done.7 = f32[8,128,128]{2,1,0:T(8,128)S(1)} async-done(((f32[8,128,128]{2,1,0:T(8,128)}), f32[8,128,128]{2,1,0:T(8,128)S(1)}, u32[]{:S(2)}, u32[]{:S(2)}) %all-to-all-start.7) | async-done | bytes 524320 | tf_op jit(solution)/shard_map/all_to_all | solution.py:17
  175.2 0.6 slice_bitcast_fusion
  175.8 2.8 %collective-permute-start.3 = (f32[24,128]{1,0:T(8,128)S(1)}, f32[24,128]{1,0:T(8,128)S(1)}, u32[]{:S(2)}, u32[]{:S(2)}) collective-permute-start(f32[24,128]{1,0:T(8,128)S(1)} %dynamic-slice_bitcast_fusion), channel_id=1, source_target_pairs={{0,8},{8,0},{1,9},{9,1},{2,10},{10,2},{3,11},{11,3},{4,12},{12,4},... | collective-permute-start | bytes 36872 | tf_op jit(solution)/shard_map/ppermute | solution.py:21
  178.6 1.9 %shard_map.272 = f32[1,1,384,128]{3,2,1,0:T(8,128)} custom-call(s32[1,1]{1,0:T(1,128)S(6)} %copy.29.refs_0_, f32[32,128]{1,0:T(8,128)S(1)} %slice.29.refs_1_, f32[384,128]{1,0:T(8,128)S(1)} %copy-done.14, f32[1,1,2,384,384]{4,3,2,1,0:T(8,128)S(1)} %copy-done.5, f32[1,1,2,32,384]{4,3,2,1,0:T(8,128)S(1)} %bitcast.34), custom_call_target="tpu_custom_call" | custom-call | flops 1000000000 | bytes 4194304 | tf_op jit(solution)/shard_map/pallas_call | solution.py:447
  180.5 1.2 collective-permute-done.3
  181.7 0.6 broadcast_in_dim.12
  182.3 0.6 broadcast_in_dim.13
  (36 shorter events, 0.2 us)
Async XLA Ops:
  4.8 17.9 %all-to-all-start = ((f32[8,128,128]{2,1,0:T(8,128)}), f32[8,128,128]{2,1,0:T(8,128)S(1)}, u32[]{:S(2)}, u32[]{:S(2)}) async-start(f32[8,128,128]{2,1,0:T(8,128)} %get-tuple-element.21), calls=%async_computation | async-start | bytes 1048576 | tf_op jit(solution)/shard_map/all_to_all | solution.py:17
  16.3 19.7 %collective-permute-start = (f32[16,64,128]{2,1,0:T(8,128)}, f32[16,64,128]{2,1,0:T(8,128)S(1)}, u32[]{:S(2)}, u32[]{:S(2)}) collective-permute-start(f32[16,64,128]{2,1,0:T(8,128)} %get-tuple-element.25), channel_id=1, source_target_pairs={{0,16},{16,0},{1,17},{17,1},{2,18},{18,2},{3,19},{19,3},{4,20},{20... | collective-permute-start | bytes 1572872 | tf_op jit(solution)/shard_map/ppermute | solution.py:21
  22.7 0.8 copy-start
  23.5 16.7 %copy-start.2 = (f32[16,64,128]{2,1,0:T(8,128)S(1)}, f32[16,64,128]{2,1,0:T(8,128)}, u32[]{:S(2)}) copy-start(f32[16,64,128]{2,1,0:T(8,128)} %get-tuple-element.24.refs_1_) | copy-start | bytes 1572868
  26.8 13.4 %all-to-all-start.1 = ((f32[32,8,128]{2,1,0:T(8,128)}), f32[32,8,128]{2,1,0:T(8,128)S(1)}, u32[]{:S(2)}, u32[]{:S(2)}) async-start(f32[32,8,128]{2,1,0:T(8,128)} %get-tuple-element.23), calls=%async_computation.1 | async-start | bytes 262144 | tf_op jit(solution)/shard_map/all_to_all | solution.py:17
  32.7 3.4 %collective-permute-start.1 = (f32[16,8,128]{2,1,0:T(8,128)}, f32[16,8,128]{2,1,0:T(8,128)S(1)}, u32[]{:S(2)}, u32[]{:S(2)}) collective-permute-start(f32[16,8,128]{2,1,0:T(8,128)} %get-tuple-element.27), channel_id=1, source_target_pairs={{0,16},{16,0},{1,17},{17,1},{2,18},{18,2},{3,19},{19,3},{4,20},{20... | collective-permute-start | bytes 196616 | tf_op jit(solution)/shard_map/ppermute | solution.py:21
  40.2 0.8 copy-start.3
  41.1 63.3 %copy-start.4 = (s32[14]{0:T(128)S(1)}, s32[14]{0:T(128)}, u32[]{:S(2)}) copy-start(s32[14]{0:T(128)} %refs_4_.3) | copy-start | bytes 172
  87.8 69.8 %copy-start.10 = (f32[1,4,2,192,32]{3,4,2,1,0:T(8,128)S(1)}, f32[1,4,2,192,32]{3,4,2,1,0:T(8,128)}, u32[]{:S(2)}) copy-start(f32[1,4,2,192,32]{3,4,2,1,0:T(8,128)} %param.44) | copy-start | bytes 589828
  87.8 69.8 %copy-start.11 = (f32[1,2,2,384,32]{3,4,2,1,0:T(8,128)S(1)}, f32[1,2,2,384,32]{3,4,2,1,0:T(8,128)}, u32[]{:S(2)}) copy-start(f32[1,2,2,384,32]{3,4,2,1,0:T(8,128)} %param.43) | copy-start | bytes 589828
  87.8 69.8 %copy-start.12 = (f32[1,2,2,192,32]{3,4,2,1,0:T(8,128)S(1)}, f32[1,2,2,192,32]{3,4,2,1,0:T(8,128)}, u32[]{:S(2)}) copy-start(f32[1,2,2,192,32]{3,4,2,1,0:T(8,128)} %param.42) | copy-start | bytes 294916
  104.4 53.2 %copy-start.9 = (f32[1,1,2,192,192]{4,3,2,1,0:T(8,128)S(1)}, f32[1,1,2,192,192]{4,3,2,1,0:T(8,128)}, u32[]{:S(2)}) copy-start(f32[1,1,2,192,192]{4,3,2,1,0:T(8,128)} %refs_12_.1) | copy-start | bytes 884740
  104.4 53.2 %copy-start.1 = (f32[8,128,128]{2,1,0:T(8,128)S(1)}, f32[8,128,128]{2,1,0:T(8,128)}, u32[]{:S(2)}) copy-start(f32[8,128,128]{2,1,0:T(8,128)} %copy-done) | copy-start | bytes 1572868
  104.4 53.2 %copy-start.6 = (f32[1,1,2,384,192]{3,4,2,1,0:T(8,128)S(1)}, f32[1,1,2,384,192]{3,4,2,1,0:T(8,128)}, u32[]{:S(2)}) copy-start(f32[1,1,2,384,192]{3,4,2,1,0:T(8,128)} %param.24) | copy-start | bytes 1769476
  104.4 53.2 %copy-start.7 = (f32[1,1,2,384,192]{3,4,2,1,0:T(8,128)S(1)}, f32[1,1,2,384,192]{3,4,2,1,0:T(8,128)}, u32[]{:S(2)}) copy-start(f32[1,1,2,384,192]{3,4,2,1,0:T(8,128)} %param.26) | copy-start | bytes 1769476
  104.4 53.2 %copy-start.8 = (f32[1,1,2,192,192]{4,3,2,1,0:T(8,128)S(1)}, f32[1,1,2,192,192]{4,3,2,1,0:T(8,128)}, u32[]{:S(2)}) copy-start(f32[1,1,2,192,192]{4,3,2,1,0:T(8,128)} %refs_10_.1) | copy-start | bytes 884740
  137.8 19.7 %collective-permute-start.2 = (f32[576,128]{1,0:T(8,128)S(1)}, f32[576,128]{1,0:T(8,128)S(1)}, u32[]{:S(2)}, u32[]{:S(2)}) collective-permute-start(f32[576,128]{1,0:T(8,128)S(1)} %get-tuple-element.35.refs_7_), channel_id=1, source_target_pairs={{0,16},{16,0},{1,17},{17,1},{2,18},{18,2},{3,19},{19,3},{4,20},{20... | collective-permute-start | bytes 884744 | tf_op jit(solution)/shard_map/ppermute | solution.py:21
  161.3 17.3 %copy-start.5 = (f32[1,1,2,384,384]{4,3,2,1,0:T(8,128)S(1)}, f32[1,1,2,384,384]{4,3,2,1,0:T(8,128)}, u32[]{:S(2)}) copy-start(f32[1,1,2,384,384]{4,3,2,1,0:T(8,128)} %refs_3_.1) | copy-start | bytes 3538948
  161.3 17.3 %copy-start.13 = (f32[1,1,2,384,32]{3,4,2,1,0:T(8,128)S(1)}, f32[1,1,2,384,32]{3,4,2,1,0:T(8,128)}, u32[]{:S(2)}) copy-start(f32[1,1,2,384,32]{3,4,2,1,0:T(8,128)} %param.45) | copy-start | bytes 294916
  161.3 17.3 %copy-start.14 = (f32[384,128]{1,0:T(8,128)S(1)}, f32[384,128]{1,0:T(8,128)}, u32[]{:S(2)}) copy-start(f32[384,128]{1,0:T(8,128)} %get-tuple-element.36.refs_2_) | copy-start | bytes 589828
  161.3 13.8 %all-to-all-start.7 = ((f32[8,128,128]{2,1,0:T(8,128)}), f32[8,128,128]{2,1,0:T(8,128)S(1)}, u32[]{:S(2)}, u32[]{:S(2)}) async-start(f32[8,128,128]{2,1,0:T(8,128)} %shard_map.271), calls=%async_computation.7 | async-start | bytes 1048576 | tf_op jit(solution)/shard_map/all_to_all | solution.py:17
  175.8 5.9 %collective-permute-start.3 = (f32[24,128]{1,0:T(8,128)S(1)}, f32[24,128]{1,0:T(8,128)S(1)}, u32[]{:S(2)}, u32[]{:S(2)}) collective-permute-start(f32[24,128]{1,0:T(8,128)S(1)} %dynamic-slice_bitcast_fusion), channel_id=1, source_target_pairs={{0,8},{8,0},{1,9},{9,1},{2,10},{10,2},{3,11},{11,3},{4,12},{12,4},... | collective-permute-start | bytes 36872 | tf_op jit(solution)/shard_map/ppermute | solution.py:21

commit v7 on v6

--- a/solution.py
+++ b/solution.py
@@ -202,6 +202,7 @@
     spots,
     ranks,
     gains,
+    belows,
     lows,
     mine,
     theirs,
@@ -227,9 +228,14 @@
         jnp.where(d == 0, gains[:, 12, :], gains[:, 13, :]),
         jnp.where(d == 0, gains[:, 14, :], gains[:, 15, :]),
     )
-    back1 = cut(lows[:, 0, :], ranks[a])
-    back2 = cut(lows[:, 1, :] - gain_back(gain1, back1, d), ranks[2 + 2 * a + d])
-    back3 = cut(lows[:, 2, :] - gain_back(gain2, back2, e), ranks[6 + 4 * a + 2 * e + d])
+
+    def upward(level):
+        square = lows[:, 2 * level + 1, :]
+        return lows[:, 2 * level, :] - times(square[:, :64], square[:, 64:], belows[level])
+
+    back1 = cut(upward(0), ranks[a])
+    back2 = cut(upward(1) - gain_back(gain1, back1, d), ranks[2 + 2 * a + d])
+    back3 = cut(upward(2) - gain_back(gain2, back2, e), ranks[6 + 4 * a + 2 * e + d])
 
     def whole(start, stop):
         left, right = mine[start:stop], theirs[start:stop]
@@ -293,7 +299,8 @@
         pieces[chip, 16:80] = applied_keep[chip] + applied_got[chip]
 
 
-def total_kernel(parts, pieces, sums, lower):
+def total_kernel(spots, parts, pieces, sums, lower):
+    a = spots[0]
     tiles = []
     for at in range(4):
         total = parts[4 * at]
@@ -312,10 +319,23 @@
     rows += [jnp.zeros((4, 128), jnp.float32)]
     tile = jnp.concatenate(rows, axis=0)
     for place in range(32):
-        pieces[place] = tile
-
-
-def forward_kernel(spots, ranks, gains, sums, wide_out, upper_out, rows):
+        pieces[place, 0:24] = tile
+    everything = upper[0][16:64] + upper[1][16:64]
+    for x in range(2):
+        wide = jnp.where(a == 0, everything, upper[x][16:64])
+        thin = upper[x][64:80]
+        for at, slices in ((24, wide), (32, thin)):
+            count = slices.shape[0] // 2
+            gain = slices[count:]
+            both = jnp.concatenate([slices[:count], gain], axis=-1)
+            low = times_back(gain[:, :64], gain[:, 64:], both)
+            for child in range(2):
+                row = at + 4 * x + 2 * child
+                pieces[:, row, :] = low[32 * child : 32 * child + 32, :128]
+                pieces[:, row + 1, :] = low[32 * child : 32 * child + 32, 128:]
+
+
+def forward_kernel(spots, ranks, gains, sums, lower, pieces, belows):
     a, d = spots[0], spots[3]
     coeffs3 = [cut(gains[:, at, :], ranks[6 + at]) for at in range(8)]
     pairs3 = [
@@ -342,58 +362,57 @@
         [chain(gains[:, 16 + x, :], gains[:, 18 + x, :], pairs2[x], ranks[x]) for x in range(2)],
         axis=0,
     )
+    belows[0] = pair1
+    belows[1] = jnp.where(a == 0, pairs2[0], pairs2[1])
+    belows[2] = jnp.where(
+        a == 0,
+        jnp.where(d == 0, pairs3[0][0], pairs3[0][1]),
+        jnp.where(d == 0, pairs3[1][0], pairs3[1][1]),
+    )
     everything = sums[0, 0:48] + sums[1, 0:48]
+    wide, upper = [], []
     for x in range(2):
         below = jnp.where(a == 0, pair1, jnp.where(d == 0, pairs3[x][0], pairs3[x][1]))
         slices = jnp.where(a == 0, everything, sums[x, 0:48])
         gain = slices[24:48]
-        result = slices[0:24] - times(gain[:, :64], gain[:, 64:], below)
-        wide_out[x] = result
-        low = times_back(gain[:, :64], gain[:, 64:], result)
-        rows[:, 2 * x, :] = low[:32]
-        rows[:, 2 * x + 1, :] = low[32:]
+        wide.append(slices[0:24] - times(gain[:, :64], gain[:, 64:], below))
         gain = sums[x, 56:64]
-        result = sums[x, 48:56] - times(gain[:, :64], gain[:, 64:], pairs2[x])
-        upper_out[x] = result
-        low = times_back(gain[:, :64], gain[:, 64:], result)
-        rows[:, 4 + 2 * x, :] = low[:32]
-        rows[:, 5 + 2 * x, :] = low[32:]
-
-
-def slices_kernel(spots, parts, wide, upper, lower, pieces):
-    a = spots[0]
-    sums = []
+        upper.append(sums[x, 48:56] - times(gain[:, :64], gain[:, 64:], pairs2[x]))
+    totals = []
     for place in range(2):
-        total = jnp.zeros((8, 128), jnp.float32)
+        total = jnp.zeros((16, 128), jnp.float32)
         for core in range(2):
             for at in range(8):
-                total += parts[16 * core + 8 * place + at]
-        sums.append(total)
-    joined = sums[0] + sums[1]
-    nothing = jnp.zeros((1, 128), jnp.float32)
+                total += gains[16 * core + 8 * place + at, 24:40]
+        totals.append(total)
+    joined = totals[0] + totals[1]
+    nothing = jnp.zeros((2, 128), jnp.float32)
+    tail = jnp.zeros((4, 128), jnp.float32)
     for to_a in range(2):
         for to_e in range(2):
-            row = 2 * to_a + to_e
+            row = 4 * to_a + 2 * to_e
             tile = jnp.concatenate(
                 [
-                    jnp.where(a == 0, joined[to_a : to_a + 1], sums[0][row : row + 1]),
-                    jnp.where(a == 0, nothing, sums[1][row : row + 1]),
-                    joined[4 + 2 * to_a : 6 + 2 * to_a],
+                    upper[to_a][0:6],
+                    lower[2 * to_a + to_e][0:6],
+                    jnp.where(a == 0, joined[2 * to_a : 2 * to_a + 2], totals[0][row : row + 2]),
+                    jnp.where(a == 0, nothing, totals[1][row : row + 2]),
+                    joined[8 + 4 * to_a : 12 + 4 * to_a],
+                    tail,
                 ],
                 axis=0,
             )
-            tile = jnp.concatenate([upper[to_a][0:6], lower[row][0:6], tile], axis=0)
             for chip in range(4):
                 place = 8 * to_a + 4 * to_e + chip
                 pieces[place, 0:24] = wide[to_a]
-                pieces[place, 24:40] = tile
+                pieces[place, 24:48] = tile
 
 
 def arrange_kernel(parts, mine, pieces):
     for chip in range(8):
         mine[24 * chip : 24 * chip + 24] = parts[chip, 0:24]
         mine[192 + 24 * chip : 216 + 24 * chip] = parts[8 + chip, 0:24]
-    tails = [parts[chip, 24:40] for chip in range(16)]
+    tails = [parts[chip, 24:48] for chip in range(16)]
     mine[384:480] = jnp.concatenate([tail[0:6] for tail in tails], axis=0)
     mine[480:576] = jnp.concatenate([tail[6:12] for tail in tails], axis=0)
     sums = []
@@ -401,12 +420,13 @@
         total = tails[8 * place]
         for chip in range(1, 8):
             total += tails[8 * place + chip]
-        sums.append(total[12:16])
+        sums.append(total[12:20])
     upper = sums[0] + sums[1]
-    tail = jnp.zeros((5, 128), jnp.float32)
+    tail = jnp.zeros((2, 128), jnp.float32)
     for to_d in range(2):
+        row = 2 * to_d
         tile = jnp.concatenate(
-            [sums[0][0:1], upper[2 + to_d : 3 + to_d], sums[1][to_d : to_d + 1], tail], axis=0
+            [sums[0][0:2], upper[4 + row : 6 + row], sums[1][row : row + 2], tail], axis=0
         )
         for core in range(2):
             for to_c in range(8):
@@ -540,20 +560,16 @@
     (pieces,) = call(gather_kernel, [(16, 80, width)], [], [parts, *applied, *lower], 10**7)
     parts = exchange(pieces, CHIPS)
     pieces, sums, lower_slices = call(
-        total_kernel, [(32, 24, width), (2, 64, width), (4, 8, width)], [], [parts], 10**7
+        total_kernel, [(32, 40, width), (2, 64, width), (4, 8, width)], [spots], [parts], 10**7
     )
     gains = exchange(pieces, PLANE)
 
-    wide, upper, rows = call(
+    pieces, belows = call(
         forward_kernel,
-        [(2, 24, width), (2, 8, width), (rank, 8, width)],
+        [(16, 48, width), (3, 2 * rank, width)],
         [spots, front_ranks],
-        [gains, sums],
+        [gains, sums, lower_slices],
         10**8,
-    )
-    parts = exchange(rows, PLANE)
-    (pieces,) = call(
-        slices_kernel, [(16, 40, width)], [spots], [parts, wide, upper, lower_slices], 10**7
     )
     parts = exchange(pieces, CHIPS)
     mine, pieces = call(
@@ -568,6 +584,7 @@
         [spots, front_ranks],
         [
             gains,
+            belows,
             low_rows,
             mine,
             theirs,

time: 184 us -> 179 us (0.973)
  blocking collectives: 105 us -> 99.7 us
    all_to_all x5 -> x4, blocking collectives: 105 us -> 99.7 us  [exchange(): return lax.all_to_all(pieces, axes, 0, 0)]
    pallas_call x10 -> x9, Pallas kernels: 20.7 us -> 20.4 us  [call(): pl.pallas_call(outer, out_shape=[jax.ShapeDtypeStruct(shape, jnp.float32)...]
where the time goes in v7:
time: 179 us; the launch traced here: 178 us
  blocking collectives  99.7 us (56%)
  starting transfers between devices  36 us (20%)
  Pallas kernels  20.4 us (11%)
  waiting for transfers between devices  16.8 us (9%)
  local copies, waits for them, and re-layouts  3.54 us (2%)
    all_to_all x4, blocking collectives, exchange(): return lax.all_to_all(pieces, axes, 0, 0)  99.7 us
    ppermute x4, starting transfers between devices, partner(): return lax.ppermute(values, axis, [(0, 1), (1, 0)])  20.6 us
    pallas_call x9, Pallas kernels, call(): pl.pallas_call(outer, out_shape=[jax.ShapeDtypeStruct(shape, jnp.float32)...  20.4 us
    all_to_all x3, starting transfers between devices, exchange(): return lax.all_to_all(pieces, axes, 0, 0)  15.4 us
    all_to_all x3, waiting for transfers between devices, exchange(): return lax.all_to_all(pieces, axes, 0, 0)  14.4 us
  transfers between devices with their start and end apart: 7, of which 4 were waited for; matrix products, arithmetic and copies ran while one was open for 0% of the time, Pallas kernels for 6%

profile of v7, /device:TPU:1, one launch (start us, length us, event | category | flops | bytes accessed | tf_op | source)
XLA Modules:
  0.0 178.0 jit_solution(13679596467385280102)
XLA Ops:
  1.3 3.5 %shard_map.263 = (f32[384,128]{1,0:T(8,128)}, f32[8,128,128]{2,1,0:T(8,128)}) custom-call(s32[1,1]{1,0:T(1,128)S(6)} %copy.29.refs_0_, f32[1,1,2,384,384]{4,3,2,1,0:T(8,128)} %refs_3_.1, f32[1,1,384,128]{3,2,1,0:T(8,128)} %refs_2_.1, f32[1,1,2,32,384]{4,3,2,1,0:T(8,128)} %bitcast.33, f32[1,1,2,32,96]{4,3,2,1,0:T(8,128)} %bitcast.40, s32[1,1,96]{2,1,0:T(1,128)} %refs_5_.2), custom_call_target="tpu_custom_call" | custom-call | flops 1000000000 | bytes 4194304 | tf_op jit(solution)/shard_map/pallas_call | solution.py:467
  4.8 5.9 %all-to-all-start = ((f32[8,128,128]{2,1,0:T(8,128)}), f32[8,128,128]{2,1,0:T(8,128)S(1)}, u32[]{:S(2)}, u32[]{:S(2)}) async-start(f32[8,128,128]{2,1,0:T(8,128)} %get-tuple-element.20), calls=%async_computation | async-start | bytes 1048576 | tf_op jit(solution)/shard_map/all_to_all | solution.py:17
  10.7 5.6 %shard_map.264 = (f32[16,64,128]{2,1,0:T(8,128)}, f32[16,64,128]{2,1,0:T(8,128)}, f32[4,32,128]{2,1,0:T(8,128)}) custom-call(s32[1]{0:T(128)} %bitcast.refs_0_, s32[1]{0:T(128)} %bitcast.1.refs_1_, s32[1]{0:T(128)} %bitcast.2.refs_2_, s32[1]{0:T(128)} %bitcast.3.refs_3_, f32[1,1,2,192,384]{4,3,2,1,0:T(8,128)} %bitcast.23, f32[1,1,2,192,192]{4,3,2,1,0:T(8,128)} %refs_11_.1, ...), custom_call_target="tpu_custom_call" | custom-call | flops 4000000000 | bytes 4194304 | tf_op jit(solution)/shard_map/pallas_call | solution.py:467
  16.3 6.4 %collective-permute-start = (f32[16,64,128]{2,1,0:T(8,128)}, f32[16,64,128]{2,1,0:T(8,128)S(1)}, u32[]{:S(2)}, u32[]{:S(2)}) collective-permute-start(f32[16,64,128]{2,1,0:T(8,128)} %get-tuple-element.24), channel_id=1, source_target_pairs={{0,16},{16,0},{1,17},{17,1},{2,18},{18,2},{3,19},{19,3},{4,20},{20... | collective-permute-start | bytes 1572872 | tf_op jit(solution)/shard_map/ppermute | solution.py:21
  22.7 0.8 copy-done
  23.5 3.2 %shard_map.265 = (f32[16,8,128]{2,1,0:T(8,128)}, f32[16,8,128]{2,1,0:T(8,128)}, f32[32,8,128]{2,1,0:T(8,128)}) custom-call(s32[1]{0:T(128)} %bitcast.refs_0_, s32[1]{0:T(128)} %bitcast.1.refs_1_, s32[1]{0:T(128)} %bitcast.2.refs_2_, s32[1]{0:T(128)} %bitcast.3.refs_3_, f32[8,128,128]{2,1,0:T(8,128)} %copy-done, f32[4,32,128]{2,1,0:T(8,128)} %get-tuple-element.21.refs_5_, ...), custom_call_target="tpu_custom_call" | custom-call | flops 1000000000 | bytes 4194304 | tf_op jit(solution)/shard_map/pallas_call | solution.py:467
  26.8 5.9 %all-to-all-start.1 = ((f32[32,8,128]{2,1,0:T(8,128)}), f32[32,8,128]{2,1,0:T(8,128)S(1)}, u32[]{:S(2)}, u32[]{:S(2)}) async-start(f32[32,8,128]{2,1,0:T(8,128)} %get-tuple-element.22), calls=%async_computation.1 | async-start | bytes 262144 | tf_op jit(solution)/shard_map/all_to_all | solution.py:17
  32.7 2.1 %collective-permute-start.1 = (f32[16,8,128]{2,1,0:T(8,128)}, f32[16,8,128]{2,1,0:T(8,128)S(1)}, u32[]{:S(2)}, u32[]{:S(2)}) collective-permute-start(f32[16,8,128]{2,1,0:T(8,128)} %get-tuple-element.26), channel_id=1, source_target_pairs={{0,16},{16,0},{1,17},{17,1},{2,18},{18,2},{3,19},{19,3},{4,20},{20... | collective-permute-start | bytes 196616 | tf_op jit(solution)/shard_map/ppermute | solution.py:21
  34.8 1.2 collective-permute-done.1.refs_4_
  36.0 4.2 %all-to-all-done.1.refs_0_ = f32[32,8,128]{2,1,0:T(8,128)S(1)} async-done(((f32[32,8,128]{2,1,0:T(8,128)}), f32[32,8,128]{2,1,0:T(8,128)S(1)}, u32[]{:S(2)}, u32[]{:S(2)}) %all-to-all-start.1) | async-done | bytes 131104 | tf_op jit(solution)/shard_map/all_to_all | solution.py:17
  40.2 0.8 copy-done.3
  41.1 0.1 shard_map.266
  41.1 46.6 %all_to_all.35.refs_4_ = f32[16,80,128]{2,1,0:T(8,128)S(1)} all-to-all(f32[16,80,128]{2,1,0:T(8,128)S(1)} %shard_map.266), channel_id=1, replica_groups=mesh['a'=2,'e'=2,'z'=4,'k'=2,'d'=2,'c'=8] {'a','e','z'}, dimensions={0} | all-to-all | bytes 1310720 | tf_op jit(solution)/shard_map/all_to_all | solution.py:17
  87.7 0.5 shard_map.267
  88.2 0.0 copy-start.9
  88.2 0.0 copy-start.10
  88.3 0.0 copy-start.11
  88.3 0.0 copy-start.12
  88.3 19.4 %all_to_all.36.refs_5_ = f32[32,40,128]{2,1,0:T(8,128)S(1)} all-to-all(f32[32,40,128]{2,1,0:T(8,128)S(1)} %get-tuple-element.27), channel_id=1, replica_groups=mesh['a'=2,'e'=2,'z'=4,'k'=2,'d'=2,'c'=8] {'k','d','c'}, dimensions={0} | all-to-all | bytes 1310720 | tf_op jit(solution)/shard_map/all_to_all | solution.py:17
  107.7 1.5 shard_map.268
  109.2 20.8 %all_to_all.37.refs_0_ = f32[16,48,128]{2,1,0:T(8,128)S(1)} all-to-all(f32[16,48,128]{2,1,0:T(8,128)S(1)} %get-tuple-element.31), channel_id=1, replica_groups=mesh['a'=2,'e'=2,'z'=4,'k'=2,'d'=2,'c'=8] {'a','e','z'}, dimensions={0} | all-to-all | bytes 786432 | tf_op jit(solution)/shard_map/all_to_all | solution.py:17
  130.0 9.3 %collective-permute-start.2 = (f32[576,128]{1,0:T(8,128)S(1)}, f32[576,128]{1,0:T(8,128)S(1)}, u32[]{:S(2)}, u32[]{:S(2)}) collective-permute-start(f32[576,128]{1,0:T(8,128)S(1)} %get-tuple-element.33.refs_8_), channel_id=1, source_target_pairs={{0,16},{16,0},{1,17},{17,1},{2,18},{18,2},{3,19},{19,3},{4,20},{20... | collective-permute-start | bytes 884744 | tf_op jit(solution)/shard_map/ppermute | solution.py:21
  139.3 13.0 %all_to_all.38.refs_7_ = f32[32,8,128]{2,1,0:T(8,128)S(1)} all-to-all(f32[32,8,128]{2,1,0:T(8,128)S(1)} %get-tuple-element.32), channel_id=1, replica_groups=mesh['a'=2,'e'=2,'z'=4,'k'=2,'d'=2,'c'=8] {'k','d','c'}, dimensions={0} | all-to-all | bytes 262144 | tf_op jit(solution)/shard_map/all_to_all | solution.py:17
  152.4 3.9 %shard_map.270 = f32[8,128,128]{2,1,0:T(8,128)} custom-call(s32[1]{0:T(128)} %bitcast.refs_0_, s32[1]{0:T(128)} %bitcast.1.refs_1_, s32[1]{0:T(128)} %bitcast.2.refs_2_, s32[1]{0:T(128)} %bitcast.3.refs_3_, s32[14]{0:T(128)S(1)} %copy-done.4, f32[32,40,128]{2,1,0:T(8,128)S(1)} %all_to_all.36.refs_5_, f32[3,64,128]{2,1,0:T(8,128)S(1)} %get-tuple-element.30.refs_6_, ...), custom_call_target="tpu_custom_call" | custom-call | flops 3000000000 | bytes 4194304 | tf_op jit(solution)/shard_map/pallas_call | solution.py:467
  156.3 3.6 %all-to-all-start.6 = ((f32[8,128,128]{2,1,0:T(8,128)}), f32[8,128,128]{2,1,0:T(8,128)S(1)}, u32[]{:S(2)}, u32[]{:S(2)}) async-start(f32[8,128,128]{2,1,0:T(8,128)} %shard_map.270), calls=%async_computation.6 | async-start | bytes 1048576 | tf_op jit(solution)/shard_map/all_to_all | solution.py:17
  159.9 10.2 %all-to-all-done.6 = f32[8,128,128]{2,1,0:T(8,128)S(1)} async-done(((f32[8,128,128]{2,1,0:T(8,128)}), f32[8,128,128]{2,1,0:T(8,128)S(1)}, u32[]{:S(2)}, u32[]{:S(2)}) %all-to-all-start.6) | async-done | bytes 524320 | tf_op jit(solution)/shard_map/all_to_all | solution.py:17
  170.2 0.6 slice_bitcast_fusion
  170.8 2.8 %collective-permute-start.3 = (f32[24,128]{1,0:T(8,128)S(1)}, f32[24,128]{1,0:T(8,128)S(1)}, u32[]{:S(2)}, u32[]{:S(2)}) collective-permute-start(f32[24,128]{1,0:T(8,128)S(1)} %dynamic-slice_bitcast_fusion), channel_id=1, source_target_pairs={{0,8},{8,0},{1,9},{9,1},{2,10},{10,2},{3,11},{11,3},{4,12},{12,4},... | collective-permute-start | bytes 36872 | tf_op jit(solution)/shard_map/ppermute | solution.py:21
  173.6 1.9 %shard_map.271 = f32[1,1,384,128]{3,2,1,0:T(8,128)} custom-call(s32[1,1]{1,0:T(1,128)S(6)} %copy.29.refs_0_, f32[32,128]{1,0:T(8,128)S(1)} %slice.29.refs_1_, f32[384,128]{1,0:T(8,128)S(1)} %copy-done.14, f32[1,1,2,384,384]{4,3,2,1,0:T(8,128)S(1)} %copy-done.5, f32[1,1,2,32,384]{4,3,2,1,0:T(8,128)S(1)} %bitcast.34), custom_call_target="tpu_custom_call" | custom-call | flops 1000000000 | bytes 4194304 | tf_op jit(solution)/shard_map/pallas_call | solution.py:467
  175.5 1.2 collective-permute-done.3
  176.8 0.6 broadcast_in_dim.12
  177.4 0.6 broadcast_in_dim.13
  (34 shorter events, 0.1 us)
Async XLA Ops:
  4.8 17.9 %all-to-all-start = ((f32[8,128,128]{2,1,0:T(8,128)}), f32[8,128,128]{2,1,0:T(8,128)S(1)}, u32[]{:S(2)}, u32[]{:S(2)}) async-start(f32[8,128,128]{2,1,0:T(8,128)} %get-tuple-element.20), calls=%async_computation | async-start | bytes 1048576 | tf_op jit(solution)/shard_map/all_to_all | solution.py:17
  16.3 19.7 %collective-permute-start = (f32[16,64,128]{2,1,0:T(8,128)}, f32[16,64,128]{2,1,0:T(8,128)S(1)}, u32[]{:S(2)}, u32[]{:S(2)}) collective-permute-start(f32[16,64,128]{2,1,0:T(8,128)} %get-tuple-element.24), channel_id=1, source_target_pairs={{0,16},{16,0},{1,17},{17,1},{2,18},{18,2},{3,19},{19,3},{4,20},{20... | collective-permute-start | bytes 1572872 | tf_op jit(solution)/shard_map/ppermute | solution.py:21
  22.7 0.8 copy-start
  23.5 16.7 %copy-start.2 = (f32[16,64,128]{2,1,0:T(8,128)S(1)}, f32[16,64,128]{2,1,0:T(8,128)}, u32[]{:S(2)}) copy-start(f32[16,64,128]{2,1,0:T(8,128)} %get-tuple-element.23.refs_1_) | copy-start | bytes 1572868
  26.8 13.4 %all-to-all-start.1 = ((f32[32,8,128]{2,1,0:T(8,128)}), f32[32,8,128]{2,1,0:T(8,128)S(1)}, u32[]{:S(2)}, u32[]{:S(2)}) async-start(f32[32,8,128]{2,1,0:T(8,128)} %get-tuple-element.22), calls=%async_computation.1 | async-start | bytes 262144 | tf_op jit(solution)/shard_map/all_to_all | solution.py:17
  32.7 3.4 %collective-permute-start.1 = (f32[16,8,128]{2,1,0:T(8,128)}, f32[16,8,128]{2,1,0:T(8,128)S(1)}, u32[]{:S(2)}, u32[]{:S(2)}) collective-permute-start(f32[16,8,128]{2,1,0:T(8,128)} %get-tuple-element.26), channel_id=1, source_target_pairs={{0,16},{16,0},{1,17},{17,1},{2,18},{18,2},{3,19},{19,3},{4,20},{20... | collective-permute-start | bytes 196616 | tf_op jit(solution)/shard_map/ppermute | solution.py:21
  40.2 0.8 copy-start.3
  87.7 20.0 %copy-start.4 = (s32[14]{0:T(128)S(1)}, s32[14]{0:T(128)}, u32[]{:S(2)}) copy-start(s32[14]{0:T(128)} %refs_4_.3) | copy-start | bytes 172
  88.2 64.1 %copy-start.9 = (f32[1,1,2,192,192]{4,3,2,1,0:T(8,128)S(1)}, f32[1,1,2,192,192]{4,3,2,1,0:T(8,128)}, u32[]{:S(2)}) copy-start(f32[1,1,2,192,192]{4,3,2,1,0:T(8,128)} %refs_13_.3) | copy-start | bytes 884740
  88.2 64.1 %copy-start.10 = (f32[1,4,2,192,32]{3,4,2,1,0:T(8,128)S(1)}, f32[1,4,2,192,32]{3,4,2,1,0:T(8,128)}, u32[]{:S(2)}) copy-start(f32[1,4,2,192,32]{3,4,2,1,0:T(8,128)} %param.44) | copy-start | bytes 589828
  88.3 64.1 %copy-start.11 = (f32[1,2,2,384,32]{3,4,2,1,0:T(8,128)S(1)}, f32[1,2,2,384,32]{3,4,2,1,0:T(8,128)}, u32[]{:S(2)}) copy-start(f32[1,2,2,384,32]{3,4,2,1,0:T(8,128)} %param.43) | copy-start | bytes 589828
  88.3 64.1 %copy-start.12 = (f32[1,2,2,192,32]{3,4,2,1,0:T(8,128)S(1)}, f32[1,2,2,192,32]{3,4,2,1,0:T(8,128)}, u32[]{:S(2)}) copy-start(f32[1,2,2,192,32]{3,4,2,1,0:T(8,128)} %param.42) | copy-start | bytes 294916
  107.6 44.7 %copy-start.1 = (f32[8,128,128]{2,1,0:T(8,128)S(1)}, f32[8,128,128]{2,1,0:T(8,128)}, u32[]{:S(2)}) copy-start(f32[8,128,128]{2,1,0:T(8,128)} %copy-done) | copy-start | bytes 1572868
  107.6 44.7 %copy-start.6 = (f32[1,1,2,384,192]{3,4,2,1,0:T(8,128)S(1)}, f32[1,1,2,384,192]{3,4,2,1,0:T(8,128)}, u32[]{:S(2)}) copy-start(f32[1,1,2,384,192]{3,4,2,1,0:T(8,128)} %param.24) | copy-start | bytes 1769476
  107.6 44.7 %copy-start.7 = (f32[1,1,2,384,192]{3,4,2,1,0:T(8,128)S(1)}, f32[1,1,2,384,192]{3,4,2,1,0:T(8,128)}, u32[]{:S(2)}) copy-start(f32[1,1,2,384,192]{3,4,2,1,0:T(8,128)} %param.26) | copy-start | bytes 1769476
  107.6 44.7 %copy-start.8 = (f32[1,1,2,192,192]{4,3,2,1,0:T(8,128)S(1)}, f32[1,1,2,192,192]{4,3,2,1,0:T(8,128)}, u32[]{:S(2)}) copy-start(f32[1,1,2,192,192]{4,3,2,1,0:T(8,128)} %refs_11_.1) | copy-start | bytes 884740
  130.0 22.3 %collective-permute-start.2 = (f32[576,128]{1,0:T(8,128)S(1)}, f32[576,128]{1,0:T(8,128)S(1)}, u32[]{:S(2)}, u32[]{:S(2)}) collective-permute-start(f32[576,128]{1,0:T(8,128)S(1)} %get-tuple-element.33.refs_8_), channel_id=1, source_target_pairs={{0,16},{16,0},{1,17},{17,1},{2,18},{18,2},{3,19},{19,3},{4,20},{20... | collective-permute-start | bytes 884744 | tf_op jit(solution)/shard_map/ppermute | solution.py:21
  156.3 17.3 %copy-start.5 = (f32[1,1,2,384,384]{4,3,2,1,0:T(8,128)S(1)}, f32[1,1,2,384,384]{4,3,2,1,0:T(8,128)}, u32[]{:S(2)}) copy-start(f32[1,1,2,384,384]{4,3,2,1,0:T(8,128)} %refs_3_.1) | copy-start | bytes 3538948
  156.3 17.3 %copy-start.13 = (f32[1,1,2,384,32]{3,4,2,1,0:T(8,128)S(1)}, f32[1,1,2,384,32]{3,4,2,1,0:T(8,128)}, u32[]{:S(2)}) copy-start(f32[1,1,2,384,32]{3,4,2,1,0:T(8,128)} %param.45) | copy-start | bytes 294916
  156.3 17.3 %copy-start.14 = (f32[384,128]{1,0:T(8,128)S(1)}, f32[384,128]{1,0:T(8,128)}, u32[]{:S(2)}) copy-start(f32[384,128]{1,0:T(8,128)} %get-tuple-element.34.refs_2_) | copy-start | bytes 589828
  156.3 13.8 %all-to-all-start.6 = ((f32[8,128,128]{2,1,0:T(8,128)}), f32[8,128,128]{2,1,0:T(8,128)S(1)}, u32[]{:S(2)}, u32[]{:S(2)}) async-start(f32[8,128,128]{2,1,0:T(8,128)} %shard_map.270), calls=%async_computation.6 | async-start | bytes 1048576 | tf_op jit(solution)/shard_map/all_to_all | solution.py:17
  170.8 5.9 %collective-permute-start.3 = (f32[24,128]{1,0:T(8,128)S(1)}, f32[24,128]{1,0:T(8,128)S(1)}, u32[]{:S(2)}, u32[]{:S(2)}) collective-permute-start(f32[24,128]{1,0:T(8,128)S(1)} %dynamic-slice_bitcast_fusion), channel_id=1, source_target_pairs={{0,8},{8,0},{1,9},{9,1},{2,10},{10,2},{3,11},{11,3},{4,12},{12,4},... | collective-permute-start | bytes 36872 | tf_op jit(solution)/shard_map/ppermute | solution.py:21

commit v8 on v7

--- a/solution.py
+++ b/solution.py
@@ -5,8 +5,6 @@
 from jax.experimental.pallas import tpu as pltpu
 from jax.sharding import Mesh, PartitionSpec as P
 
-precise = lax.Precision.HIGHEST
-
 ROW = ("a", "e", "z", "k")
 COL = ("d", "c")
 CHIPS = ("a", "e", "z")
@@ -43,6 +41,17 @@
         )
 
     return one(left_high, right_high) + (one(left_high, right_low) + one(left_low, right_high))
+
+
+def placed(values, onehot, rows):
+    def one(part):
+        left, right = (onehot, part) if rows else (part, onehot)
+        return lax.dot_general(
+            left, right, (((1,), (1,)), ((), ())), preferred_element_type=jnp.float32
+        )
+
+    high, low = halves(values)
+    return one(high) + one(low)
 
 
 def times(real, imag, vector):
@@ -72,15 +81,9 @@
     low = cut(times(basis[0, 0, 0], basis[0, 0, 1], result), ranks[0, 0])
     height = inner // 2
     places = lax.broadcasted_iota(jnp.int32, (height, slots.shape[-1]), 0)
-    onehot = (places == slots[0]).astype(jnp.float32)
+    onehot = (places == slots[0]).astype(jnp.bfloat16)
     flat = jnp.concatenate([update[0, 0, 0], update[0, 0, 1]], axis=0)
-    spread_out = lax.dot_general(
-        flat,
-        onehot,
-        (((1,), (1,)), ((), ())),
-        precision=precise,
-        preferred_element_type=jnp.float32,
-    )
+    spread_out = placed(flat, onehot, False)
     half = low.shape[0]
     pack = jnp.concatenate(
         [
@@ -127,17 +130,11 @@
         places = lax.broadcasted_iota(jnp.int32, (height, lists.shape[-1]), 0)
         spread_out = jnp.zeros((height, 128), jnp.float32)
         for child in range(2):
-            onehot = (places == lists[child : child + 1]).astype(jnp.float32)
+            onehot = (places == lists[child : child + 1]).astype(jnp.bfloat16)
             real, imag = update[0, at, child, 0], update[0, at, child, 1]
             nothing = jnp.zeros_like(real)
             order = [real, nothing, imag, nothing] if child == 0 else [nothing, real, nothing, imag]
-            spread_out += lax.dot_general(
-                onehot,
-                jnp.concatenate(order, axis=0),
-                (((1,), (1,)), ((), ())),
-                precision=precise,
-                preferred_element_type=jnp.float32,
-            )
+            spread_out += placed(jnp.concatenate(order, axis=0), onehot, True)
         both = jnp.concatenate([right, spread_out], axis=-1)
         apply = times if inverse is inverse1 else times_back
         results.append(apply(inverse[0, 0, 0], inverse[0, 0, 1], both))

time: 179 us -> 178 us (level)
  no operation moved by 1% of the time
where the time goes in v8:
time: 178 us
  blocking collectives  99.9 us (56%)
  starting transfers between devices  36 us (20%)
  Pallas kernels  19.8 us (11%)
  waiting for transfers between devices  16.8 us (9%)
  local copies, waits for them, and re-layouts  3.54 us (2%)
    all_to_all x4, blocking collectives, exchange(): return lax.all_to_all(pieces, axes, 0, 0)  99.9 us
    ppermute x4, starting transfers between devices, partner(): return lax.ppermute(values, axis, [(0, 1), (1, 0)])  20.6 us
    pallas_call x9, Pallas kernels, call(): pl.pallas_call(outer, out_shape=[jax.ShapeDtypeStruct(shape, jnp.float32)...  19.8 us
    all_to_all x3, starting transfers between devices, exchange(): return lax.all_to_all(pieces, axes, 0, 0)  15.4 us
    all_to_all x3, waiting for transfers between devices, exchange(): return lax.all_to_all(pieces, axes, 0, 0)  14.4 us
  transfers between devices with their start and end apart: 7, of which 4 were waited for; matrix products, arithmetic and copies ran while one was open for 0% of the time, Pallas kernels for 6%

profile of v8, /device:TPU:1, one launch (start us, length us, event | category | flops | bytes accessed | tf_op | source)
XLA Modules:
  0.0 177.5 jit_solution(1461913790205594284)
XLA Ops:
  1.3 3.2 %shard_map.263 = (f32[384,128]{1,0:T(8,128)}, f32[8,128,128]{2,1,0:T(8,128)}) custom-call(s32[1,1]{1,0:T(1,128)S(6)} %copy.29.refs_0_, f32[1,1,2,384,384]{4,3,2,1,0:T(8,128)} %refs_3_.1, f32[1,1,384,128]{3,2,1,0:T(8,128)} %refs_2_.1, f32[1,1,2,32,384]{4,3,2,1,0:T(8,128)} %bitcast.33, f32[1,1,2,32,96]{4,3,2,1,0:T(8,128)} %bitcast.40, s32[1,1,96]{2,1,0:T(1,128)} %refs_5_.2), custom_call_target="tpu_custom_call" | custom-call | flops 1000000000 | bytes 4194304 | tf_op jit(solution)/shard_map/pallas_call | solution.py:464
  4.5 5.9 %all-to-all-start = ((f32[8,128,128]{2,1,0:T(8,128)}), f32[8,128,128]{2,1,0:T(8,128)S(1)}, u32[]{:S(2)}, u32[]{:S(2)}) async-start(f32[8,128,128]{2,1,0:T(8,128)} %get-tuple-element.20), calls=%async_computation | async-start | bytes 1048576 | tf_op jit(solution)/shard_map/all_to_all | solution.py:15
  10.4 5.3 %shard_map.264 = (f32[16,64,128]{2,1,0:T(8,128)}, f32[16,64,128]{2,1,0:T(8,128)}, f32[4,32,128]{2,1,0:T(8,128)}) custom-call(s32[1]{0:T(128)} %bitcast.refs_0_, s32[1]{0:T(128)} %bitcast.1.refs_1_, s32[1]{0:T(128)} %bitcast.2.refs_2_, s32[1]{0:T(128)} %bitcast.3.refs_3_, f32[1,1,2,192,384]{4,3,2,1,0:T(8,128)} %bitcast.23, f32[1,1,2,192,192]{4,3,2,1,0:T(8,128)} %refs_11_.1, ...), custom_call_target="tpu_custom_call" | custom-call | flops 4000000000 | bytes 4194304 | tf_op jit(solution)/shard_map/pallas_call | solution.py:464
  15.7 6.4 %collective-permute-start = (f32[16,64,128]{2,1,0:T(8,128)}, f32[16,64,128]{2,1,0:T(8,128)S(1)}, u32[]{:S(2)}, u32[]{:S(2)}) collective-permute-start(f32[16,64,128]{2,1,0:T(8,128)} %get-tuple-element.24), channel_id=1, source_target_pairs={{0,16},{16,0},{1,17},{17,1},{2,18},{18,2},{3,19},{19,3},{4,20},{20... | collective-permute-start | bytes 1572872 | tf_op jit(solution)/shard_map/ppermute | solution.py:19
  22.1 0.8 copy-done
  22.9 3.2 %shard_map.265 = (f32[16,8,128]{2,1,0:T(8,128)}, f32[16,8,128]{2,1,0:T(8,128)}, f32[32,8,128]{2,1,0:T(8,128)}) custom-call(s32[1]{0:T(128)} %bitcast.refs_0_, s32[1]{0:T(128)} %bitcast.1.refs_1_, s32[1]{0:T(128)} %bitcast.2.refs_2_, s32[1]{0:T(128)} %bitcast.3.refs_3_, f32[8,128,128]{2,1,0:T(8,128)} %copy-done, f32[4,32,128]{2,1,0:T(8,128)} %get-tuple-element.21.refs_5_, ...), custom_call_target="tpu_custom_call" | custom-call | flops 1000000000 | bytes 4194304 | tf_op jit(solution)/shard_map/pallas_call | solution.py:464
  26.2 5.9 %all-to-all-start.1 = ((f32[32,8,128]{2,1,0:T(8,128)}), f32[32,8,128]{2,1,0:T(8,128)S(1)}, u32[]{:S(2)}, u32[]{:S(2)}) async-start(f32[32,8,128]{2,1,0:T(8,128)} %get-tuple-element.22), calls=%async_computation.1 | async-start | bytes 262144 | tf_op jit(solution)/shard_map/all_to_all | solution.py:15
  32.1 2.1 %collective-permute-start.1 = (f32[16,8,128]{2,1,0:T(8,128)}, f32[16,8,128]{2,1,0:T(8,128)S(1)}, u32[]{:S(2)}, u32[]{:S(2)}) collective-permute-start(f32[16,8,128]{2,1,0:T(8,128)} %get-tuple-element.26), channel_id=1, source_target_pairs={{0,16},{16,0},{1,17},{17,1},{2,18},{18,2},{3,19},{19,3},{4,20},{20... | collective-permute-start | bytes 196616 | tf_op jit(solution)/shard_map/ppermute | solution.py:19
  34.2 1.2 collective-permute-done.1.refs_4_
  35.4 4.2 %all-to-all-done.1.refs_0_ = f32[32,8,128]{2,1,0:T(8,128)S(1)} async-done(((f32[32,8,128]{2,1,0:T(8,128)}), f32[32,8,128]{2,1,0:T(8,128)S(1)}, u32[]{:S(2)}, u32[]{:S(2)}) %all-to-all-start.1) | async-done | bytes 131104 | tf_op jit(solution)/shard_map/all_to_all | solution.py:15
  39.6 0.8 copy-done.3
  40.4 0.1 shard_map.266
  40.5 46.7 %all_to_all.35.refs_4_ = f32[16,80,128]{2,1,0:T(8,128)S(1)} all-to-all(f32[16,80,128]{2,1,0:T(8,128)S(1)} %shard_map.266), channel_id=1, replica_groups=mesh['a'=2,'e'=2,'z'=4,'k'=2,'d'=2,'c'=8] {'a','e','z'}, dimensions={0} | all-to-all | bytes 1310720 | tf_op jit(solution)/shard_map/all_to_all | solution.py:15
  87.3 0.5 shard_map.267
  87.8 0.0 copy-start.9
  87.8 0.0 copy-start.10
  87.8 0.0 copy-start.11
  87.8 0.0 copy-start.12
  87.8 19.4 %all_to_all.36.refs_5_ = f32[32,40,128]{2,1,0:T(8,128)S(1)} all-to-all(f32[32,40,128]{2,1,0:T(8,128)S(1)} %get-tuple-element.27), channel_id=1, replica_groups=mesh['a'=2,'e'=2,'z'=4,'k'=2,'d'=2,'c'=8] {'k','d','c'}, dimensions={0} | all-to-all | bytes 1310720 | tf_op jit(solution)/shard_map/all_to_all | solution.py:15
  107.2 1.5 shard_map.268
  108.8 20.8 %all_to_all.37.refs_0_ = f32[16,48,128]{2,1,0:T(8,128)S(1)} all-to-all(f32[16,48,128]{2,1,0:T(8,128)S(1)} %get-tuple-element.31), channel_id=1, replica_groups=mesh['a'=2,'e'=2,'z'=4,'k'=2,'d'=2,'c'=8] {'a','e','z'}, dimensions={0} | all-to-all | bytes 786432 | tf_op jit(solution)/shard_map/all_to_all | solution.py:15
  129.6 9.3 %collective-permute-start.2 = (f32[576,128]{1,0:T(8,128)S(1)}, f32[576,128]{1,0:T(8,128)S(1)}, u32[]{:S(2)}, u32[]{:S(2)}) collective-permute-start(f32[576,128]{1,0:T(8,128)S(1)} %get-tuple-element.33.refs_8_), channel_id=1, source_target_pairs={{0,16},{16,0},{1,17},{17,1},{2,18},{18,2},{3,19},{19,3},{4,20},{20... | collective-permute-start | bytes 884744 | tf_op jit(solution)/shard_map/ppermute | solution.py:19
  138.8 13.0 %all_to_all.38.refs_7_ = f32[32,8,128]{2,1,0:T(8,128)S(1)} all-to-all(f32[32,8,128]{2,1,0:T(8,128)S(1)} %get-tuple-element.32), channel_id=1, replica_groups=mesh['a'=2,'e'=2,'z'=4,'k'=2,'d'=2,'c'=8] {'k','d','c'}, dimensions={0} | all-to-all | bytes 262144 | tf_op jit(solution)/shard_map/all_to_all | solution.py:15
  151.9 3.9 %shard_map.270 = f32[8,128,128]{2,1,0:T(8,128)} custom-call(s32[1]{0:T(128)} %bitcast.refs_0_, s32[1]{0:T(128)} %bitcast.1.refs_1_, s32[1]{0:T(128)} %bitcast.2.refs_2_, s32[1]{0:T(128)} %bitcast.3.refs_3_, s32[14]{0:T(128)S(1)} %copy-done.4, f32[32,40,128]{2,1,0:T(8,128)S(1)} %all_to_all.36.refs_5_, f32[3,64,128]{2,1,0:T(8,128)S(1)} %get-tuple-element.30.refs_6_, ...), custom_call_target="tpu_custom_call" | custom-call | flops 3000000000 | bytes 4194304 | tf_op jit(solution)/shard_map/pallas_call | solution.py:464
  155.9 3.6 %all-to-all-start.6 = ((f32[8,128,128]{2,1,0:T(8,128)}), f32[8,128,128]{2,1,0:T(8,128)S(1)}, u32[]{:S(2)}, u32[]{:S(2)}) async-start(f32[8,128,128]{2,1,0:T(8,128)} %shard_map.270), calls=%async_computation.6 | async-start | bytes 1048576 | tf_op jit(solution)/shard_map/all_to_all | solution.py:15
  159.5 10.2 %all-to-all-done.6 = f32[8,128,128]{2,1,0:T(8,128)S(1)} async-done(((f32[8,128,128]{2,1,0:T(8,128)}), f32[8,128,128]{2,1,0:T(8,128)S(1)}, u32[]{:S(2)}, u32[]{:S(2)}) %all-to-all-start.6) | async-done | bytes 524320 | tf_op jit(solution)/shard_map/all_to_all | solution.py:15
  169.8 0.6 slice_bitcast_fusion
  170.4 2.8 %collective-permute-start.3 = (f32[24,128]{1,0:T(8,128)S(1)}, f32[24,128]{1,0:T(8,128)S(1)}, u32[]{:S(2)}, u32[]{:S(2)}) collective-permute-start(f32[24,128]{1,0:T(8,128)S(1)} %dynamic-slice_bitcast_fusion), channel_id=1, source_target_pairs={{0,8},{8,0},{1,9},{9,1},{2,10},{10,2},{3,11},{11,3},{4,12},{12,4},... | collective-permute-start | bytes 36872 | tf_op jit(solution)/shard_map/ppermute | solution.py:19
  173.2 1.9 %shard_map.271 = f32[1,1,384,128]{3,2,1,0:T(8,128)} custom-call(s32[1,1]{1,0:T(1,128)S(6)} %copy.29.refs_0_, f32[32,128]{1,0:T(8,128)S(1)} %slice.29.refs_1_, f32[384,128]{1,0:T(8,128)S(1)} %copy-done.14, f32[1,1,2,384,384]{4,3,2,1,0:T(8,128)S(1)} %copy-done.5, f32[1,1,2,32,384]{4,3,2,1,0:T(8,128)S(1)} %bitcast.34), custom_call_target="tpu_custom_call" | custom-call | flops 1000000000 | bytes 4194304 | tf_op jit(solution)/shard_map/pallas_call | solution.py:464
  175.1 1.2 collective-permute-done.3
  176.3 0.6 broadcast_in_dim.12
  176.9 0.6 broadcast_in_dim.13
  (34 shorter events, 0.1 us)
Async XLA Ops:
  4.5 17.6 %all-to-all-start = ((f32[8,128,128]{2,1,0:T(8,128)}), f32[8,128,128]{2,1,0:T(8,128)S(1)}, u32[]{:S(2)}, u32[]{:S(2)}) async-start(f32[8,128,128]{2,1,0:T(8,128)} %get-tuple-element.20), calls=%async_computation | async-start | bytes 1048576 | tf_op jit(solution)/shard_map/all_to_all | solution.py:15
  15.7 19.7 %collective-permute-start = (f32[16,64,128]{2,1,0:T(8,128)}, f32[16,64,128]{2,1,0:T(8,128)S(1)}, u32[]{:S(2)}, u32[]{:S(2)}) collective-permute-start(f32[16,64,128]{2,1,0:T(8,128)} %get-tuple-element.24), channel_id=1, source_target_pairs={{0,16},{16,0},{1,17},{17,1},{2,18},{18,2},{3,19},{19,3},{4,20},{20... | collective-permute-start | bytes 1572872 | tf_op jit(solution)/shard_map/ppermute | solution.py:19
  22.1 0.8 copy-start
  22.9 16.7 %copy-start.2 = (f32[16,64,128]{2,1,0:T(8,128)S(1)}, f32[16,64,128]{2,1,0:T(8,128)}, u32[]{:S(2)}) copy-start(f32[16,64,128]{2,1,0:T(8,128)} %get-tuple-element.23.refs_1_) | copy-start | bytes 1572868
  26.2 13.4 %all-to-all-start.1 = ((f32[32,8,128]{2,1,0:T(8,128)}), f32[32,8,128]{2,1,0:T(8,128)S(1)}, u32[]{:S(2)}, u32[]{:S(2)}) async-start(f32[32,8,128]{2,1,0:T(8,128)} %get-tuple-element.22), calls=%async_computation.1 | async-start | bytes 262144 | tf_op jit(solution)/shard_map/all_to_all | solution.py:15
  32.1 3.4 %collective-permute-start.1 = (f32[16,8,128]{2,1,0:T(8,128)}, f32[16,8,128]{2,1,0:T(8,128)S(1)}, u32[]{:S(2)}, u32[]{:S(2)}) collective-permute-start(f32[16,8,128]{2,1,0:T(8,128)} %get-tuple-element.26), channel_id=1, source_target_pairs={{0,16},{16,0},{1,17},{17,1},{2,18},{18,2},{3,19},{19,3},{4,20},{20... | collective-permute-start | bytes 196616 | tf_op jit(solution)/shard_map/ppermute | solution.py:19
  39.6 0.8 copy-start.3
  87.3 20.0 %copy-start.4 = (s32[14]{0:T(128)S(1)}, s32[14]{0:T(128)}, u32[]{:S(2)}) copy-start(s32[14]{0:T(128)} %refs_4_.3) | copy-start | bytes 172
  87.8 64.1 %copy-start.9 = (f32[1,1,2,192,192]{4,3,2,1,0:T(8,128)S(1)}, f32[1,1,2,192,192]{4,3,2,1,0:T(8,128)}, u32[]{:S(2)}) copy-start(f32[1,1,2,192,192]{4,3,2,1,0:T(8,128)} %refs_13_.3) | copy-start | bytes 884740
  87.8 64.1 %copy-start.10 = (f32[1,4,2,192,32]{3,4,2,1,0:T(8,128)S(1)}, f32[1,4,2,192,32]{3,4,2,1,0:T(8,128)}, u32[]{:S(2)}) copy-start(f32[1,4,2,192,32]{3,4,2,1,0:T(8,128)} %param.44) | copy-start | bytes 589828
  87.8 64.1 %copy-start.11 = (f32[1,2,2,384,32]{3,4,2,1,0:T(8,128)S(1)}, f32[1,2,2,384,32]{3,4,2,1,0:T(8,128)}, u32[]{:S(2)}) copy-start(f32[1,2,2,384,32]{3,4,2,1,0:T(8,128)} %param.43) | copy-start | bytes 589828
  87.8 64.1 %copy-start.12 = (f32[1,2,2,192,32]{3,4,2,1,0:T(8,128)S(1)}, f32[1,2,2,192,32]{3,4,2,1,0:T(8,128)}, u32[]{:S(2)}) copy-start(f32[1,2,2,192,32]{3,4,2,1,0:T(8,128)} %param.42) | copy-start | bytes 294916
  107.2 44.7 %copy-start.1 = (f32[8,128,128]{2,1,0:T(8,128)S(1)}, f32[8,128,128]{2,1,0:T(8,128)}, u32[]{:S(2)}) copy-start(f32[8,128,128]{2,1,0:T(8,128)} %copy-done) | copy-start | bytes 1572868
  107.2 44.7 %copy-start.6 = (f32[1,1,2,384,192]{3,4,2,1,0:T(8,128)S(1)}, f32[1,1,2,384,192]{3,4,2,1,0:T(8,128)}, u32[]{:S(2)}) copy-start(f32[1,1,2,384,192]{3,4,2,1,0:T(8,128)} %param.24) | copy-start | bytes 1769476
  107.2 44.7 %copy-start.7 = (f32[1,1,2,384,192]{3,4,2,1,0:T(8,128)S(1)}, f32[1,1,2,384,192]{3,4,2,1,0:T(8,128)}, u32[]{:S(2)}) copy-start(f32[1,1,2,384,192]{3,4,2,1,0:T(8,128)} %param.26) | copy-start | bytes 1769476
  107.2 44.7 %copy-start.8 = (f32[1,1,2,192,192]{4,3,2,1,0:T(8,128)S(1)}, f32[1,1,2,192,192]{4,3,2,1,0:T(8,128)}, u32[]{:S(2)}) copy-start(f32[1,1,2,192,192]{4,3,2,1,0:T(8,128)} %refs_11_.1) | copy-start | bytes 884740
  129.6 22.3 %collective-permute-start.2 = (f32[576,128]{1,0:T(8,128)S(1)}, f32[576,128]{1,0:T(8,128)S(1)}, u32[]{:S(2)}, u32[]{:S(2)}) collective-permute-start(f32[576,128]{1,0:T(8,128)S(1)} %get-tuple-element.33.refs_8_), channel_id=1, source_target_pairs={{0,16},{16,0},{1,17},{17,1},{2,18},{18,2},{3,19},{19,3},{4,20},{20... | collective-permute-start | bytes 884744 | tf_op jit(solution)/shard_map/ppermute | solution.py:19
  155.9 17.3 %copy-start.5 = (f32[1,1,2,384,384]{4,3,2,1,0:T(8,128)S(1)}, f32[1,1,2,384,384]{4,3,2,1,0:T(8,128)}, u32[]{:S(2)}) copy-start(f32[1,1,2,384,384]{4,3,2,1,0:T(8,128)} %refs_3_.1) | copy-start | bytes 3538948
  155.9 17.3 %copy-start.13 = (f32[1,1,2,384,32]{3,4,2,1,0:T(8,128)S(1)}, f32[1,1,2,384,32]{3,4,2,1,0:T(8,128)}, u32[]{:S(2)}) copy-start(f32[1,1,2,384,32]{3,4,2,1,0:T(8,128)} %param.45) | copy-start | bytes 294916
  155.9 17.3 %copy-start.14 = (f32[384,128]{1,0:T(8,128)S(1)}, f32[384,128]{1,0:T(8,128)}, u32[]{:S(2)}) copy-start(f32[384,128]{1,0:T(8,128)} %get-tuple-element.34.refs_2_) | copy-start | bytes 589828
  155.9 13.8 %all-to-all-start.6 = ((f32[8,128,128]{2,1,0:T(8,128)}), f32[8,128,128]{2,1,0:T(8,128)S(1)}, u32[]{:S(2)}, u32[]{:S(2)}) async-start(f32[8,128,128]{2,1,0:T(8,128)} %shard_map.270), calls=%async_computation.6 | async-start | bytes 1048576 | tf_op jit(solution)/shard_map/all_to_all | solution.py:15
  170.4 5.9 %collective-permute-start.3 = (f32[24,128]{1,0:T(8,128)S(1)}, f32[24,128]{1,0:T(8,128)S(1)}, u32[]{:S(2)}, u32[]{:S(2)}) collective-permute-start(f32[24,128]{1,0:T(8,128)S(1)} %dynamic-slice_bitcast_fusion), channel_id=1, source_target_pairs={{0,8},{8,0},{1,9},{9,1},{2,10},{10,2},{3,11},{11,3},{4,12},{12,4},... | collective-permute-start | bytes 36872 | tf_op jit(solution)/shard_map/ppermute | solution.py:19
